TPU v7x, 32 devices: a whole 2x2x4 slice. The times are simulated.
32 devices in a mesh: expert: 8 (over y, x, core), wshard: 4 (over z).
Axes of the slice: x: 2, y: 2, z: 4, core: 2. Of those that a mesh axis runs over, the one named last changes fastest.
Arguments:
- tokens: bfloat16 [4, 1024, 768], P('wshard', 'expert'), may hold values from -6 to 6
- gain_attn: bfloat16 [768], P('wshard'), may hold values from 0.099609375 to 1.8984375
- gain_mix: bfloat16 [768], P('wshard'), may hold values from 0.099609375 to 1.8984375
- attn_in: bfloat16 [768, 2304], P('wshard'), may hold values from -0.109375 to 0.109375
- attn_out: bfloat16 [768, 768], P('wshard'), may hold values from -0.625 to 0.625
- router: bfloat16 [768, 16], P('wshard'), may hold values from -0.15625 to 0.15625
- bias_table: bfloat16 [32, 12], P('wshard'), may hold values from -4 to 4
- expert_in: bfloat16 [16, 768, 3072], P('expert', None, 'wshard'), may hold values from -0.21875 to 0.21875
- expert_down: bfloat16 [16, 768, 3072], P('expert', None, 'wshard'), may hold values from -2.5 to 2.5
- routes: int32 [4, 1024], P('wshard', 'expert'), may hold values from 0 to 15, as said below
- buckets: int32 [2047], replicated, may hold values from 0 to 31
- out_grad: bfloat16 [4, 1024, 768], P('wshard', 'expert'), may hold values from -6 to 6
Outputs:
- result: bfloat16 [4, 1024, 768], P('wshard', 'expert')
- tokens_grad: bfloat16 [4, 1024, 768], P('wshard', 'expert')
- gain_attn_grad: float32 [768], P('wshard')
- gain_mix_grad: float32 [768], P('wshard')
- attn_in_grad: float32 [768, 2304], P('wshard')
- attn_out_grad: float32 [768, 768], P('wshard')
- router_grad: float32 [768, 16], P('wshard')
- bias_table_grad: float32 [32, 12], P('wshard')
- expert_in_grad: float32 [16, 768, 3072], P('expert', None, 'wshard')
- expert_down_grad: float32 [16, 768, 3072], P('expert', None, 'wshard')
Inputs may be any that keep to these rules, and one draw needn't show every extreme that they name: `routes`: among the 128 tokens of one device no expert is chosen more than 12 times, and in every draw one expert is chosen exactly 12 times by the tokens of every device.
All inputs are finite; a program needn't handle non-finite values.
Results may differ from a plain program's by a relative error of at most 0.025.
Values may be sent and summed in bfloat16 or wider, within the bound.
No kernel may reach another device: no remote copies, remote signals or barrier semaphores. Data moves between devices by JAX's collectives and lax.ppermute only.
A program may use at most 320 MiB of HBM per device.

v0:
```python
import jax
import jax.numpy as jnp
from jax import lax
from jax.sharding import PartitionSpec as P

FULL_PRECISION = lax.Precision.HIGHEST


def norm_rows(values, gain):
    scale = lax.rsqrt(jnp.mean(values * values, axis=-1, keepdims=True) + 1e-06)
    return values * scale * gain


def toeplitz_bias(vector, query_start, key_start, query_count, key_count, key_total):
    row_index = query_start + jnp.arange(query_count, dtype=jnp.int32)
    column_index = key_start + jnp.arange(key_count, dtype=jnp.int32)
    offsets = column_index[None, :] - row_index[:, None] + (key_total - 1)
    return jnp.take(vector, offsets, axis=1)


def diagonal_sums(score_block):
    head_count, query_count, key_count = score_block.shape
    flipped = score_block[:, ::-1, :]
    padded = jnp.pad(flipped, ((0, 0), (0, 0), (0, query_count)))
    padded = padded.reshape(head_count, query_count * (key_count + query_count))
    kept_part = padded[:, : query_count * (key_count + query_count - 1)]
    kept_part = kept_part.reshape(head_count, query_count, key_count + query_count - 1)
    return jnp.sum(kept_part, axis=1)


def attend_forward(queries, key_rows, value_rows, bias_vec, query_base):
    row_count, head_count, head_dim = queries.shape
    key_total = key_rows.shape[0]
    query_block = min(512, row_count)
    key_block = min(1024, key_total)

    def one_query_block(block_index):
        query_start = block_index * query_block

        def one_advance(step_index, loop_state):
            running_top, running_mass, running_sum = loop_state
            key_start = step_index * key_block
            key_part = lax.dynamic_slice_in_dim(key_rows, key_start, key_block, 0)
            value_part = lax.dynamic_slice_in_dim(value_rows, key_start, key_block, 0)
            scores = jnp.einsum(
                "qhd,khd->hqk", queries, key_part, preferred_element_type=jnp.float32
            )
            scores = scores + toeplitz_bias(
                bias_vec, query_base + query_start, key_start, query_block, key_block, key_total
            )
            new_top = jnp.maximum(running_top, jnp.max(scores, axis=2))
            factor = jnp.exp(running_top - new_top)
            prob_block = jnp.exp(scores - new_top[:, :, None])
            running_mass = running_mass * factor + jnp.sum(prob_block, axis=2)
            running_sum = running_sum * factor[:, :, None] + jnp.einsum(
                "hqk,khd->hqd",
                prob_block.astype(jnp.bfloat16),
                value_part,
                preferred_element_type=jnp.float32,
            )
            return (new_top, running_mass, running_sum)

        start_state = (
            jnp.full((head_count, query_block), -jnp.inf, jnp.float32),
            jnp.zeros((head_count, query_block), jnp.float32),
            jnp.zeros((head_count, query_block, head_dim), jnp.float32),
        )
        final_top, final_mass, final_sum = lax.fori_loop(
            0, key_total // key_block, one_advance, start_state
        )
        output = (final_sum / final_mass[:, :, None]).transpose(1, 0, 2)
        log_mass = (final_top + jnp.log(final_mass)).T
        return (output, log_mass)

    outputs, masses = lax.map(
        one_query_block, jnp.arange(row_count // query_block, dtype=jnp.int32)
    )
    return (
        outputs.reshape(row_count, head_count * head_dim),
        masses.reshape(row_count, head_count),
    )


def sweep(
    query_rows,
    dout_rows,
    log_mass,
    row_delta,
    key_rows,
    value_rows,
    bias_vec,
    query_base,
    key_base,
    key_total,
    want_queries,
    want_keys,
):
    query_count, head_count, head_dim = query_rows.shape
    key_count = key_rows.shape[0]
    model_width = head_count * head_dim
    query_block = min(512 if want_queries else 2048, query_count)
    key_block = min(1024, key_count)
    key_steps = key_count // key_block
    query_steps = query_count // query_block
    placeholder = jnp.zeros((1,), jnp.float32)
    start_state = (
        (
            jnp.zeros((query_count, head_count, head_dim), jnp.float32)
            if want_queries
            else placeholder
        ),
        jnp.zeros((key_count, 2 * model_width), jnp.float32) if want_keys else placeholder,
        jnp.zeros(bias_vec.shape, jnp.float32) if want_queries else placeholder,
    )

    def sweep_advance(step_index, loop_state):
        query_grad, key_value_grad, bias_grad = loop_state
        query_start = step_index // key_steps * query_block
        key_start = step_index % key_steps * key_block
        query_part = lax.dynamic_slice_in_dim(query_rows, query_start, query_block, 0)
        dout_part = lax.dynamic_slice_in_dim(dout_rows, query_start, query_block, 0)
        mass_part = lax.dynamic_slice_in_dim(log_mass, query_start, query_block, 0).T
        delta_part = lax.dynamic_slice_in_dim(row_delta, query_start, query_block, 0).T
        key_part = lax.dynamic_slice_in_dim(key_rows, key_start, key_block, 0)
        value_part = lax.dynamic_slice_in_dim(value_rows, key_start, key_block, 0)
        scores = jnp.einsum(
            "qhd,khd->hqk", query_part, key_part, preferred_element_type=jnp.float32
        )
        scores = scores + toeplitz_bias(
            bias_vec,
            query_base + query_start,
            key_base + key_start,
            query_block,
            key_block,
            key_total,
        )
        prob_block = jnp.exp(scores - mass_part[:, :, None])
        prob_grad = jnp.einsum(
            "qhd,khd->hqk", dout_part, value_part, preferred_element_type=jnp.float32
        )
        score_grad = (prob_block * (prob_grad - delta_part[:, :, None])).astype(jnp.bfloat16)
        if want_queries:
            update = jnp.einsum(
                "hqk,khd->qhd", score_grad, key_part, preferred_element_type=jnp.float32
            )
            current = query_grad
            query_grad = current + update
            window_start = (
                key_base + key_start - query_base - query_start - (query_block - 1) + key_total - 1
            )
            window_size = query_block + key_block - 1
            previous = lax.dynamic_slice_in_dim(bias_grad, window_start, window_size, 1)
            bias_grad = lax.dynamic_update_slice_in_dim(
                bias_grad, previous + diagonal_sums(score_grad.astype(jnp.float32)), window_start, 1
            )
        if want_keys:
            key_update = jnp.einsum(
                "hqk,qhd->khd", score_grad, query_part, preferred_element_type=jnp.float32
            ).reshape(key_block, model_width)
            value_update = jnp.einsum(
                "hqk,qhd->khd",
                prob_block.astype(jnp.bfloat16),
                dout_part,
                preferred_element_type=jnp.float32,
            ).reshape(key_block, model_width)
            current_rows = key_value_grad
            joined_update = jnp.concatenate([key_update, value_update], axis=1)
            key_value_grad = current_rows + joined_update
        return (query_grad, key_value_grad, bias_grad)

    return lax.fori_loop(0, query_steps * key_steps, sweep_advance, start_state)


def local(
    tokens,
    gain_attn,
    gain_mix,
    attn_in,
    attn_out,
    router,
    bias_table,
    expert_in,
    expert_down,
    routes,
    buckets,
    out_grad,
):
    gain_one, gain_two, input_weight, output_weight, w_router, bias_rows = (
        lax.all_gather(gain_attn, "wshard", axis=0, tiled=True),
        lax.all_gather(gain_mix, "wshard", axis=0, tiled=True),
        lax.all_gather(attn_in, "wshard", axis=0, tiled=True),
        lax.all_gather(attn_out, "wshard", axis=0, tiled=True),
        lax.all_gather(router, "wshard", axis=0, tiled=True),
        lax.all_gather(bias_table, "wshard", axis=0, tiled=True),
    )
    w_up, w_down = (
        lax.all_gather(expert_in, "wshard", axis=2, tiled=True),
        lax.all_gather(expert_down, "wshard", axis=2, tiled=True),
    )
    source_rows = tokens[0].astype(jnp.float32)
    row_count, model_width = source_rows.shape
    head_count = bias_rows.shape[1]
    head_dim = model_width // head_count
    experts = w_router.shape[1]
    peer_count = lax.axis_size("expert")
    key_total = row_count * peer_count
    capacity = 3 * row_count // (2 * experts)
    query_base = lax.axis_index("expert") * row_count
    first_normalized, pull_one = jax.vjp(norm_rows, source_rows, gain_one.astype(jnp.float32))
    xn_one = first_normalized.astype(jnp.bfloat16)
    joined_heads = jnp.dot(xn_one, input_weight, preferred_element_type=jnp.float32).astype(
        jnp.bfloat16
    )
    query_heads = joined_heads[:, :model_width].reshape(row_count, head_count, head_dim)
    kv_all = lax.all_gather(joined_heads[:, model_width:], "expert", axis=0, tiled=True)
    keys_all = kv_all[:, :model_width].reshape(key_total, head_count, head_dim)
    values_all = kv_all[:, model_width:].reshape(key_total, head_count, head_dim)
    bucket_hot = (
        buckets[:, None] == jnp.arange(bias_rows.shape[0], dtype=jnp.int32)[None, :]
    ).astype(jnp.float32)
    bias_vec = jnp.dot(bucket_hot, bias_rows.astype(jnp.float32), precision=FULL_PRECISION).T
    mixed_f, log_mass = attend_forward(query_heads, keys_all, values_all, bias_vec, query_base)
    mixed_b = mixed_f.astype(jnp.bfloat16)
    post_attention_rows = source_rows + jnp.dot(
        mixed_b, output_weight, preferred_element_type=jnp.float32
    )
    normed_two, pull_two = jax.vjp(norm_rows, post_attention_rows, gain_two.astype(jnp.float32))
    xn_two = normed_two.astype(jnp.bfloat16)
    logits = jnp.dot(xn_two, w_router, preferred_element_type=jnp.float32)
    router_probs = jax.nn.softmax(logits, axis=-1)
    route_row = routes[0]
    chosen = route_row[:, None] == jnp.arange(experts, dtype=jnp.int32)[None, :]
    gate_values = jnp.sum(jnp.where(chosen, router_probs, 0.0), axis=1)
    counted = chosen.astype(jnp.int32)
    slot_rank = jnp.sum((jnp.cumsum(counted, axis=0) - 1) * counted, axis=1)
    slot_of = route_row * capacity + slot_rank
    token_of = (
        jnp.full((experts * capacity,), row_count, jnp.int32)
        .at[slot_of]
        .set(jnp.arange(row_count, dtype=jnp.int32))
    )

    def to_slots(row_values):
        padded = jnp.concatenate(
            [row_values, jnp.zeros((1, row_values.shape[1]), row_values.dtype)], axis=0
        )
        return jnp.take(padded, token_of, axis=0).reshape(experts, capacity, row_values.shape[1])

    received = lax.all_to_all(to_slots(xn_two), "expert", split_axis=0, concat_axis=1, tiled=True)
    pre_act = jnp.einsum("erd,edf->erf", received, w_up, preferred_element_type=jnp.float32)
    activated, gelu_pull = jax.vjp(jax.nn.gelu, pre_act)
    hidden = activated.astype(jnp.bfloat16)
    expert_out = jnp.einsum(
        "erf,edf->erd", hidden, w_down, preferred_element_type=jnp.float32
    ).astype(jnp.bfloat16)
    returned = lax.all_to_all(
        expert_out, "expert", split_axis=1, concat_axis=0, tiled=True
    ).reshape(experts * capacity, model_width)
    returned_rows = jnp.take(returned, slot_of, axis=0).astype(jnp.float32)
    result = post_attention_rows + gate_values[:, None] * returned_rows
    upstream = out_grad[0].astype(jnp.float32)
    gate_grad = jnp.sum(upstream * returned_rows, axis=1)
    row_grad = (gate_values[:, None] * upstream).astype(jnp.bfloat16)
    grad_received = lax.all_to_all(
        to_slots(row_grad), "expert", split_axis=0, concat_axis=1, tiled=True
    )
    hidden_grad = jnp.einsum(
        "erd,edf->erf", grad_received, w_down, preferred_element_type=jnp.float32
    )
    pre_grad = gelu_pull(hidden_grad)[0].astype(jnp.bfloat16)
    down_grad = jnp.einsum(
        "erd,erf->edf", grad_received, hidden, preferred_element_type=jnp.float32
    )
    up_grad = jnp.einsum("erd,erf->edf", received, pre_grad, preferred_element_type=jnp.float32)
    input_back = jnp.einsum(
        "erf,edf->erd", pre_grad, w_up, preferred_element_type=jnp.float32
    ).astype(jnp.bfloat16)
    returned_grad = lax.all_to_all(
        input_back, "expert", split_axis=1, concat_axis=0, tiled=True
    ).reshape(experts * capacity, model_width)
    expert_path = jnp.take(returned_grad, slot_of, axis=0).astype(jnp.float32)
    up_total, down_total = (
        lax.psum_scatter(
            up_grad.astype(jnp.bfloat16), "wshard", scatter_dimension=2, tiled=True
        ).astype(jnp.float32),
        lax.psum_scatter(
            down_grad.astype(jnp.bfloat16), "wshard", scatter_dimension=2, tiled=True
        ).astype(jnp.float32),
    )
    chosen_grad = jnp.where(chosen, gate_grad[:, None], 0.0)
    logit_grad = router_probs * (
        chosen_grad - jnp.sum(router_probs * chosen_grad, axis=1, keepdims=True)
    )
    router_part = jnp.dot(xn_two.astype(jnp.float32).T, logit_grad, precision=FULL_PRECISION)
    normed_two_grad = expert_path + jnp.dot(
        logit_grad, w_router.astype(jnp.float32).T, precision=FULL_PRECISION
    )
    resid_grad, gain_two_part = pull_two(normed_two_grad)
    resid_grad = resid_grad + upstream
    out_proj_part = jnp.dot(mixed_b.astype(jnp.float32).T, resid_grad, precision=FULL_PRECISION)
    mixed_low = jnp.dot(
        resid_grad, output_weight.astype(jnp.float32).T, precision=FULL_PRECISION
    ).astype(jnp.bfloat16)
    dout_heads = mixed_low.reshape(row_count, head_count, head_dim)
    row_delta = jnp.sum(
        (mixed_low.astype(jnp.float32) * mixed_f).reshape(row_count, head_count, head_dim), axis=2
    )
    query_all, dout_all = (
        lax.all_gather(joined_heads[:, :model_width], "expert", axis=0, tiled=True),
        lax.all_gather(mixed_low, "expert", axis=0, tiled=True),
    )
    mass_all, delta_all = (
        lax.all_gather(log_mass, "expert", axis=0, tiled=True),
        lax.all_gather(row_delta, "expert", axis=0, tiled=True),
    )
    local_keys = joined_heads[:, model_width : 2 * model_width].reshape(
        row_count, head_count, head_dim
    )
    local_values = joined_heads[:, 2 * model_width :].reshape(row_count, head_count, head_dim)
    first_pass = sweep(
        query_heads,
        dout_heads,
        log_mass,
        row_delta,
        keys_all,
        values_all,
        bias_vec,
        query_base,
        0,
        key_total,
        True,
        False,
    )
    query_grad = first_pass[0]
    bias_grad = first_pass[2]
    second_pass = sweep(
        query_all.reshape(key_total, head_count, head_dim),
        dout_all.reshape(key_total, head_count, head_dim),
        mass_all,
        delta_all,
        local_keys,
        local_values,
        bias_vec,
        0,
        query_base,
        key_total,
        False,
        True,
    )
    kv_grad = second_pass[1]
    joined_grad = jnp.concatenate(
        [query_grad.reshape(row_count, model_width), kv_grad], axis=1
    ).astype(jnp.bfloat16)
    in_proj_part = jnp.einsum("td,te->de", xn_one, joined_grad, preferred_element_type=jnp.float32)
    normed_one_grad = jnp.einsum(
        "te,de->td", joined_grad, input_weight, preferred_element_type=jnp.float32
    )
    source_grad, gain_one_part = pull_one(normed_one_grad)
    source_grad = source_grad + resid_grad
    table_part = jnp.dot(bucket_hot.T, bias_grad.T, precision=FULL_PRECISION)
    shard_sums = (
        lax.psum_scatter(
            gain_one_part.astype(jnp.bfloat16), "wshard", scatter_dimension=0, tiled=True
        ).astype(jnp.float32),
        lax.psum_scatter(
            gain_two_part.astype(jnp.bfloat16), "wshard", scatter_dimension=0, tiled=True
        ).astype(jnp.float32),
        lax.psum_scatter(
            in_proj_part.astype(jnp.bfloat16), "wshard", scatter_dimension=0, tiled=True
        ).astype(jnp.float32),
        lax.psum_scatter(
            out_proj_part.astype(jnp.bfloat16), "wshard", scatter_dimension=0, tiled=True
        ).astype(jnp.float32),
        lax.psum_scatter(
            router_part.astype(jnp.bfloat16), "wshard", scatter_dimension=0, tiled=True
        ).astype(jnp.float32),
        lax.psum_scatter(
            table_part.astype(jnp.bfloat16), "wshard", scatter_dimension=0, tiled=True
        ).astype(jnp.float32),
    )
    totals = (
        lax.psum(shard_sums[0].astype(jnp.bfloat16), "expert").astype(jnp.float32),
        lax.psum(shard_sums[1].astype(jnp.bfloat16), "expert").astype(jnp.float32),
        lax.psum(shard_sums[2].astype(jnp.bfloat16), "expert").astype(jnp.float32),
        lax.psum(shard_sums[3].astype(jnp.bfloat16), "expert").astype(jnp.float32),
        lax.psum(shard_sums[4].astype(jnp.bfloat16), "expert").astype(jnp.float32),
        lax.psum(shard_sums[5].astype(jnp.bfloat16), "expert").astype(jnp.float32),
    )
    return (
        result.astype(jnp.bfloat16)[None],
        source_grad.astype(jnp.bfloat16)[None],
        totals[0],
        totals[1],
        totals[2],
        totals[3],
        totals[4],
        totals[5],
        up_total,
        down_total,
    )


def solution(mesh):
    return jax.shard_map(
        local,
        mesh=mesh,
        in_specs=(
            P("wshard", "expert", None),
            P("wshard"),
            P("wshard"),
            P("wshard", None),
            P("wshard", None),
            P("wshard", None),
            P("wshard", None),
            P("expert", None, "wshard"),
            P("expert", None, "wshard"),
            P("wshard", "expert"),
            P(),
            P("wshard", "expert", None),
        ),
        out_specs=(
            P("wshard", "expert", None),
            P("wshard", "expert", None),
            P("wshard"),
            P("wshard"),
            P("wshard", None),
            P("wshard", None),
            P("wshard", None),
            P("wshard", None),
            P("expert", None, "wshard"),
            P("expert", None, "wshard"),
        ),
        check_vma=False,
    )
```

profile of v0, /device:TPU:0, one launch (start us, length us, event | category | flops | bytes accessed | tf_op | source)
XLA Modules:
  0.0 1714.3 jit_solution(8474630812538705393)
XLA Ops:
  11.6 13.6 all-reduce.11
  26.3 56.0 %all-gather.9.cloned.1.call-done = bf16[768,2304]{1,0:T(8,128)(2,1)} async-done(((bf16[192,2304]{1,0:T(8,128)(2,1)}), bf16[768,2304]{1,0:T(8,128)(2,1)}) %all-gather.9.cloned.1.call-update) | async-done | bytes 3538960 | tf_op jit(solution)/shard_map/all_gather | solution.py:191
  88.2 11.9 all_gather.42
  101.2 433.3 %gather_fusion.1 = f32[131072,12]{1,0:T(8,128)} fusion(f32[12,2047]{0,1:T(8,128)S(1)} %copy.72, s32[131072]{0:T(1024)S(1)} %broadcast_clamp_fusion), kind=kCustom, calls=%fused_computation.clone | custom fusion | bytes 13107200 | tf_op jit(solution)/shard_map/while/body/eval_jaxpr/while/body/eval_jaxpr/jit(_take)/gather | solution.py:18
  534.5 40.3 %copy.99 = f32[128,1024,12]{1,0,2:T(8,128)} copy(f32[128,1024,12]{2,1,0:T(8,128)} %bitcast.6) | data formatting | bytes 12582912 | tf_op jit(solution)/shard_map/while/body/eval_jaxpr/while/body/eval_jaxpr/jit(_take)/gather | solution.py:18
  574.8 13.1 all-gather
  616.9 8.3 all-to-all-done
  631.5 7.6 convolution_convert_fusion.6
  662.7 7.8 all-to-all-done.2
  679.3 7.4 convolution_convert_fusion.5
  703.8 433.3 %gather_fusion = f32[131072,12]{1,0:T(8,128)} fusion(f32[12,2047]{0,1:T(8,128)S(1)} %copy.72, s32[131072]{0:T(1024)S(1)} %fusion.36), kind=kCustom, calls=%fused_computation.5 | custom fusion | bytes 13107200 | tf_op jit(solution)/shard_map/while/body/eval_jaxpr/jit(_take)/gather | solution.py:18
  1137.1 37.0 %copy.104 = f32[1024,128,12]{1,0,2:T(8,128)} copy(f32[1024,128,12]{2,1,0:T(8,128)} %bitcast.41) | data formatting | bytes 12582912 | tf_op jit(solution)/shard_map/while/body/eval_jaxpr/jit(_take)/gather | solution.py:18
  1177.0 8.1 all_gather.49
  1185.1 7.3 fusion.1
  1195.7 10.0 all_gather.51
  1219.2 7.3 fusion.29
  1232.6 61.8 %reduce-scatter.8.cloned.1.call-done = bf16[192,2304]{1,0:T(8,128)(2,1)} async-done(((bf16[768,2304]{1,0:T(8,128)(2,1)}), bf16[192,2304]{1,0:T(8,128)(2,1)}) %reduce-scatter.8.cloned.1.call-update) | async-done | bytes 884752 | tf_op jit(solution)/shard_map/reduce_scatter | solution.py:368
  1294.4 8.1 convolution_convert_fusion
  1317.6 31.7 %rev.4 = f32[12,128,1024]{2,1,0:T(8,128)} reverse(bf16[12,128,1024]{2,1,0:T(8,128)(2,1)S(1)} %multiply_convert_fusion.1), dimensions={1} | reverse | bytes 9437184 | tf_op jit(solution)/shard_map/while/body/eval_jaxpr/rev | solution.py:23
  1363.2 16.0 reshape.295
  1387.8 16.1 all-reduce.10
  1404.1 23.1 %all-reduce.8 = (bf16[192]{0:T(256)(128)(2,1)S(1)}, bf16[192]{0:T(256)(128)(2,1)S(1)}, bf16[192,16]{0,1:T(8,128)(2,1)S(1)}, bf16[8,12]{1,0:T(8,128)(2,1)S(1)}) all-reduce(bf16[192]{0:T(256)(128)(2,1)S(1)} %dynamic-slice.3, bf16[192]{0:T(256)(128)(2,1)S(1)} %dynamic-slice.5, ...), channel_id=1, replica_groups=mesh['expert'=8,'wshard'=4] {'expert'}, use_global_device_ids=true, to_apply=%region_17.21 | all-reduce | flops 3552 | bytes 14208 | tf_op jit(solution)/shard_map/psum | solution.py:382
  1433.8 105.1 %reduce-scatter.14.cloned.1.call-done = bf16[2,768,768]{2,1,0:T(8,128)(2,1)} async-done(((bf16[2,768,3072]{2,1,0:T(8,128)(2,1)}), bf16[2,768,768]{2,1,0:T(8,128)(2,1)}) %reduce-scatter.14.cloned.1.call-update) | async-done | bytes 2359312 | tf_op jit(solution)/shard_map/reduce_scatter | solution.py:286
  1543.1 160.3 %reduce-scatter.12.cloned.1.call-done = bf16[2,768,768]{2,1,0:T(8,128)(2,1)} async-done(((bf16[2,768,3072]{2,1,0:T(8,128)(2,1)}), bf16[2,768,768]{2,1,0:T(8,128)(2,1)}) %reduce-scatter.12.cloned.1.call-update) | async-done | bytes 2359312 | tf_op jit(solution)/shard_map/reduce_scatter | solution.py:283
  (263 shorter events, 173.0 us)
Async XLA Ops:
  7.2 75.2 %all-gather.9.cloned.1.call-start = ((), (), s32[]{:S(2)}) async-start(), calls=%async_computation.9 | async-start | bytes 4423680 | tf_op jit(solution)/shard_map/all_gather | solution.py:191
  7.9 582.8 %all-gather.11.cloned.1.call-start = ((), (), s32[]{:S(2)}) async-start(), calls=%async_computation.10 | async-start | bytes 3538944 | tf_op jit(solution)/shard_map/all_gather | solution.py:215
  26.3 59.6 %copy-start.49 = (f32[128]{0:T(128)}, f32[128]{0:T(128)S(1)}, u32[]{:S(2)}) copy-start(f32[128]{0:T(128)S(1)} %fusion.56) | copy-start | bytes 1540
  26.3 59.6 %copy-start.44 = (f32[128]{0:T(128)}, f32[128]{0:T(128)S(1)}, u32[]{:S(2)}) copy-start(f32[128]{0:T(128)S(1)} %fusion.93) | copy-start | bytes 1540
  86.0 521.5 %all-gather.13.cloned.1.call-start = ((), (), s32[]{:S(2)}) async-start(), calls=%async_computation.11 | async-start | bytes 1474560 | tf_op jit(solution)/shard_map/all_gather | solution.py:192
  86.7 539.4 %all-gather.15.cloned.1.call-start = ((), (), s32[]{:S(2)}) async-start(), calls=%async_computation.12 | async-start | bytes 11796480 | tf_op jit(solution)/shard_map/all_gather | solution.py:197
  87.3 544.2 %all-gather.17.cloned.1.call-start = ((), (), s32[]{:S(2)}) async-start(), calls=%async_computation.13 | async-start | bytes 11796480 | tf_op jit(solution)/shard_map/all_gather | solution.py:198
  534.5 53.5 %copy-start.35 = (s32[1,128]{1,0:T(1,128)S(1)}, s32[1,128]{1,0:T(1,128)}, u32[]{:S(2)}) copy-start(s32[1,128]{1,0:T(1,128)} %param.27) | copy-start | bytes 1540
  612.7 12.5 all-to-all-start
  640.1 10.8 all-to-all-start.1
  644.8 54.7 %copy-start.36 = (f32[128]{0:T(128)}, f32[128]{0:T(128)S(1)}, u32[]{:S(2)}) copy-start(f32[128]{0:T(128)S(1)} %get-tuple-element.185) | copy-start | bytes 1540
  644.9 54.7 %copy-start.40 = (f32[128]{0:T(128)}, f32[128]{0:T(128)S(1)}, u32[]{:S(2)}) copy-start(f32[128]{0:T(128)S(1)} %fusion.79) | copy-start | bytes 1540
  652.2 47.4 %copy-start.38 = (f32[128]{0:T(128)}, f32[128]{0:T(128)S(1)}, u32[]{:S(2)}) copy-start(f32[128]{0:T(128)S(1)} %fusion.55) | copy-start | bytes 1540
  658.0 12.4 all-to-all-start.2
  662.1 513.1 %all-gather.19.cloned.1.call-start = ((), (), s32[]{:S(2)}) async-start(), calls=%async_computation.14 | async-start | bytes 1769472 | tf_op jit(solution)/shard_map/all_gather | solution.py:309
  687.8 10.8 all-to-all-start.3
  691.3 520.7 %all-gather.21.cloned.1.call-start = ((), (), s32[]{:S(2)}) async-start(), calls=%async_computation.15 | async-start | bytes 1769472 | tf_op jit(solution)/shard_map/all_gather | solution.py:310
  701.6 490.9 %copy-start.15 = (f32[128,768]{1,0:T(8,128)}, f32[128,768]{1,0:T(8,128)S(1)}, u32[]{:S(2)}) copy-start(f32[128,768]{1,0:T(8,128)S(1)} %get-tuple-element.174) | copy-start | bytes 1179652
  703.5 529.1 %reduce-scatter.10.cloned.1.call-start = ((), (), s32[]{:S(2)}) async-start(), calls=%async_computation.17 | async-start | bytes 1474560 | tf_op jit(solution)/shard_map/reduce_scatter | solution.py:371
  1194.7 99.7 %reduce-scatter.8.cloned.1.call-start = ((), (), s32[]{:S(2)}) async-start(), calls=%async_computation.16 | async-start | bytes 4423680 | tf_op jit(solution)/shard_map/reduce_scatter | solution.py:368
  1230.6 86.2 %reduce-scatter.16.cloned.1.call-start = ((), (), s32[]{:S(2)}) async-start(), calls=%async_computation.20 | async-start | bytes 245760
  1232.5 197.9 %all-reduce.14.cloned.1.call-start = ((), (), s32[]{:S(2)}) async-start(), calls=%async_computation.21 | async-start | bytes 2359296 | tf_op jit(solution)/shard_map/psum | solution.py:384
  1294.4 244.5 %reduce-scatter.14.cloned.1.call-start = ((), (), s32[]{:S(2)}) async-start(), calls=%async_computation.19 | async-start | bytes 11796480 | tf_op jit(solution)/shard_map/reduce_scatter | solution.py:286
  1302.5 400.9 %reduce-scatter.12.cloned.1.call-start = ((), (), s32[]{:S(2)}) async-start(), calls=%async_computation.18 | async-start | bytes 11796480 | tf_op jit(solution)/shard_map/reduce_scatter | solution.py:283
  (46 other events, 465.1 us)
Sparse Core Ops, SparseCore 0:
  9.6 72.7 all-gather.8
  86.1 30.8 all-gather.10
  118.6 30.4 all-gather.12
  150.5 165.8 all-gather.14
  317.8 164.9 all-gather.16
  664.6 24.2 all-gather.18
  703.7 22.0 all-gather.20
  1194.8 26.4 reduce-scatter.9
  1230.7 63.6 reduce-scatter.7
  1297.0 19.6 reduce-scatter.15
  1320.3 55.4 all-reduce.13
  1378.0 160.7 reduce-scatter.13
  1541.2 162.1 reduce-scatter.11
where the time goes:
time: 1720 us; the launch traced here: 1710 us
  local copies, waits for them, and re-layouts  1050 us (61%)
  waiting for transfers between devices  421 us (24%)
  blocking collectives  95.9 us (6%)
  matrix products  92.7 us (5%)
  other arithmetic  26.2 us (2%)
    gather x4, local copies, waits for them, and re-layouts, toeplitz_bias(): return jnp.take(vector, offsets, axis=1)  944 us
    reduce_scatter x1, waiting for transfers between devices, local(): lax.psum_scatter(up_grad.astype(jnp.bfloat16), 'wshard', scatter_dimensio...  160 us
    reduce_scatter x1, waiting for transfers between devices, local(): lax.psum_scatter(down_grad.astype(jnp.bfloat16), 'wshard', scatter_dimens...  105 us
    reduce_scatter x1, waiting for transfers between devices, local(): lax.psum_scatter(in_proj_part.astype(jnp.bfloat16), 'wshard', scatter_dim...  61.8 us
    all_gather x1, waiting for transfers between devices, local(): lax.all_gather(attn_in, 'wshard', axis=0, tiled=True)  56 us
  transfers between devices with their start and end apart: 17, of which 9 were waited for; matrix products, arithmetic and copies ran while one was open for 66% of the time, Pallas kernels for 0%

commit v1 on v0

v1 whole, which is shorter than its diff:
```python
import functools

import jax
import jax.numpy as jnp
from jax import lax
from jax.experimental import pallas as pl
from jax.experimental.pallas import tpu as pltpu
from jax.sharding import PartitionSpec as P

BF = jnp.bfloat16
F32 = jnp.float32
EPS = 1e-06
LANES = 128
VMEM_BYTES = 60 * 1024 * 1024
NN = (((1,), (0,)), ((), ()))
NT = (((1,), (1,)), ((), ()))
TN = (((0,), (0,)), ((), ()))


def dot(a, b, dims=NN):
    return lax.dot_general(a, b, dims, preferred_element_type=F32)


def dot_two(a, b, dims=NN):
    high = a.astype(BF)
    low = (a - high.astype(F32)).astype(BF)
    return dot(high, b, dims) + dot(low, b, dims)


def swap(x, axis, mask):
    count = lax.axis_size(axis)
    return lax.ppermute(x, axis, [(i, i ^ mask) for i in range(count)])


def tie(*groups):
    return lax.optimization_barrier(groups)


def chip_pieces(x):
    return [x] + [swap(x, "expert", mask) for mask in range(2, lax.axis_size("expert"), 2)]


def core_pieces(pieces):
    return [block for piece in pieces for block in (piece, swap(piece, "expert", 1))]


def gather_rows(x):
    count = lax.axis_size("wshard")
    mine = lax.axis_index("wshard")
    blocks = jnp.stack([x] + [swap(x, "wshard", mask) for mask in range(1, count)])
    return jnp.take(blocks, mine ^ jnp.arange(count), axis=0, mode="clip")


def weight_chunks(shard):
    rows, columns = shard.shape
    chips = lax.axis_size("expert") // 2
    if rows % (16 * chips) or columns % (2 * LANES):
        return [lax.all_gather(shard, "wshard", axis=0, tiled=True)]
    mine = lax.axis_index("expert")
    chunk = lax.dynamic_slice(
        shard,
        (mine // 2 * (rows // chips), mine % 2 * (columns // 2)),
        (rows // chips, columns // 2),
    )
    return [chunk] + [swap(chunk, "wshard", mask) for mask in range(1, lax.axis_size("wshard"))]


def place_weight(pieces, target, expert_id, shard_id, shards):
    if len(pieces) == 1:
        target[...] = pieces[0][...]
        return
    rows, columns = target.shape
    chips = len(pieces) // 2
    chunk = rows // shards // chips
    for mask, piece in enumerate(pieces):
        source = expert_id ^ mask
        column = pl.multiple_of(source % 2 * (columns // 2), LANES)
        for step in range(shards):
            row = (shard_id ^ step) * (rows // shards) + source // 2 * chunk
            target[pl.ds(pl.multiple_of(row, 16), chunk), pl.ds(column, columns // 2)] = piece[
                step * chunk : (step + 1) * chunk, :
            ]


def place_blocks(pieces, target, expert_id, change=None):
    for mask, piece in enumerate(pieces):
        count = piece.shape[0]
        start = pl.multiple_of((expert_id ^ mask) * count, count)
        block = piece[...]
        target[pl.ds(start, count), :] = block if change is None else change(block)


def bias_rows(window, head, rows, keys):
    row = window[pl.ds(head, 1), :]
    width = row.shape[1]
    spread = jnp.broadcast_to(row, (rows, width))
    return pltpu.roll(spread, width - (rows - 1), 1, stride=1, stride_axis=0)[:, :keys]


def pair_rows(block, head_dim):
    lane = lax.broadcasted_iota(jnp.int32, block.shape, 1)
    zero = jnp.zeros_like(block)
    return jnp.concatenate(
        [jnp.where(lane < head_dim, block, zero), jnp.where(lane < head_dim, zero, block)], axis=0
    )


def pair_join(both, rows, head_dim):
    lane = lax.broadcasted_iota(jnp.int32, (rows, both.shape[1]), 1)
    return jnp.where(lane < head_dim, both[:rows], both[rows:])


def bucket_hot(window_ref, buckets):
    width = window_ref.shape[1]
    index = lax.broadcasted_iota(jnp.int32, (buckets, width), 0)
    return (index == window_ref[...]).astype(BF)


def whole(shape):
    return pl.BlockSpec(shape, lambda *_: (0,) * len(shape))


def call(body, args, outs, scratch=(), name=None, us=1.0):
    ids = pl.BlockSpec(memory_space=pltpu.SMEM)
    return pl.pallas_call(
        body,
        in_specs=[ids] + [pl.BlockSpec(memory_space=pltpu.VMEM)] * (len(args) - 1),
        out_specs=[pl.BlockSpec(memory_space=pltpu.VMEM)] * len(outs),
        out_shape=[jax.ShapeDtypeStruct(shape, kind) for shape, kind in outs],
        scratch_shapes=list(scratch),
        compiler_params=pltpu.CompilerParams(vmem_limit_bytes=VMEM_BYTES),
        cost_estimate=cost(us),
        name=name,
    )(*args)


def cost(us):
    return pl.CostEstimate(flops=int(us * 1e9), bytes_accessed=int(us * 1e6), transcendentals=0)


def normalize(block, gain):
    values = block.astype(F32)
    scale = lax.rsqrt(jnp.mean(values * values, axis=1, keepdims=True) + EPS)
    return (values * scale * gain).astype(BF)


def forward_body(sizes, *refs):
    devices, shards, heads, head_dim, buckets, in_count = sizes
    refs = list(refs)
    ids = refs.pop(0)
    tokens = [refs.pop(0) for _ in range(devices)]
    in_pieces = [refs.pop(0) for _ in range(in_count)]
    gains, table, window_ref, mirror_ref = [refs.pop(0) for _ in range(4)]
    xn_all, joined, joined_own, ext, w_in, window, mirror = refs
    expert_id = ids[0]
    shard_id = ids[1]
    rows, width = tokens[0].shape
    keys = rows * devices
    gain_one = gains[0:1, :].astype(F32)
    place_blocks(tokens, xn_all, expert_id, lambda block: normalize(block, gain_one))
    place_weight(in_pieces, w_in, expert_id, shard_id, shards)
    column_block = 2 * LANES
    row_block = min(1024, keys)

    def project(step, carry):
        row = pl.multiple_of(step // (3 * width // column_block) * row_block, row_block)
        column = pl.multiple_of(step % (3 * width // column_block) * column_block, column_block)
        joined[pl.ds(row, row_block), pl.ds(column, column_block)] = dot(
            xn_all[pl.ds(row, row_block), :], w_in[:, pl.ds(column, column_block)]
        ).astype(BF)
        return carry

    lax.fori_loop(0, (3 * width // column_block) * (keys // row_block), project, 0)
    window[...] = dot(table[...], bucket_hot(window_ref, buckets))
    mirror[...] = dot(table[...], bucket_hot(mirror_ref, buckets))
    own = pl.multiple_of(expert_id * rows, rows)
    joined_own[...] = joined[pl.ds(own, rows), :]
    lane = lax.broadcasted_iota(jnp.int32, (rows, LANES), 1)

    def attend(pair, masses):
        column = pl.multiple_of(pair * LANES, LANES)
        queries = pair_rows(joined_own[:, pl.ds(column, LANES)], head_dim)
        scores = dot(queries, joined[:, pl.ds(width + column, LANES)], NT)
        scores = scores + jnp.concatenate(
            [bias_rows(window, 2 * pair + k, rows, keys) for k in range(2)], axis=0
        )
        top = jnp.max(scores, axis=1, keepdims=True)
        probs = jnp.exp(scores - top)
        mass = jnp.sum(probs, axis=1, keepdims=True)
        mixed = dot(probs.astype(BF), joined[:, pl.ds(2 * width + column, LANES)]) / mass
        ext[:, pl.ds(column, LANES)] = pair_join(mixed, rows, head_dim).astype(BF)
        total = top + jnp.log(mass)
        masses = jnp.where(lane == 2 * pair, total[:rows], masses)
        return jnp.where(lane == 2 * pair + 1, total[rows:], masses)

    masses = lax.fori_loop(0, heads // 2, attend, jnp.zeros((rows, LANES), F32))
    high = masses.astype(BF).astype(F32)
    middle = (masses - high).astype(BF).astype(F32)
    low = (masses - high - middle).astype(BF).astype(F32)
    ext[:, width:] = (high + pltpu.roll(middle, 32, 1) + pltpu.roll(low, 64, 1)).astype(BF)


def route_body(sizes, *refs):
    shards, experts, out_count = sizes
    refs = list(refs)
    ids = refs.pop(0)
    out_pieces = [refs.pop(0) for _ in range(out_count)]
    tokens, ext, gains, router, chosen, slots = [refs.pop(0) for _ in range(6)]
    after, gate, send, w_out = refs
    rows, width = tokens.shape
    place_weight(out_pieces, w_out, ids[0], ids[1], shards)
    lane = lax.broadcasted_iota(jnp.int32, (rows, LANES), 1)
    post = tokens[...].astype(F32) + dot(ext[:, :width], w_out[...])
    after[...] = post
    xn_two = normalize(post, gains[1:2, :].astype(F32))
    logits = jnp.where(lane < experts, dot(xn_two, router[...]), -1e30)
    weights = jnp.exp(logits - jnp.max(logits, axis=1, keepdims=True))
    weights = weights / jnp.sum(weights, axis=1, keepdims=True)
    gate[...] = jnp.broadcast_to(
        jnp.sum(weights * chosen[...].astype(F32), axis=1, keepdims=True), (rows, LANES)
    )
    send[...] = dot(slots[...], xn_two).astype(BF)


def slot_pick(count, total, capacity, which):
    row = lax.broadcasted_iota(jnp.int32, (count, total), 0)
    column = lax.broadcasted_iota(jnp.int32, (count, total), 1)
    block = total // count * capacity
    return (column == row // capacity * block + which * capacity + row % capacity).astype(BF)


def upstream_body(sizes, *refs):
    shards, per_device, capacity = sizes
    refs = list(refs)
    chunks = [refs.pop(0) for _ in range(shards)]
    w_down, up_ref, spread_ref = refs
    total = chunks[0].shape[0]
    count = total // per_device
    pick = slot_pick(count, total, capacity, pl.program_id(0))
    for step, chunk in enumerate(chunks):
        up_ref[0, step * count : (step + 1) * count, :] = dot(pick, chunk[...]).astype(BF)
    spread_ref[0] = dot(up_ref[0], w_down[0])


def expert_body(sizes, ids, rows_in, ups_in, spread_in, w_up, router, back_ref, x_ref, up_ref, hidden_ref, pre_ref, logit_ref):
    experts, per_device, capacity = sizes
    which = pl.program_id(0)
    mine = ids[0] * per_device + which
    total = rows_in.shape[0]
    count = total // per_device
    pick = slot_pick(count, total, capacity, which)
    x = dot(pick, rows_in[...]).astype(BF)
    lane = lax.broadcasted_iota(jnp.int32, (count, LANES), 1)
    logits = jnp.where(lane < experts, dot(x, router[...]), -1e30)
    probs = jnp.exp(logits - jnp.max(logits, axis=1, keepdims=True))
    probs = probs / jnp.sum(probs, axis=1, keepdims=True)
    hot = (lane == mine).astype(F32)
    gate = jnp.sum(probs * hot, axis=1, keepdims=True)
    pre = dot(x, w_up[0])
    inner = 0.7978845608028654 * (pre + 0.044715 * pre * pre * pre)
    bend = jnp.tanh(inner)
    hidden = 0.5 * pre * (1.0 + bend)
    slope = 0.5 * (1.0 + bend) + 0.5 * pre * (1.0 - bend * bend) * (
        0.7978845608028654 * (1.0 + 3.0 * 0.044715 * pre * pre)
    )
    hidden_low = hidden.astype(BF)
    spread = spread_in[0]
    gate_part = jnp.sum(hidden_low.astype(F32) * spread, axis=1, keepdims=True)
    pre_grad = (gate * spread * slope).astype(BF)
    logit_grad = gate_part * probs * (hot - gate)
    back = dot(pre_grad, w_up[0], NT) + dot_two(logit_grad, router[...], NT)
    x_ref[0] = x
    up_ref[0] = (gate * ups_in[0].astype(F32)).astype(BF)
    hidden_ref[0] = hidden_low
    pre_ref[0] = pre_grad
    logit_ref[0] = logit_grad
    back = dot(pick, back.astype(BF), TN).astype(BF)

    @pl.when(which == 0)
    def _():
        back_ref[...] = back

    @pl.when(which > 0)
    def _():
        back_ref[...] = (back_ref[...].astype(F32) + back.astype(F32)).astype(BF)


def expert_weights_body(sizes, *refs):
    shards, per_device, capacity = sizes
    refs = list(refs)
    x, up, hidden, pre, logit = [
        jnp.concatenate([refs.pop(0)[0] for _ in range(shards)], axis=0) for _ in range(5)
    ]
    w_down = refs.pop(0)
    out_refs = [refs.pop(0) for _ in range(shards)]
    up_grad, down_grad, router_part = refs
    which = pl.program_id(0)
    down_grad[0] = dot(up, hidden, TN)
    up_grad[0] = dot(x, pre, TN)
    router_add = dot_two(logit, x, TN)
    out = dot(hidden, w_down[0], NT).astype(BF)
    count = out.shape[0] // shards
    total = count * per_device
    pick = slot_pick(count, total, capacity, which)
    parts = [dot(pick, out[m * count : (m + 1) * count], TN).astype(BF) for m in range(shards)]

    @pl.when(which == 0)
    def _():
        router_part[...] = router_add
        for ref, part in zip(out_refs, parts):
            ref[...] = part

    @pl.when(which > 0)
    def _():
        router_part[...] = router_part[...] + router_add
        for ref, part in zip(out_refs, parts):
            ref[...] = (ref[...].astype(F32) + part.astype(F32)).astype(BF)


def norm_back(values, gain, grad):
    scale = lax.rsqrt(jnp.mean(values * values, axis=1, keepdims=True) + EPS)
    unit = values * scale
    inner = grad * gain
    gain_grad = jnp.sum(grad * unit, axis=0, keepdims=True)
    return scale * (inner - unit * jnp.mean(inner * unit, axis=1, keepdims=True)), gain_grad


def residual_body(ids, returned, back_slots, after, upstream, gains, resid, resid_low, gain_part):
    grad = dot(back_slots[...], returned[...])
    value, part = norm_back(after[...], gains[1:2, :].astype(F32), grad)
    value = value + upstream[...].astype(F32)
    resid[...] = value
    resid_low[...] = value.astype(BF)
    gain_part[...] = part


def result_body(ids, returned, back_slots, after, gate, result):
    rows = dot(back_slots[...], returned[...]).astype(BF).astype(F32)
    result[...] = (after[...] + gate[:, :1] * rows).astype(BF)


def diagonal_parts(block, width):
    rows, keys = block.shape
    total = jnp.zeros((8, width), F32)
    for group in range(rows // 8):
        part = jnp.concatenate(
            [block[group * 8 : group * 8 + 8], jnp.zeros((8, width - keys), F32)], axis=1
        )
        total = total + pltpu.roll(part, rows - 8 - 8 * group, 1)
    return total


def member_rows(head_rows, width, head_dim):
    head_of = lax.broadcasted_iota(jnp.int32, (head_rows, width), 1) // head_dim
    return (head_of == lax.broadcasted_iota(jnp.int32, (head_rows, width), 0)).astype(BF)


def part_rows(head_rows):
    part_of = lax.broadcasted_iota(jnp.int32, (head_rows, LANES), 1) % 32
    return (part_of == lax.broadcasted_iota(jnp.int32, (head_rows, LANES), 0)).astype(BF)


def query_body(sizes, ids, resid_low, ext, joined_own, w_out, window, window_ref, keys_in, values_in, query_grad, table_part, grads, delta, mass, diagonals):
    head_dim, buckets = sizes
    pair = pl.program_id(0)
    rows, width = resid_low.shape
    keys = keys_in.shape[0]
    head_rows, span = window.shape

    @pl.when(pair == 0)
    def _():
        low = dot(resid_low[...], w_out[...], NT).astype(BF)
        grads[...] = low
        product = low.astype(F32) * ext[:, :width].astype(F32)
        delta[...] = dot_two(product, member_rows(head_rows, width, head_dim), NT)
        mass[...] = dot(ext[:, width:], part_rows(head_rows), NT)

    head_lane = lax.broadcasted_iota(jnp.int32, (rows, head_rows), 1)

    def column_of(ref):
        return jnp.concatenate(
            [
                jnp.sum(jnp.where(head_lane == 2 * pair + k, ref[...], 0.0), axis=1, keepdims=True)
                for k in range(2)
            ],
            axis=0,
        )

    column = pl.multiple_of(pair * LANES, LANES)
    queries = pair_rows(joined_own[:, pl.ds(column, LANES)], head_dim)
    grad_own = pair_rows(grads[:, pl.ds(column, LANES)], head_dim)
    scores = dot(queries, keys_in[...], NT) + jnp.concatenate(
        [bias_rows(window, 2 * pair + k, rows, keys) for k in range(2)], axis=0
    )
    probs = jnp.exp(scores - column_of(mass))
    score_grad = (probs * (dot(grad_own, values_in[...], NT) - column_of(delta))).astype(BF)
    query_grad[0] = pair_join(dot(score_grad, keys_in[...]), rows, head_dim).astype(BF)
    wide = score_grad.astype(F32)
    for k in range(2):
        start = pl.multiple_of((2 * pair + k) * 8, 8)
        diagonals[pl.ds(start, 8), :] = diagonal_parts(wide[k * rows : (k + 1) * rows], span)

    @pl.when(pair == pl.num_programs(0) - 1)
    def _():
        every = diagonals[...]
        total_rows = every.shape[0]
        lined = jnp.zeros((total_rows, span), F32)
        place = lax.broadcasted_iota(jnp.int32, (total_rows, span), 0) % 8
        for step in range(8):
            moved = every if step == 7 else pltpu.roll(every, 7 - step, 1)
            lined = jnp.where(place == step, moved, lined)
        line_rows = lax.broadcasted_iota(jnp.int32, (head_rows, total_rows), 1) // 8
        fold = (line_rows == lax.broadcasted_iota(jnp.int32, (head_rows, total_rows), 0)).astype(BF)
        high = lined.astype(BF)
        low = (lined - high.astype(F32)).astype(BF)
        sums = dot(fold, high) + dot(fold, low)
        table_part[...] = dot_two(sums, bucket_hot(window_ref, buckets), NT)


def key_body(sizes, *refs):
    devices, heads, head_dim = sizes
    refs = list(refs)
    ids = refs.pop(0)
    resid_pieces = [refs.pop(0) for _ in range(devices)]
    ext_pieces = [refs.pop(0) for _ in range(devices)]
    joined_own, w_out, mirror, query_grad, queries_in = [refs.pop(0) for _ in range(5)]
    blocks, mixed_all, grads, delta_rows, mass_rows, mass_all = refs
    expert_id = ids[0]
    pair = pl.program_id(0)
    rows, width = resid_pieces[0].shape
    keys = rows * devices
    head_rows = mirror.shape[0]
    pairs = heads // 2

    @pl.when(pair == 0)
    def _():
        place_blocks(resid_pieces, grads, expert_id)
        for mask, piece in enumerate(ext_pieces):
            start = pl.multiple_of((expert_id ^ mask) * rows, rows)
            mixed_all[pl.ds(start, rows), :] = piece[:, :width]
            mass_all[pl.ds(start, rows), :] = piece[:, width:]
        mass_rows[...] = dot(part_rows(head_rows), mass_all[...], NT)
        member = member_rows(head_rows, width, head_dim)
        step = min(1024, keys)
        for start in range(0, keys, step):
            low = dot(grads[start : start + step, :], w_out[...], NT).astype(BF)
            grads[start : start + step, :] = low
            product = low.astype(F32) * mixed_all[start : start + step, :].astype(F32)
            high = product.astype(BF)
            rest = (product - high.astype(F32)).astype(BF)
            delta_rows[:, start : start + step] = dot(member, high, NT) + dot(member, rest, NT)
        blocks[:pairs] = query_grad[...]
        for block in range(pairs):
            blocks[3 * pairs + block] = resid_pieces[0][:, block * LANES : (block + 1) * LANES]
        for block in range(4 * pairs, blocks.shape[0]):
            blocks[block] = jnp.zeros((rows, LANES), BF)

    def row_of(ref):
        return jnp.concatenate(
            [jnp.broadcast_to(ref[pl.ds(2 * pair + k, 1), :], (rows, keys)) for k in range(2)],
            axis=0,
        )

    column = pl.multiple_of(pair * LANES, LANES)
    grad_all = grads[:, pl.ds(column, LANES)]
    key_own = pair_rows(joined_own[:, pl.ds(width + column, LANES)], head_dim)
    value_own = pair_rows(joined_own[:, pl.ds(2 * width + column, LANES)], head_dim)
    scores = dot(key_own, queries_in[...], NT) + jnp.concatenate(
        [bias_rows(mirror, 2 * pair + k, rows, keys) for k in range(2)], axis=0
    )
    probs = jnp.exp(scores - row_of(mass_rows))
    score_grad = (probs * (dot(value_own, grad_all, NT) - row_of(delta_rows))).astype(BF)
    blocks[pairs + pair] = pair_join(dot(score_grad, queries_in[...]), rows, head_dim).astype(BF)
    blocks[2 * pairs + pair] = pair_join(dot(probs.astype(BF), grad_all), rows, head_dim).astype(BF)


def source_body(ids, blocks, w_in, tokens, gains, resid, tokens_grad, gain_part, joined):
    for block in range(joined.shape[1] // LANES):
        joined[:, block * LANES : (block + 1) * LANES] = blocks[block]
    grad = dot(joined[...], w_in[...], NT)
    value, part = norm_back(tokens[...].astype(F32), gains[0:1, :].astype(F32), grad)
    tokens_grad[...] = (value + resid[...]).astype(BF)
    gain_part[...] = part


def weight_body(per, pairs, ids, xn_all, mixed_all, received, part, columns):
    devices, _, rows, _ = received.shape
    for source in range(devices):
        for block in range(per):
            columns[source * rows : (source + 1) * rows, block * LANES : (block + 1) * LANES] = received[
                source, block
            ]
    for block in range(per):
        inside = ids[0] * per + block < 3 * pairs
        line = slice(block * LANES, (block + 1) * LANES)

        @pl.when(inside)
        def _():
            part[:, line] = dot(xn_all[...], columns[:, line], TN).astype(BF)

        @pl.when(jnp.logical_not(inside))
        def _():
            part[:, line] = dot(mixed_all[...], columns[:, line], TN).astype(BF)


def spread_body(per, pairs, ids, *refs):
    pieces, (in_grad, out_grad) = refs[:-2], refs[-2:]
    for mask, piece in enumerate(pieces):
        source = ids[0] ^ mask
        for block in range(per):
            index = source * per + block
            values = piece[:, block * LANES : (block + 1) * LANES].astype(F32)

            @pl.when(index < 3 * pairs)
            def _():
                in_grad[:, pl.ds(pl.multiple_of(index * LANES, LANES), LANES)] = values

            @pl.when(jnp.logical_and(index >= 3 * pairs, index < 4 * pairs))
            def _():
                out_grad[:, pl.ds(pl.multiple_of((index - 3 * pairs) * LANES, LANES), LANES)] = values


def pad_to(x, shape):
    return jnp.pad(x, [(0, size - have) for size, have in zip(shape, x.shape)])


def local(
    tokens, gain_attn, gain_mix, attn_in, attn_out, router, bias_table, expert_in, expert_down, routes, buckets, out_grad
):
    own_tokens = tokens[0]
    own_grad = out_grad[0]
    rows, width = own_tokens.shape
    devices = lax.axis_size("expert")
    shards = lax.axis_size("wshard")
    expert_id = lax.axis_index("expert")
    shard_id = lax.axis_index("wshard")
    heads = bias_table.shape[1]
    head_dim = width // heads
    experts = router.shape[1]
    bucket_count = bias_table.shape[0] * shards
    per_device = expert_in.shape[0]
    keys = rows * devices
    capacity = 3 * rows // (2 * experts)
    part = width // shards
    ids = jnp.stack([expert_id, shard_id]).astype(jnp.int32)

    in_chunks = weight_chunks(attn_in)
    token_pieces, in_chunks, attn_out, own_grad = tie(
        chip_pieces(own_tokens), in_chunks, attn_out, own_grad
    )
    out_chunks = weight_chunks(attn_out)
    chunked = len(in_chunks) > 1
    if chunked:
        in_pieces = chip_pieces(jnp.concatenate(in_chunks, axis=0))
    token_pieces = core_pieces(token_pieces)
    if chunked:
        in_pieces = core_pieces(in_pieces)
    else:
        in_pieces = in_chunks
    small_columns = -(-(experts + 2 + heads) // LANES) * LANES
    table_rows = bias_table.shape[0]
    small = jnp.concatenate(
        [
            router,
            gain_attn[:, None],
            gain_mix[:, None],
            pad_to(bias_table, (part, heads)),
            jnp.zeros((part, small_columns - experts - 2 - heads), BF),
        ],
        axis=1,
    )
    small = gather_rows(small)
    router_all = small[:, :, :experts].reshape(width, experts)
    router_pad = pad_to(router_all, (width, LANES))
    gains = pad_to(small[:, :, experts : experts + 2].reshape(width, 2).T, (8, width))
    table = small[:, :table_rows, experts + 2 : experts + 2 + heads].reshape(bucket_count, heads)
    head_rows = 16
    table_t = pad_to(table.T, (head_rows, bucket_count))

    window_width = keys + rows
    start = keys - 1 - expert_id * rows - (rows - 1)
    window_buckets = lax.dynamic_slice(jnp.pad(buckets, (0, rows)), (start,), (window_width,))
    mirror_buckets = lax.dynamic_slice(jnp.pad(buckets[::-1], (0, rows)), (start,), (window_width,))
    last = jnp.arange(window_width) == window_width - 1
    window_buckets = jnp.where(last, -1, window_buckets)[None]
    mirror_buckets = jnp.where(last, -1, mirror_buckets)[None]

    route = routes[0]
    earlier = jnp.arange(rows)[None, :] < jnp.arange(rows)[:, None]
    rank = jnp.sum(((route[None, :] == route[:, None]) & earlier).astype(jnp.int32), axis=1)
    slot = route * capacity + rank
    slot_count = experts * capacity
    slots = (jnp.arange(slot_count)[:, None] == slot[None, :]).astype(BF)
    back_slots = (slot[:, None] == jnp.arange(slot_count)[None, :]).astype(BF)
    chosen = (route[:, None] == jnp.arange(LANES)[None, :]).astype(BF)

    block = per_device * capacity

    def scatter_rows(parts):
        mine = lax.dynamic_index_in_dim(parts, shard_id, 0, keepdims=False).astype(F32)
        for mask in range(1, shards):
            sent = lax.dynamic_index_in_dim(parts, shard_id ^ mask, 0, keepdims=False)
            mine = mine + swap(sent, "wshard", mask).astype(F32)
        return mine

    def sum_lines(lines):
        lines = lines.reshape(lines.shape[0], shards, part).transpose(1, 0, 2)
        lines = scatter_rows(lines)
        mask = 1
        while mask < devices:
            lines = lines + swap(lines, "expert", mask)
            mask *= 2
        return lines

    def exchange(slot_rows):
        blocks = slot_rows.reshape(devices, block, width)
        moved = lax.all_to_all(blocks, "expert", split_axis=0, concat_axis=0, tiled=True)
        return moved.reshape(devices * block, width)

    def to_shards(x):
        return [x] + [swap(x, "wshard", mask) for mask in range(1, shards)]

    def sum_back(parts):
        total = parts[0].astype(F32)
        for mask in range(1, shards):
            total = total + swap(parts[mask], "wshard", mask).astype(F32)
        return total.astype(BF)

    ups, in_pieces, out_chunks = tie(
        exchange(dot(slots, own_grad).astype(BF)), in_pieces, out_chunks
    )
    ups_chunks = to_shards(ups)
    if len(out_chunks) > 1:
        out_chunks = chip_pieces(jnp.concatenate(out_chunks, axis=0))

    sizes = (devices, shards, heads, head_dim, bucket_count, len(in_pieces))
    xn_all, joined, joined_own, ext, w_in, window, mirror = call(
        functools.partial(forward_body, sizes),
        [ids, *token_pieces, *in_pieces, gains, table_t, window_buckets, mirror_buckets],
        [
            ((keys, width), BF),
            ((keys, 3 * width), BF),
            ((rows, 3 * width), BF),
            ((rows, width + LANES), BF),
            ((width, 3 * width), BF),
            ((head_rows, window_width), F32),
            ((head_rows, window_width), F32),
        ],
        name="attention_forward",
        us=18.0,
    )
    out_pieces, ext = tie(out_chunks, ext)
    if len(out_pieces) > 1:
        out_pieces = core_pieces(out_pieces)
    after, gate, send, w_out = call(
        functools.partial(route_body, (shards, experts, len(out_pieces))),
        [ids, *out_pieces, own_tokens, ext, gains, router_pad, chosen, slots],
        [
            ((rows, width), F32),
            ((rows, LANES), F32),
            ((slot_count, width), BF),
            ((width, width), BF),
        ],
        name="route",
        us=4.0,
    )
    rows_own = exchange(send)
    row_chunks = to_shards(rows_own)
    ext_later, _ = tie(ext, rows_own)
    ext_pieces = core_pieces(chip_pieces(ext_later))
    total = devices * block
    count = total // per_device
    ff = expert_in.shape[2]
    by_expert = pl.BlockSpec((1, width, ff), lambda k: (k, 0, 0))
    kept_ff = pl.BlockSpec((1, count, ff), lambda k: (k, 0, 0))
    kept_width = pl.BlockSpec((1, count, width), lambda k: (k, 0, 0))
    kept_lanes = pl.BlockSpec((1, count, LANES), lambda k: (k, 0, 0))
    upstream_width = pl.BlockSpec((1, shards * count, width), lambda k: (k, 0, 0))
    upstream_ff = pl.BlockSpec((1, shards * count, ff), lambda k: (k, 0, 0))
    ups_all, spread_all = pl.pallas_call(
        functools.partial(upstream_body, (shards, per_device, capacity)),
        grid=(per_device,),
        in_specs=[whole((total, width))] * shards + [by_expert],
        out_specs=[upstream_width, upstream_ff],
        out_shape=[
            jax.ShapeDtypeStruct((per_device, shards * count, width), BF),
            jax.ShapeDtypeStruct((per_device, shards * count, ff), F32),
        ],
        compiler_params=pltpu.CompilerParams(vmem_limit_bytes=VMEM_BYTES),
        cost_estimate=cost(5.0),
        name="upstream",
    )(*ups_chunks, expert_down)
    rows_own, ups_all, spread_all = tie(rows_own, ups_all, spread_all)
    row_chunks = [rows_own] + row_chunks[1:]
    kept = [[], [], [], [], []]
    back_parts = []
    for step, row_chunk in enumerate(row_chunks):
        back, *saved = pl.pallas_call(
            functools.partial(expert_body, (experts, per_device, capacity)),
            grid=(per_device,),
            in_specs=[
                pl.BlockSpec(memory_space=pltpu.SMEM),
                whole((total, width)),
                pl.BlockSpec((1, count, width), lambda k, step=step: (k, step, 0)),
                pl.BlockSpec((1, count, ff), lambda k, step=step: (k, step, 0)),
                by_expert,
                whole((width, LANES)),
            ],
            out_specs=[whole((total, width)), kept_width, kept_width, kept_ff, kept_ff, kept_lanes],
            out_shape=[
                jax.ShapeDtypeStruct((total, width), BF),
                jax.ShapeDtypeStruct((per_device, count, width), BF),
                jax.ShapeDtypeStruct((per_device, count, width), BF),
                jax.ShapeDtypeStruct((per_device, count, ff), BF),
                jax.ShapeDtypeStruct((per_device, count, ff), BF),
                jax.ShapeDtypeStruct((per_device, count, LANES), F32),
            ],
            compiler_params=pltpu.CompilerParams(vmem_limit_bytes=VMEM_BYTES),
            cost_estimate=cost(5.0),
            name="experts",
        )(ids, row_chunk, ups_all, spread_all, expert_in, router_pad)
        back_parts.append(back)
        for group, value in zip(kept, saved):
            group.append(value)
    returned_grad = exchange(sum_back(back_parts))
    *out_parts, up_grad, down_grad, router_part = pl.pallas_call(
        functools.partial(expert_weights_body, (shards, per_device, capacity)),
        grid=(per_device,),
        in_specs=[kept_width] * (2 * shards)
        + [kept_ff] * (2 * shards)
        + [kept_lanes] * shards
        + [by_expert],
        out_specs=[whole((total, width))] * shards + [by_expert, by_expert, whole((LANES, width))],
        out_shape=[jax.ShapeDtypeStruct((total, width), BF)] * shards
        + [
            jax.ShapeDtypeStruct((per_device, width, ff), F32),
            jax.ShapeDtypeStruct((per_device, width, ff), F32),
            jax.ShapeDtypeStruct((LANES, width), F32),
        ],
        compiler_params=pltpu.CompilerParams(vmem_limit_bytes=VMEM_BYTES),
        cost_estimate=cost(8.0),
        name="expert_weights",
    )(*[value for group in kept for value in group], expert_down)
    resid, resid_low, gain_two_part = call(
        residual_body,
        [ids, returned_grad, back_slots, after, own_grad, gains],
        [((rows, width), F32), ((rows, width), BF), ((1, width), F32)],
        name="residual",
        us=2.0,
    )
    out_sum = sum_back(out_parts)
    resid_pieces = chip_pieces(resid_low)
    pairs = heads // 2

    def column_block(offset):
        return pl.BlockSpec((keys, LANES), lambda p: (0, offset * pairs + p))

    query_grad, table_part = pl.pallas_call(
        functools.partial(query_body, (head_dim, bucket_count)),
        grid=(pairs,),
        in_specs=[
            pl.BlockSpec(memory_space=pltpu.SMEM),
            whole((rows, width)),
            whole((rows, width + LANES)),
            whole((rows, 3 * width)),
            whole((width, width)),
            whole((head_rows, window_width)),
            whole((1, window_width)),
            column_block(1),
            column_block(2),
        ],
        out_specs=[pl.BlockSpec((1, rows, LANES), lambda p: (p, 0, 0)), whole((head_rows, bucket_count))],
        out_shape=[
            jax.ShapeDtypeStruct((pairs, rows, LANES), BF),
            jax.ShapeDtypeStruct((head_rows, bucket_count), F32),
        ],
        scratch_shapes=[
            pltpu.VMEM((rows, width), BF),
            pltpu.VMEM((rows, head_rows), F32),
            pltpu.VMEM((rows, head_rows), F32),
            pltpu.VMEM((head_rows * 8, window_width), F32),
        ],
        compiler_params=pltpu.CompilerParams(vmem_limit_bytes=VMEM_BYTES),
        cost_estimate=cost(10.0),
        name="query_grad",
    )(ids, resid_low, ext, joined_own, w_out, window, window_buckets, joined, joined)
    per = -(-4 * pairs // devices)
    resid_pieces, query_grad, table_part, out_sum = tie(resid_pieces, query_grad, table_part, out_sum)
    resid_pieces = core_pieces(resid_pieces)
    returned_rows = exchange(out_sum)
    table_line = table_part[:heads].T.reshape(shards, table_rows * heads)
    table_line = pad_to(table_line, (shards, part)).reshape(1, width)
    lines = sum_lines(jnp.concatenate([router_part[:experts], gain_two_part, table_line], axis=0))
    blocks, mixed_all = pl.pallas_call(
        functools.partial(key_body, (devices, heads, head_dim)),
        grid=(pairs,),
        in_specs=[pl.BlockSpec(memory_space=pltpu.SMEM)]
        + [whole((rows, width))] * devices
        + [whole((rows, width + LANES))] * devices
        + [
            whole((rows, 3 * width)),
            whole((width, width)),
            whole((head_rows, window_width)),
            whole((pairs, rows, LANES)),
            column_block(0),
        ],
        out_specs=[whole((per * devices, rows, LANES)), whole((keys, width))],
        out_shape=[
            jax.ShapeDtypeStruct((per * devices, rows, LANES), BF),
            jax.ShapeDtypeStruct((keys, width), BF),
        ],
        scratch_shapes=[
            pltpu.VMEM((keys, width), BF),
            pltpu.VMEM((head_rows, keys), F32),
            pltpu.VMEM((head_rows, keys), F32),
            pltpu.VMEM((keys, LANES), BF),
        ],
        compiler_params=pltpu.CompilerParams(vmem_limit_bytes=VMEM_BYTES),
        cost_estimate=cost(12.0),
        name="key_grad",
    )(ids, *resid_pieces, *ext_pieces, joined_own, w_out, mirror, query_grad, joined)
    blocks, lines, returned_rows = tie(blocks, lines, returned_rows)
    received = lax.all_to_all(
        blocks.reshape(devices, per, rows, LANES), "expert", split_axis=0, concat_axis=0, tiled=True
    )
    (result,) = call(
        result_body,
        [ids, returned_rows, back_slots, after, gate],
        [((rows, width), BF)],
        name="result",
        us=2.0,
    )
    tokens_grad, gain_one_part = call(
        source_body,
        [ids, blocks, w_in, own_tokens, gains, resid],
        [((rows, width), BF), ((1, width), F32)],
        [pltpu.VMEM((rows, 3 * width), BF)],
        name="source_grad",
        us=4.0,
    )
    (weight_part,) = call(
        functools.partial(weight_body, per, pairs),
        [ids, xn_all, mixed_all, received],
        [((width, per * LANES), BF)],
        [pltpu.VMEM((keys, per * LANES), BF)],
        name="weight_grads",
        us=4.0,
    )

    mine = scatter_rows(weight_part.reshape(shards, part, per * LANES)).astype(BF)
    attn_in_grad, attn_out_grad = call(
        functools.partial(spread_body, per, pairs),
        [ids, *core_pieces(chip_pieces(mine))],
        [((part, 3 * width), F32), ((part, width), F32)],
        name="spread",
        us=2.0,
    )

    (gain_line,) = sum_lines(gain_one_part)
    router_grad = lines[:experts].T
    table_grad = lines[experts + 1, : table_rows * heads].reshape(table_rows, heads)
    return (
        result[None],
        tokens_grad[None],
        gain_line,
        lines[experts],
        attn_in_grad,
        attn_out_grad,
        router_grad,
        table_grad,
        up_grad,
        down_grad,
    )


def solution(mesh):
    return jax.shard_map(
        local,
        mesh=mesh,
        in_specs=(
            P("wshard", "expert", None),
            P("wshard"),
            P("wshard"),
            P("wshard", None),
            P("wshard", None),
            P("wshard", None),
            P("wshard", None),
            P("expert", None, "wshard"),
            P("expert", None, "wshard"),
            P("wshard", "expert"),
            P(),
            P("wshard", "expert", None),
        ),
        out_specs=(
            P("wshard", "expert", None),
            P("wshard", "expert", None),
            P("wshard"),
            P("wshard"),
            P("wshard", None),
            P("wshard", None),
            P("wshard", None),
            P("wshard", None),
            P("expert", None, "wshard"),
            P("expert", None, "wshard"),
        ),
        check_vma=False,
    )
```

time: 1720 us -> 318 us (0.18)
  local copies, waits for them, and re-layouts: 1050 us -> 24.4 us
  waiting for transfers between devices: 421 us -> 79.7 us
  Pallas kernels: 0 us -> 101 us
  blocking collectives: 95.9 us -> 0 us
  matrix products: 92.7 us -> 2.03 us
  starting transfers between devices: 16.4 us -> 97.4 us
    gather x8 -> x1, local copies, waits for them, and re-layouts: 948 us -> 0.59 us  [gather_rows(): return jnp.take(blocks, mine ^ jnp.arange(count), axis=0, mode='clip')]
    reduce_scatter x4 -> x0, waiting for transfers between devices: 327 us -> none  [the longest x1 160 us: local(): lax.psum_scatter(up_grad.astype(jnp.bfloat16), 'wshard', scatter_dimensio...]
    pallas_call x0 -> x15, Pallas kernels: none -> 101 us  [the longest x7 38.6 us: call(): pl.pallas_call(body, in_specs=[ids] + [pl.BlockSpec(memory_space=pltpu.VM...]
    dot_general x24 -> x1, matrix products: 92.7 us -> 2.03 us  [dot(): return lax.dot_general(a, b, dims, preferred_element_type=F32)]
    ppermute x0 -> x78, starting transfers between devices: none -> 78.8 us  [swap(): return lax.ppermute(x, axis, [(i, i ^ mask) for i in range(count)])]
    ppermute x0 -> x78, waiting for transfers between devices: none -> 76.8 us  [swap(): return lax.ppermute(x, axis, [(i, i ^ mask) for i in range(count)])]
    all_gather x7 -> x0, waiting for transfers between devices: 56.1 us -> none  [the longest x1 56 us: local(): lax.all_gather(attn_in, 'wshard', axis=0, tiled=True)]
    all_gather x4 -> x0, blocking collectives: 43.1 us -> none  [the longest x1 13.1 us: local(): lax.all_gather(router, 'wshard', axis=0, tiled=True)]
  transfers between devices with their start and end apart: 17 -> 83, of which waited for: 9 -> 23; matrix products, arithmetic and copies ran while one was open for 66% -> 8% of each run, Pallas kernels for 0% -> 31%
where the time goes in v1:
time: 318 us; the launch traced here: 316 us
  Pallas kernels  101 us (32%)
  starting transfers between devices  97.4 us (31%)
  waiting for transfers between devices  79.7 us (25%)
  local copies, waits for them, and re-layouts  24.4 us (8%)
  other arithmetic  9.88 us (3%)
    ppermute x78, starting transfers between devices, swap(): return lax.ppermute(x, axis, [(i, i ^ mask) for i in range(count)])  78.8 us
    ppermute x78, waiting for transfers between devices, swap(): return lax.ppermute(x, axis, [(i, i ^ mask) for i in range(count)])  76.8 us
    pallas_call x7, Pallas kernels, call(): pl.pallas_call(body, in_specs=[ids] + [pl.BlockSpec(memory_space=pltpu.VM...  38.6 us
    pallas_call x4, Pallas kernels, local(): pl.pallas_call(functools.partial(expert_body, (experts, per_device, capac...  23 us
    all_to_all x4, starting transfers between devices, exchange(): lax.all_to_all(blocks, 'expert', split_axis=0, concat_axis=0, tiled=True)  14.5 us
    pallas_call x1, Pallas kernels, local(): pl.pallas_call(functools.partial(key_body, (devices, heads, head_dim)), g...  12.7 us
    pallas_call x1, Pallas kernels, local(): pl.pallas_call(functools.partial(query_body, (head_dim, bucket_count)), g...  11.4 us
    unnamed x124, local copies, waits for them, and re-layouts  11.2 us
  transfers between devices with their start and end apart: 83, of which 23 were waited for; matrix products, arithmetic and copies ran while one was open for 8% of the time, Pallas kernels for 31%

profile of v1, /device:TPU:0, one launch (start us, length us, event | category | flops | bytes accessed | tf_op | source)
XLA Modules:
  0.0 315.6 jit_solution(7482605751666326448)
XLA Ops:
  18.8 6.2 %collective-permute-done.5 = bf16[48,1152]{1,0:T(8,128)(2,1)S(1)} collective-permute-done((bf16[48,1152]{1,0:T(8,128)(2,1)S(1)}, bf16[48,1152]{1,0:T(8,128)(2,1)S(1)}, u32[]{:S(2)}, u32[]{:S(2)}) %collective-permute-start.5) | collective-permute-done | bytes 110624 | tf_op jit(solution)/shard_map/ppermute | solution.py:32
  37.1 7.2 %collective-permute-done.9.refs_13_ = bf16[192,1152]{1,0:T(8,128)(2,1)S(1)} collective-permute-done((bf16[192,1152]{1,0:T(8,128)(2,1)S(1)}, bf16[192,1152]{1,0:T(8,128)(2,1)S(1)}, u32[]{:S(2)}, u32[]{:S(2)}) %collective-permute-start.9) | collective-permute-done | bytes 442400 | tf_op jit(solution)/shard_map/ppermute | solution.py:32
  47.6 3.7 %all-to-all-start = ((bf16[8,24,768]{2,1,0:T(8,128)(2,1)}), bf16[8,24,768]{2,1,0:T(8,128)(2,1)S(1)}, u32[]{:S(2)}, u32[]{:S(2)}) async-start(bf16[8,24,768]{2,1,0:T(8,128)(2,1)} %bitcast.7), calls=%async_computation | async-start | bytes 589824 | tf_op jit(solution)/shard_map/all_to_all | solution.py:617
  58.5 4.1 %collective-permute-done.15 = bf16[48,384]{1,0:T(8,128)(2,1)S(1)} collective-permute-done((bf16[48,384]{1,0:T(8,128)(2,1)S(1)}, bf16[48,384]{1,0:T(8,128)(2,1)S(1)}, u32[]{:S(2)}, u32[]{:S(2)}) %collective-permute-start.15) | collective-permute-done | bytes 36896 | tf_op jit(solution)/shard_map/ppermute | solution.py:32
  67.4 18.0 %attention_forward.1 = (bf16[1024,768]{1,0:T(8,128)(2,1)}, bf16[1024,2304]{1,0:T(8,128)(2,1)}, bf16[128,2304]{1,0:T(8,128)(2,1)}, bf16[128,896]{1,0:T(8,128)(2,1...) custom-call(s32[2]{0:T(128)} %pad_add_fusion.refs_0_.ids, bf16[128,768]{1,0:T(8,128)(2,1)} %bitcast.121, ...), custom_call_target="tpu_custom_call" | custom-call | flops 17999998976 | bytes 18000000 | tf_op jit(solution)/shard_map/attention_forward/pallas_call | solution.py:125
  96.4 3.8 %all-to-all-start.1 = ((bf16[8,24,768]{2,1,0:T(8,128)(2,1)}), bf16[8,24,768]{2,1,0:T(8,128)(2,1)S(1)}, u32[]{:S(2)}, u32[]{:S(2)}) async-start(bf16[8,24,768]{2,1,0:T(8,128)(2,1)} %bitcast.99), calls=%async_computation.1 | async-start | bytes 589824 | tf_op jit(solution)/shard_map/all_to_all | solution.py:617
  101.6 9.3 %collective-permute-done.31.refs_2_ = bf16[192,768]{1,0:T(8,128)(2,1)S(1)} collective-permute-done((bf16[192,768]{1,0:T(8,128)(2,1)S(1)}, bf16[192,768]{1,0:T(8,128)(2,1)S(1)}, u32[]{:S(2)}, u32[]{:S(2)}) %collective-permute-start.31) | collective-permute-done | bytes 294944 | tf_op jit(solution)/shard_map/ppermute | solution.py:32
  112.3 4.2 %upstream.1 = (bf16[2,384,768]{2,1,0:T(8,128)(2,1)}, f32[2,384,768]{2,1,0:T(8,128)}) custom-call(bf16[192,768]{1,0:T(8,128)(2,1)} %bitcast.93, bf16[192,768]{1,0:T(8,128)(2,1)} %copy-done.17, bf16[192,768]{1,0:T(8,128)(2,1)} %copy-done.19, bf16[192,768]{1,0:T(8,128)(2,1)} %copy-done.20, bf16[2,768,768]{2,1,0:T(8,128)(2,1)} %refs_20_.1), custom_call_target="tpu_custom_call" | custom-call | flops 5000000000 | bytes 5000000 | tf_op jit(solution)/shard_map/upstream/pallas_call | solution.py:680
  116.5 5.4 %collective-permute-start.33 = (bf16[192,768]{1,0:T(8,128)(2,1)S(1)}, bf16[192,768]{1,0:T(8,128)(2,1)S(1)}, u32[]{:S(2)}, u32[]{:S(2)}) collective-permute-start(bf16[192,768]{1,0:T(8,128)(2,1)S(1)} %bitcast.95), channel_id=1, source_target_pairs={{0,1},{1,0},{2,3},{3,2},{4,5},{5,4},{6,7},{7,6},{8,9},{9,8},{10,11... | collective-permute-start | bytes 884744 | tf_op jit(solution)/shard_map/ppermute | solution.py:32
  124.3 5.7 %experts.4 = (bf16[192,768]{1,0:T(8,128)(2,1)}, bf16[2,96,768]{2,1,0:T(8,128)(2,1)}, bf16[2,96,768]{2,1,0:T(8,128)(2,1)}, bf16[2,96,768]{2,1,0:T(8,128)(2,1)}, b...) custom-call(s32[2]{0:T(128)} %pad_add_fusion.refs_0_.ids, bf16[192,768]{1,0:T(8,128)(2,1)} %bitcast.98, ...), custom_call_target="tpu_custom_call" | custom-call | flops 5000000000 | bytes 5000000 | tf_op jit(solution)/shard_map/experts/pallas_call | solution.py:698
  133.6 5.8 %experts.5 = (bf16[192,768]{1,0:T(8,128)(2,1)}, bf16[2,96,768]{2,1,0:T(8,128)(2,1)}, bf16[2,96,768]{2,1,0:T(8,128)(2,1)}, bf16[2,96,768]{2,1,0:T(8,128)(2,1)}, b...) custom-call(s32[2]{0:T(128)} %pad_add_fusion.refs_0_.ids, bf16[192,768]{1,0:T(8,128)(2,1)} %copy-done.22, ...), custom_call_target="tpu_custom_call" | custom-call | flops 5000000000 | bytes 5000000 | tf_op jit(solution)/shard_map/experts/pallas_call | solution.py:698
  139.5 5.9 %collective-permute-done.35.rows_in = bf16[192,768]{1,0:T(8,128)(2,1)S(1)} collective-permute-done((bf16[192,768]{1,0:T(8,128)(2,1)S(1)}, bf16[192,768]{1,0:T(8,128)(2,1)S(1)}, u32[]{:S(2)}, u32[]{:S(2)}) %collective-permute-start.35) | collective-permute-done | bytes 294944 | tf_op jit(solution)/shard_map/ppermute | solution.py:32
  146.1 5.8 %experts.6 = (bf16[192,768]{1,0:T(8,128)(2,1)}, bf16[2,96,768]{2,1,0:T(8,128)(2,1)}, bf16[2,96,768]{2,1,0:T(8,128)(2,1)}, bf16[2,96,768]{2,1,0:T(8,128)(2,1)}, b...) custom-call(s32[2]{0:T(128)} %pad_add_fusion.refs_0_.ids, bf16[192,768]{1,0:T(8,128)(2,1)} %copy-done.21, ...), custom_call_target="tpu_custom_call" | custom-call | flops 5000000000 | bytes 5000000 | tf_op jit(solution)/shard_map/experts/pallas_call | solution.py:698
  152.6 5.8 %experts.7 = (bf16[192,768]{1,0:T(8,128)(2,1)}, bf16[2,96,768]{2,1,0:T(8,128)(2,1)}, bf16[2,96,768]{2,1,0:T(8,128)(2,1)}, bf16[2,96,768]{2,1,0:T(8,128)(2,1)}, b...) custom-call(s32[2]{0:T(128)} %pad_add_fusion.refs_0_.ids, bf16[192,768]{1,0:T(8,128)(2,1)} %copy-done.18, ...), custom_call_target="tpu_custom_call" | custom-call | flops 5000000000 | bytes 5000000 | tf_op jit(solution)/shard_map/experts/pallas_call | solution.py:698
  160.0 10.6 %expert_weights.1 = (bf16[192,768]{1,0:T(8,128)(2,1)}, bf16[192,768]{1,0:T(8,128)(2,1)}, bf16[192,768]{1,0:T(8,128)(2,1)}, bf16[192,768]{1,0:T(8,128)(2,1)}, f32...) custom-call(bf16[2,96,768]{2,1,0:T(8,128)(2,1)} %get-tuple-element.154.refs_0_, ...), custom_call_target="tpu_custom_call" | custom-call | flops 8000000000 | bytes 8000000 | tf_op jit(solution)/shard_map/expert_weights/pallas_call | solution.py:726
  180.7 3.6 %all-to-all-start.2 = ((bf16[8,24,768]{2,1,0:T(8,128)(2,1)}), bf16[8,24,768]{2,1,0:T(8,128)(2,1)S(1)}, u32[]{:S(2)}, u32[]{:S(2)}) async-start(bf16[8,24,768]{2,1,0:T(8,128)(2,1)} %bitcast.21), calls=%async_computation.2 | async-start | bytes 589824 | tf_op jit(solution)/shard_map/all_to_all | solution.py:617
  184.3 12.1 %collective-permute-done.43 = bf16[192,768]{1,0:T(8,128)(2,1)S(1)} collective-permute-done((bf16[192,768]{1,0:T(8,128)(2,1)}, bf16[192,768]{1,0:T(8,128)(2,1)S(1)}, u32[]{:S(2)}, u32[]{:S(2)}) %collective-permute-start.43) | collective-permute-done | bytes 294944 | tf_op jit(solution)/shard_map/ppermute | solution.py:32
  203.9 11.4 %query_grad.1 = (bf16[6,128,128]{2,1,0:T(8,128)(2,1)}, f32[16,32]{1,0:T(8,128)}) custom-call(s32[2]{0:T(128)} %pad_add_fusion.refs_0_.ids, bf16[128,768]{1,0:T(8,128)(2,1)} %get-tuple-element.178.resid_low.refs_1_, bf16[128,896]{1,0:T(8,128)(2,1)} %get-tuple-element.182.refs_10_.ext.refs_9_, bf16[128,2304]{1,0:T(8,128)(2,1)} %get-tuple-element.148.joined_own.refs_17_, ...), custom_call_target="tpu_custom_call" | custom-call | flops 10000000000 | bytes 10000000 | tf_op jit(solution)/shard_map/query_grad/pallas_call | solution.py:758
  216.5 6.6 %collective-permute-start.56 = (f32[18,192]{1,0:T(8,128)S(1)}, f32[18,192]{1,0:T(8,128)S(1)}, u32[]{:S(2)}, u32[]{:S(2)}) collective-permute-start(f32[18,192]{1,0:T(8,128)S(1)} %bitcast.110), channel_id=1, source_target_pairs={{0,1},{1,0},{2,3},{3,2},{4,5},{5,4},{6,7},{7,6},{8,9},{9,8},{10,11... | collective-permute-start | bytes 41480 | tf_op jit(solution)/shard_map/ppermute | solution.py:32
  244.6 12.7 %key_grad.1 = (bf16[24,128,128]{2,1,0:T(8,128)(2,1)}, bf16[1024,768]{1,0:T(8,128)(2,1)}) custom-call(s32[2]{0:T(128)} %pad_add_fusion.refs_0_.ids, bf16[128,768]{1,0:T(8,128)(2,1)} %get-tuple-element.178.resid_low.refs_1_, bf16[128,768]{1,0:T(8,128)(2,1)} %copy-done.40, bf16[128,768]{1,0:T(8,128)(2,1)} %copy-done.36, bf16[128,768]{1,0:T(8,128)(2,1)} %copy-done.41, ...), custom_call_target="tpu_custom_call" | custom-call | flops 12000000000 | bytes 12000000 | tf_op jit(solution)/shard_map/key_grad/pallas_call | solution.py:794
  257.3 4.1 %all-to-all-start.4 = ((bf16[8,3,128,128]{3,2,1,0:T(8,128)(2,1)}), bf16[8,3,128,128]{3,2,1,0:T(8,128)(2,1)S(1)}, u32[]{:S(2)}, u32[]{:S(2)}) async-start(bf16[8,3,128,128]{3,2,1,0:T(8,128)(2,1)} %bitcast.86), calls=%async_computation.4 | async-start | bytes 1572864 | tf_op jit(solution)/shard_map/all_to_all | solution.py:823
  261.5 4.5 %source_grad.1 = (bf16[128,768]{1,0:T(8,128)(2,1)}, f32[1,768]{1,0:T(1,128)}) custom-call(s32[2]{0:T(128)} %pad_add_fusion.refs_0_.ids, bf16[24,128,128]{2,1,0:T(8,128)(2,1)} %get-tuple-element.192.blocks, bf16[768,2304]{1,0:T(8,128)(2,1)} %get-tuple-element.193.w_in, bf16[128,768]{1,0:T(8,128)(2,1)} %bitcast.123, ...), custom_call_target="tpu_custom_call" | custom-call | flops 4000000000 | bytes 4000000 | tf_op jit(solution)/shard_map/source_grad/pallas_call | solution.py:125
  274.9 5.2 %weight_grads.1 = bf16[768,384]{1,0:T(8,128)(2,1)} custom-call(s32[2]{0:T(128)} %pad_add_fusion.refs_0_.ids, bf16[1024,768]{1,0:T(8,128)(2,1)} %get-tuple-element.198.xn_all, bf16[1024,768]{1,0:T(8,128)(2,1)} %get-tuple-element.199.mixed_all, bf16[8,3,128,128]{3,2,1,0:T(8,128)(2,1)} %copy-done), custom_call_target="tpu_custom_call" | custom-call | flops 4000000000 | bytes 4000000 | tf_op jit(solution)/shard_map/weight_grads/pallas_call | solution.py:125
  289.1 4.5 %collective-permute-done.69 = bf16[192,384]{1,0:T(8,128)(2,1)S(1)} collective-permute-done((bf16[192,384]{1,0:T(8,128)(2,1)S(1)}, bf16[192,384]{1,0:T(8,128)(2,1)S(1)}, u32[]{:S(2)}, u32[]{:S(2)}) %collective-permute-start.69) | collective-permute-done | bytes 147488 | tf_op jit(solution)/shard_map/ppermute | solution.py:32
  (342 shorter events, 148.0 us)
Async XLA Ops:
  7.3 17.7 %collective-permute-start = (bf16[128,768]{1,0:T(8,128)(2,1)}, bf16[128,768]{1,0:T(8,128)(2,1)S(1)}, u32[]{:S(2)}, u32[]{:S(2)}) collective-permute-start(bf16[128,768]{1,0:T(8,128)(2,1)} %bitcast.117), channel_id=1, source_target_pairs={{0,8},{4,12},{8,0},{12,4},{16,24},{20,28},{24,16},{28,20},{1,9},{5... | collective-permute-start | bytes 589832 | tf_op jit(solution)/shard_map/ppermute | solution.py:32
  25.8 18.5 %collective-permute-start.9 = (bf16[192,1152]{1,0:T(8,128)(2,1)S(1)}, bf16[192,1152]{1,0:T(8,128)(2,1)S(1)}, u32[]{:S(2)}, u32[]{:S(2)}) collective-permute-start(bf16[192,1152]{1,0:T(8,128)(2,1)S(1)} %constant_dynamic-update-slice_fusion.refs_9_), channel_id=1, source_target_pairs={{0,16},{4,20},{8,24},{12,28},{16,0},{20,4},{24,8},{28,12},{1,17},{... | collective-permute-start | bytes 1327112 | tf_op jit(solution)/shard_map/ppermute | solution.py:32
  34.5 28.1 %collective-permute-start.6 = (bf16[192,1152]{1,0:T(8,128)(2,1)S(1)}, bf16[192,1152]{1,0:T(8,128)(2,1)S(1)}, u32[]{:S(2)}, u32[]{:S(2)}) collective-permute-start(bf16[192,1152]{1,0:T(8,128)(2,1)S(1)} %constant_dynamic-update-slice_fusion.refs_9_), channel_id=1, source_target_pairs={{0,4},{4,0},{8,12},{12,8},{16,20},{20,16},{24,28},{28,24},{1,5},{5... | collective-permute-start | bytes 1327112 | tf_op jit(solution)/shard_map/ppermute | solution.py:32
  44.3 18.8 %collective-permute-start.10 = (bf16[192,1152]{1,0:T(8,128)(2,1)S(1)}, bf16[192,1152]{1,0:T(8,128)(2,1)S(1)}, u32[]{:S(2)}, u32[]{:S(2)}) collective-permute-start(bf16[192,1152]{1,0:T(8,128)(2,1)S(1)} %collective-permute-done.9.refs_13_), channel_id=1, source_target_pairs={{0,4},{4,0},{8,12},{12,8},{16,20},{20,16},{24,28},{28,24},{1,5},{5... | collective-permute-start | bytes 1327112 | tf_op jit(solution)/shard_map/ppermute | solution.py:32
  44.3 18.8 %collective-permute-start.12 = (bf16[192,1152]{1,0:T(8,128)(2,1)S(1)}, bf16[192,1152]{1,0:T(8,128)(2,1)}, u32[]{:S(2)}, u32[]{:S(2)}) collective-permute-start(bf16[192,1152]{1,0:T(8,128)(2,1)S(1)} %collective-permute-done.11.refs_15_), channel_id=1, source_target_pairs={{0,4},{4,0},{8,12},{12,8},{16,20},{20,16},{24,28},{28,24},{1,5},{5... | collective-permute-start | bytes 1327112 | tf_op jit(solution)/shard_map/ppermute | solution.py:32
  45.5 18.1 %collective-permute-start.8 = (bf16[192,1152]{1,0:T(8,128)(2,1)S(1)}, bf16[192,1152]{1,0:T(8,128)(2,1)}, u32[]{:S(2)}, u32[]{:S(2)}) collective-permute-start(bf16[192,1152]{1,0:T(8,128)(2,1)S(1)} %collective-permute-done.7.refs_11_), channel_id=1, source_target_pairs={{0,4},{4,0},{8,12},{12,8},{16,20},{20,16},{24,28},{28,24},{1,5},{5... | collective-permute-start | bytes 1327112 | tf_op jit(solution)/shard_map/ppermute | solution.py:32
  63.7 21.7 %collective-permute-start.16 = (bf16[192,384]{1,0:T(8,128)(2,1)S(1)}, bf16[192,384]{1,0:T(8,128)(2,1)S(1)}, u32[]{:S(2)}, u32[]{:S(2)}) collective-permute-start(bf16[192,384]{1,0:T(8,128)(2,1)S(1)} %constant_dynamic-update-slice_fusion.4.refs_1_), channel_id=1, source_target_pairs={{0,8},{4,12},{8,0},{12,4},{16,24},{20,28},{24,16},{28,20},{1,9},{5... | collective-permute-start | bytes 442376 | tf_op jit(solution)/shard_map/ppermute | solution.py:32
  65.5 20.0 %collective-permute-start.17 = (bf16[192,384]{1,0:T(8,128)(2,1)S(1)}, bf16[192,384]{1,0:T(8,128)(2,1)S(1)}, u32[]{:S(2)}, u32[]{:S(2)}) collective-permute-start(bf16[192,384]{1,0:T(8,128)(2,1)S(1)} %constant_dynamic-update-slice_fusion.4.refs_1_), channel_id=1, source_target_pairs={{0,16},{4,20},{8,24},{12,28},{16,0},{20,4},{24,8},{28,12},{1,17},{... | collective-permute-start | bytes 442376 | tf_op jit(solution)/shard_map/ppermute | solution.py:32
  66.9 18.5 %collective-permute-start.18 = (bf16[192,384]{1,0:T(8,128)(2,1)S(1)}, bf16[192,384]{1,0:T(8,128)(2,1)}, u32[]{:S(2)}, u32[]{:S(2)}) collective-permute-start(bf16[192,384]{1,0:T(8,128)(2,1)S(1)} %constant_dynamic-update-slice_fusion.4.refs_1_), channel_id=1, source_target_pairs={{0,24},{4,28},{8,16},{12,20},{16,8},{20,12},{24,0},{28,4},{1,25},{... | collective-permute-start | bytes 442376 | tf_op jit(solution)/shard_map/ppermute | solution.py:32
  87.3 23.5 %collective-permute-start.31 = (bf16[192,768]{1,0:T(8,128)(2,1)S(1)}, bf16[192,768]{1,0:T(8,128)(2,1)S(1)}, u32[]{:S(2)}, u32[]{:S(2)}) collective-permute-start(bf16[192,768]{1,0:T(8,128)(2,1)S(1)} %bitcast.91), channel_id=1, source_target_pairs={{0,2},{1,3},{2,0},{3,1},{4,6},{5,7},{6,4},{7,5},{8,10},{9,11},{10,... | collective-permute-start | bytes 884744 | tf_op jit(solution)/shard_map/ppermute | solution.py:32
  88.1 22.7 %collective-permute-start.32 = (bf16[192,768]{1,0:T(8,128)(2,1)S(1)}, bf16[192,768]{1,0:T(8,128)(2,1)S(1)}, u32[]{:S(2)}, u32[]{:S(2)}) collective-permute-start(bf16[192,768]{1,0:T(8,128)(2,1)S(1)} %bitcast.92), channel_id=1, source_target_pairs={{0,3},{1,2},{2,1},{3,0},{4,7},{5,6},{6,5},{7,4},{8,11},{9,10},{10,... | collective-permute-start | bytes 884744 | tf_op jit(solution)/shard_map/ppermute | solution.py:32
  96.4 20.1 %all-to-all-start.1 = ((bf16[8,24,768]{2,1,0:T(8,128)(2,1)}), bf16[8,24,768]{2,1,0:T(8,128)(2,1)S(1)}, u32[]{:S(2)}, u32[]{:S(2)}) async-start(bf16[8,24,768]{2,1,0:T(8,128)(2,1)} %bitcast.99), calls=%async_computation.1 | async-start | bytes 589824 | tf_op jit(solution)/shard_map/all_to_all | solution.py:617
  121.9 23.5 %collective-permute-start.35 = (bf16[192,768]{1,0:T(8,128)(2,1)S(1)}, bf16[192,768]{1,0:T(8,128)(2,1)S(1)}, u32[]{:S(2)}, u32[]{:S(2)}) collective-permute-start(bf16[192,768]{1,0:T(8,128)(2,1)S(1)} %bitcast.96), channel_id=1, source_target_pairs={{0,2},{1,3},{2,0},{3,1},{4,6},{5,7},{6,4},{7,5},{8,10},{9,11},{10,... | collective-permute-start | bytes 884744 | tf_op jit(solution)/shard_map/ppermute | solution.py:32
  122.0 29.9 %collective-permute-start.37 = (bf16[192,768]{1,0:T(8,128)(2,1)S(1)}, bf16[192,768]{1,0:T(8,128)(2,1)S(1)}, u32[]{:S(2)}, u32[]{:S(2)}) collective-permute-start(bf16[192,768]{1,0:T(8,128)(2,1)S(1)} %bitcast.97), channel_id=1, source_target_pairs={{0,3},{1,2},{2,1},{3,0},{4,7},{5,6},{6,5},{7,4},{8,11},{9,10},{10,... | collective-permute-start | bytes 884744 | tf_op jit(solution)/shard_map/ppermute | solution.py:32
  139.4 34.1 %collective-permute-start.34 = (bf16[192,768]{1,0:T(8,128)(2,1)}, bf16[192,768]{1,0:T(8,128)(2,1)S(1)}, u32[]{:S(2)}, u32[]{:S(2)}) collective-permute-start(bf16[192,768]{1,0:T(8,128)(2,1)} %get-tuple-element.143), channel_id=1, source_target_pairs={{0,1},{1,0},{2,3},{3,2},{4,5},{5,4},{6,7},{7,6},{8,9},{9,8},{10,11... | collective-permute-start | bytes 884744 | tf_op jit(solution)/shard_map/ppermute | solution.py:32
  151.8 24.8 %collective-permute-start.36 = (bf16[192,768]{1,0:T(8,128)(2,1)}, bf16[192,768]{1,0:T(8,128)(2,1)S(1)}, u32[]{:S(2)}, u32[]{:S(2)}) collective-permute-start(bf16[192,768]{1,0:T(8,128)(2,1)} %get-tuple-element.144), channel_id=1, source_target_pairs={{0,2},{1,3},{2,0},{3,1},{4,6},{5,7},{6,4},{7,5},{8,10},{9,11},{10,... | collective-permute-start | bytes 884744 | tf_op jit(solution)/shard_map/ppermute | solution.py:32
  158.4 19.9 %collective-permute-start.38 = (bf16[192,768]{1,0:T(8,128)(2,1)}, bf16[192,768]{1,0:T(8,128)(2,1)S(1)}, u32[]{:S(2)}, u32[]{:S(2)}) collective-permute-start(bf16[192,768]{1,0:T(8,128)(2,1)} %get-tuple-element.145), channel_id=1, source_target_pairs={{0,3},{1,2},{2,1},{3,0},{4,7},{5,6},{6,5},{7,4},{8,11},{9,10},{10,... | collective-permute-start | bytes 884744 | tf_op jit(solution)/shard_map/ppermute | solution.py:32
  172.6 23.9 %collective-permute-start.43 = (bf16[192,768]{1,0:T(8,128)(2,1)}, bf16[192,768]{1,0:T(8,128)(2,1)S(1)}, u32[]{:S(2)}, u32[]{:S(2)}) collective-permute-start(bf16[192,768]{1,0:T(8,128)(2,1)} %get-tuple-element.176), channel_id=1, source_target_pairs={{0,2},{1,3},{2,0},{3,1},{4,6},{5,7},{6,4},{7,5},{8,10},{9,11},{10,... | collective-permute-start | bytes 884744 | tf_op jit(solution)/shard_map/ppermute | solution.py:32
  173.5 22.9 %collective-permute-start.44 = (bf16[192,768]{1,0:T(8,128)(2,1)}, bf16[192,768]{1,0:T(8,128)(2,1)S(1)}, u32[]{:S(2)}, u32[]{:S(2)}) collective-permute-start(bf16[192,768]{1,0:T(8,128)(2,1)} %get-tuple-element.177), channel_id=1, source_target_pairs={{0,3},{1,2},{2,1},{3,0},{4,7},{5,6},{6,5},{7,4},{8,11},{9,10},{10,... | collective-permute-start | bytes 884744 | tf_op jit(solution)/shard_map/ppermute | solution.py:32
  176.7 48.8 %collective-permute-start.50 = (bf16[128,896]{1,0:T(8,128)(2,1)S(1)}, bf16[128,896]{1,0:T(8,128)(2,1)S(1)}, u32[]{:S(2)}, u32[]{:S(2)}) collective-permute-start(bf16[128,896]{1,0:T(8,128)(2,1)S(1)} %copy-done.23), channel_id=1, source_target_pairs={{0,8},{4,12},{8,0},{12,4},{16,24},{20,28},{24,16},{28,20},{1,9},{5... | collective-permute-start | bytes 688136 | tf_op jit(solution)/shard_map/ppermute | solution.py:32
  178.3 47.8 %collective-permute-start.52 = (bf16[128,896]{1,0:T(8,128)(2,1)S(1)}, bf16[128,896]{1,0:T(8,128)(2,1)S(1)}, u32[]{:S(2)}, u32[]{:S(2)}) collective-permute-start(bf16[128,896]{1,0:T(8,128)(2,1)S(1)} %copy-done.23), channel_id=1, source_target_pairs={{0,16},{4,20},{8,24},{12,28},{16,0},{20,4},{24,8},{28,12},{1,17},{... | collective-permute-start | bytes 688136 | tf_op jit(solution)/shard_map/ppermute | solution.py:32
  240.2 17.1 %all-to-all-start.3 = ((bf16[8,24,768]{2,1,0:T(8,128)(2,1)}), bf16[8,24,768]{2,1,0:T(8,128)(2,1)S(1)}, u32[]{:S(2)}, u32[]{:S(2)}) async-start(bf16[8,24,768]{2,1,0:T(8,128)(2,1)} %bitcast.25), calls=%async_computation.3 | async-start | bytes 589824 | tf_op jit(solution)/shard_map/all_to_all | solution.py:617
  266.7 17.2 %collective-permute-start.62 = (f32[1,192]{1,0:T(1,128)S(1)}, f32[1,192]{1,0:T(1,128)S(1)}, u32[]{:S(2)}, u32[]{:S(2)}) collective-permute-start(f32[1,192]{1,0:T(1,128)S(1)} %get-tuple-element.211), channel_id=1, source_target_pairs={{0,1},{1,0},{2,3},{3,2},{4,5},{5,4},{6,7},{7,6},{8,9},{9,8},{10,11... | collective-permute-start | bytes 2312 | tf_op jit(solution)/shard_map/ppermute | solution.py:32
  267.9 17.8 %collective-permute-start.63 = (f32[1,192]{1,0:T(1,128)S(1)}, f32[1,192]{1,0:T(1,128)S(1)}, u32[]{:S(2)}, u32[]{:S(2)}) collective-permute-start(f32[1,192]{1,0:T(1,128)S(1)} %get-tuple-element.213), channel_id=1, source_target_pairs={{0,2},{1,3},{2,0},{3,1},{4,6},{5,7},{6,4},{7,5},{8,10},{9,11},{10,... | collective-permute-start | bytes 2312 | tf_op jit(solution)/shard_map/ppermute | solution.py:32
  (115 other events, 1116.8 us)

commit v2 on v1

--- a/solution.py
+++ b/solution.py
@@ -44,32 +44,25 @@
     return [block for piece in pieces for block in (piece, swap(piece, "expert", 1))]
 
 
-def gather_rows(x):
-    count = lax.axis_size("wshard")
-    mine = lax.axis_index("wshard")
-    blocks = jnp.stack([x] + [swap(x, "wshard", mask) for mask in range(1, count)])
-    return jnp.take(blocks, mine ^ jnp.arange(count), axis=0, mode="clip")
-
-
-def weight_chunks(shard):
+def weight_chunks(shard, small):
     rows, columns = shard.shape
     chips = lax.axis_size("expert") // 2
     if rows % (16 * chips) or columns % (2 * LANES):
-        return [lax.all_gather(shard, "wshard", axis=0, tiled=True)]
+        return [lax.all_gather(jnp.concatenate([shard, small], axis=1), "wshard", axis=0, tiled=True)]
     mine = lax.axis_index("expert")
-    chunk = lax.dynamic_slice(
-        shard,
-        (mine // 2 * (rows // chips), mine % 2 * (columns // 2)),
-        (rows // chips, columns // 2),
-    )
+    first = mine // 2 * (rows // chips)
+    chunk = lax.dynamic_slice(shard, (first, mine % 2 * (columns // 2)), (rows // chips, columns // 2))
+    beside = lax.dynamic_slice(small, (first, 0), (rows // chips, small.shape[1]))
+    chunk = jnp.concatenate([chunk, beside], axis=1)
     return [chunk] + [swap(chunk, "wshard", mask) for mask in range(1, lax.axis_size("wshard"))]
 
 
-def place_weight(pieces, target, expert_id, shard_id, shards):
+def place_weight(pieces, target, small, expert_id, shard_id, shards):
+    rows, columns = target.shape
     if len(pieces) == 1:
-        target[...] = pieces[0][...]
+        target[...] = pieces[0][:, :columns]
+        small[...] = pieces[0][:, columns:]
         return
-    rows, columns = target.shape
     chips = len(pieces) // 2
     chunk = rows // shards // chips
     for mask, piece in enumerate(pieces):
@@ -77,9 +70,11 @@
         column = pl.multiple_of(source % 2 * (columns // 2), LANES)
         for step in range(shards):
             row = (shard_id ^ step) * (rows // shards) + source // 2 * chunk
-            target[pl.ds(pl.multiple_of(row, 16), chunk), pl.ds(column, columns // 2)] = piece[
-                step * chunk : (step + 1) * chunk, :
-            ]
+            row = pl.multiple_of(row, 16)
+            lines = slice(step * chunk, (step + 1) * chunk)
+            target[pl.ds(row, chunk), pl.ds(column, columns // 2)] = piece[lines, : columns // 2]
+            if mask % 2 == 0:
+                small[pl.ds(row, chunk), :] = piece[lines, columns // 2 :]
 
 
 def place_blocks(pieces, target, expert_id, change=None):
@@ -145,20 +140,28 @@
 
 
 def forward_body(sizes, *refs):
-    devices, shards, heads, head_dim, buckets, in_count = sizes
+    devices, shards, heads, head_dim, buckets, experts, in_count = sizes
     refs = list(refs)
     ids = refs.pop(0)
     tokens = [refs.pop(0) for _ in range(devices)]
     in_pieces = [refs.pop(0) for _ in range(in_count)]
-    gains, table, window_ref, mirror_ref = [refs.pop(0) for _ in range(4)]
-    xn_all, joined, joined_own, ext, w_in, window, mirror = refs
+    window_ref, mirror_ref = [refs.pop(0) for _ in range(2)]
+    xn_all, joined, joined_own, ext, w_in, window, mirror, gains, small = refs
     expert_id = ids[0]
     shard_id = ids[1]
     rows, width = tokens[0].shape
     keys = rows * devices
-    gain_one = gains[0:1, :].astype(F32)
+    place_weight(in_pieces, w_in, small, expert_id, shard_id, shards)
+    turned = small[...].astype(F32).T
+    gains[...] = turned[experts : experts + 8, :]
+    gain_one = gains[0:1, :]
     place_blocks(tokens, xn_all, expert_id, lambda block: normalize(block, gain_one))
-    place_weight(in_pieces, w_in, expert_id, shard_id, shards)
+    head_rows = window.shape[0]
+    per_shard = buckets // shards
+    spot = lax.broadcasted_iota(jnp.int32, (buckets, width), 1)
+    bucket = lax.broadcasted_iota(jnp.int32, (buckets, width), 0)
+    spot_hot = (spot == bucket // per_shard * (width // shards) + bucket % per_shard).astype(BF)
+    table = dot(turned[experts + 2 : experts + 2 + head_rows, :].astype(BF), spot_hot, NT).astype(BF)
     column_block = 2 * LANES
     row_block = min(1024, keys)
 
@@ -171,8 +174,8 @@
         return carry
 
     lax.fori_loop(0, (3 * width // column_block) * (keys // row_block), project, 0)
-    window[...] = dot(table[...], bucket_hot(window_ref, buckets))
-    mirror[...] = dot(table[...], bucket_hot(mirror_ref, buckets))
+    window[...] = dot(table, bucket_hot(window_ref, buckets))
+    mirror[...] = dot(table, bucket_hot(mirror_ref, buckets))
     own = pl.multiple_of(expert_id * rows, rows)
     joined_own[...] = joined[pl.ds(own, rows), :]
     lane = lax.broadcasted_iota(jnp.int32, (rows, LANES), 1)
@@ -200,19 +203,12 @@
     ext[:, width:] = (high + pltpu.roll(middle, 32, 1) + pltpu.roll(low, 64, 1)).astype(BF)
 
 
-def route_body(sizes, *refs):
-    shards, experts, out_count = sizes
-    refs = list(refs)
-    ids = refs.pop(0)
-    out_pieces = [refs.pop(0) for _ in range(out_count)]
-    tokens, ext, gains, router, chosen, slots = [refs.pop(0) for _ in range(6)]
-    after, gate, send, w_out = refs
+def route_body(experts, ids, w_out, tokens, ext, gains, router, chosen, slots, after, gate, send):
     rows, width = tokens.shape
-    place_weight(out_pieces, w_out, ids[0], ids[1], shards)
     lane = lax.broadcasted_iota(jnp.int32, (rows, LANES), 1)
     post = tokens[...].astype(F32) + dot(ext[:, :width], w_out[...])
     after[...] = post
-    xn_two = normalize(post, gains[1:2, :].astype(F32))
+    xn_two = normalize(post, gains[1:2, :])
     logits = jnp.where(lane < experts, dot(xn_two, router[...]), -1e30)
     weights = jnp.exp(logits - jnp.max(logits, axis=1, keepdims=True))
     weights = weights / jnp.sum(weights, axis=1, keepdims=True)
@@ -229,16 +225,14 @@
     return (column == row // capacity * block + which * capacity + row % capacity).astype(BF)
 
 
-def upstream_body(sizes, *refs):
+def upstream_body(sizes, ids, chunks, w_down, up_ref, spread_ref):
     shards, per_device, capacity = sizes
-    refs = list(refs)
-    chunks = [refs.pop(0) for _ in range(shards)]
-    w_down, up_ref, spread_ref = refs
-    total = chunks[0].shape[0]
+    total = chunks.shape[0] // shards
     count = total // per_device
     pick = slot_pick(count, total, capacity, pl.program_id(0))
-    for step, chunk in enumerate(chunks):
-        up_ref[0, step * count : (step + 1) * count, :] = dot(pick, chunk[...]).astype(BF)
+    for step in range(shards):
+        start = pl.multiple_of((ids[1] ^ step) * total, total)
+        up_ref[0, step * count : (step + 1) * count, :] = dot(pick, chunks[pl.ds(start, total), :]).astype(BF)
     spread_ref[0] = dot(up_ref[0], w_down[0])
 
 
@@ -285,15 +279,13 @@
         back_ref[...] = (back_ref[...].astype(F32) + back.astype(F32)).astype(BF)
 
 
-def expert_weights_body(sizes, *refs):
+def expert_weights_body(sizes, ids, *refs):
     shards, per_device, capacity = sizes
     refs = list(refs)
     x, up, hidden, pre, logit = [
         jnp.concatenate([refs.pop(0)[0] for _ in range(shards)], axis=0) for _ in range(5)
     ]
-    w_down = refs.pop(0)
-    out_refs = [refs.pop(0) for _ in range(shards)]
-    up_grad, down_grad, router_part = refs
+    w_down, out_ref, up_grad, down_grad, router_part = refs
     which = pl.program_id(0)
     down_grad[0] = dot(up, hidden, TN)
     up_grad[0] = dot(x, pre, TN)
@@ -303,18 +295,19 @@
     total = count * per_device
     pick = slot_pick(count, total, capacity, which)
     parts = [dot(pick, out[m * count : (m + 1) * count], TN).astype(BF) for m in range(shards)]
+    places = [pl.ds(pl.multiple_of((ids[1] ^ m) * total, total), total) for m in range(shards)]
 
     @pl.when(which == 0)
     def _():
         router_part[...] = router_add
-        for ref, part in zip(out_refs, parts):
-            ref[...] = part
+        for place, part in zip(places, parts):
+            out_ref[place, :] = part
 
     @pl.when(which > 0)
     def _():
         router_part[...] = router_part[...] + router_add
-        for ref, part in zip(out_refs, parts):
-            ref[...] = (ref[...].astype(F32) + part.astype(F32)).astype(BF)
+        for place, part in zip(places, parts):
+            out_ref[place, :] = (out_ref[place, :].astype(F32) + part.astype(F32)).astype(BF)
 
 
 def norm_back(values, gain, grad):
@@ -327,7 +320,7 @@
 
 def residual_body(ids, returned, back_slots, after, upstream, gains, resid, resid_low, gain_part):
     grad = dot(back_slots[...], returned[...])
-    value, part = norm_back(after[...], gains[1:2, :].astype(F32), grad)
+    value, part = norm_back(after[...], gains[1:2, :], grad)
     value = value + upstream[...].astype(F32)
     resid[...] = value
     resid_low[...] = value.astype(BF)
@@ -422,9 +415,8 @@
     refs = list(refs)
     ids = refs.pop(0)
     resid_pieces = [refs.pop(0) for _ in range(devices)]
-    ext_pieces = [refs.pop(0) for _ in range(devices)]
-    joined_own, w_out, mirror, query_grad, queries_in = [refs.pop(0) for _ in range(5)]
-    blocks, mixed_all, grads, delta_rows, mass_rows, mass_all = refs
+    ext_all, joined_own, w_out, mirror, query_grad, queries_in = [refs.pop(0) for _ in range(6)]
+    blocks, grads, delta_rows, mass_rows = refs
     expert_id = ids[0]
     pair = pl.program_id(0)
     rows, width = resid_pieces[0].shape
@@ -435,17 +427,13 @@
     @pl.when(pair == 0)
     def _():
         place_blocks(resid_pieces, grads, expert_id)
-        for mask, piece in enumerate(ext_pieces):
-            start = pl.multiple_of((expert_id ^ mask) * rows, rows)
-            mixed_all[pl.ds(start, rows), :] = piece[:, :width]
-            mass_all[pl.ds(start, rows), :] = piece[:, width:]
-        mass_rows[...] = dot(part_rows(head_rows), mass_all[...], NT)
+        mass_rows[...] = dot(part_rows(head_rows), ext_all[:, width:], NT)
         member = member_rows(head_rows, width, head_dim)
         step = min(1024, keys)
         for start in range(0, keys, step):
             low = dot(grads[start : start + step, :], w_out[...], NT).astype(BF)
             grads[start : start + step, :] = low
-            product = low.astype(F32) * mixed_all[start : start + step, :].astype(F32)
+            product = low.astype(F32) * ext_all[start : start + step, :width].astype(F32)
             high = product.astype(BF)
             rest = (product - high.astype(F32)).astype(BF)
             delta_rows[:, start : start + step] = dot(member, high, NT) + dot(member, rest, NT)
@@ -478,38 +466,54 @@
     for block in range(joined.shape[1] // LANES):
         joined[:, block * LANES : (block + 1) * LANES] = blocks[block]
     grad = dot(joined[...], w_in[...], NT)
-    value, part = norm_back(tokens[...].astype(F32), gains[0:1, :].astype(F32), grad)
+    value, part = norm_back(tokens[...].astype(F32), gains[0:1, :], grad)
     tokens_grad[...] = (value + resid[...]).astype(BF)
     gain_part[...] = part
 
 
-def weight_body(per, pairs, ids, xn_all, mixed_all, received, part, columns):
+def weight_body(sizes, ids, xn_all, ext_all, received, lines, part, columns):
+    per, pairs, shards = sizes
     devices, _, rows, _ = received.shape
+    width = xn_all.shape[1]
+    rows_each = width // shards
     for source in range(devices):
         for block in range(per):
             columns[source * rows : (source + 1) * rows, block * LANES : (block + 1) * LANES] = received[
                 source, block
             ]
-    for block in range(per):
+
+    def store(value, line):
+        for owner in range(shards):
+            part[owner, :rows_each, line] = value[owner * rows_each : (owner + 1) * rows_each].astype(BF)
+
+    step = per if 3 * pairs % per == 0 else 1
+    for block in range(0, per, step):
         inside = ids[0] * per + block < 3 * pairs
-        line = slice(block * LANES, (block + 1) * LANES)
+        line = slice(block * LANES, (block + step) * LANES)
 
         @pl.when(inside)
         def _():
-            part[:, line] = dot(xn_all[...], columns[:, line], TN).astype(BF)
+            store(dot(xn_all[...], columns[:, line], TN), line)
 
         @pl.when(jnp.logical_not(inside))
         def _():
-            part[:, line] = dot(mixed_all[...], columns[:, line], TN).astype(BF)
-
-
-def spread_body(per, pairs, ids, *refs):
-    pieces, (in_grad, out_grad) = refs[:-2], refs[-2:]
+            store(dot(ext_all[:, :width], columns[:, line], TN), line)
+
+    part[:, rows_each:, :] = lines[...]
+
+
+def spread_body(sizes, ids, *refs):
+    per, pairs = sizes
+    pieces, (in_grad, out_grad, lines) = refs[:-3], refs[-3:]
+    rows = in_grad.shape[0]
+    total = None
     for mask, piece in enumerate(pieces):
         source = ids[0] ^ mask
+        extra = piece[rows:, :].astype(F32)
+        total = extra if total is None else total + extra
         for block in range(per):
             index = source * per + block
-            values = piece[:, block * LANES : (block + 1) * LANES].astype(F32)
+            values = piece[:rows, block * LANES : (block + 1) * LANES].astype(F32)
 
             @pl.when(index < 3 * pairs)
             def _():
@@ -518,6 +522,8 @@
             @pl.when(jnp.logical_and(index >= 3 * pairs, index < 4 * pairs))
             def _():
                 out_grad[:, pl.ds(pl.multiple_of((index - 3 * pairs) * LANES, LANES), LANES)] = values
+
+    lines[...] = total
 
 
 def pad_to(x, shape):
@@ -544,39 +550,19 @@
     part = width // shards
     ids = jnp.stack([expert_id, shard_id]).astype(jnp.int32)
 
-    in_chunks = weight_chunks(attn_in)
-    token_pieces, in_chunks, attn_out, own_grad = tie(
-        chip_pieces(own_tokens), in_chunks, attn_out, own_grad
-    )
-    out_chunks = weight_chunks(attn_out)
-    chunked = len(in_chunks) > 1
-    if chunked:
-        in_pieces = chip_pieces(jnp.concatenate(in_chunks, axis=0))
-    token_pieces = core_pieces(token_pieces)
-    if chunked:
-        in_pieces = core_pieces(in_pieces)
-    else:
-        in_pieces = in_chunks
-    small_columns = -(-(experts + 2 + heads) // LANES) * LANES
     table_rows = bias_table.shape[0]
+    head_rows = 16
     small = jnp.concatenate(
         [
             router,
             gain_attn[:, None],
             gain_mix[:, None],
-            pad_to(bias_table, (part, heads)),
-            jnp.zeros((part, small_columns - experts - 2 - heads), BF),
+            pad_to(bias_table, (part, LANES - experts - 2)),
         ],
         axis=1,
     )
-    small = gather_rows(small)
-    router_all = small[:, :, :experts].reshape(width, experts)
-    router_pad = pad_to(router_all, (width, LANES))
-    gains = pad_to(small[:, :, experts : experts + 2].reshape(width, 2).T, (8, width))
-    table = small[:, :table_rows, experts + 2 : experts + 2 + heads].reshape(bucket_count, heads)
-    head_rows = 16
-    table_t = pad_to(table.T, (head_rows, bucket_count))
-
+    in_chunks = weight_chunks(attn_in, small)
+    chip_tokens = chip_pieces(own_tokens)
     window_width = keys + rows
     start = keys - 1 - expert_id * rows - (rows - 1)
     window_buckets = lax.dynamic_slice(jnp.pad(buckets, (0, rows)), (start,), (window_width,))
@@ -603,22 +589,10 @@
             mine = mine + swap(sent, "wshard", mask).astype(F32)
         return mine
 
-    def sum_lines(lines):
-        lines = lines.reshape(lines.shape[0], shards, part).transpose(1, 0, 2)
-        lines = scatter_rows(lines)
-        mask = 1
-        while mask < devices:
-            lines = lines + swap(lines, "expert", mask)
-            mask *= 2
-        return lines
-
     def exchange(slot_rows):
         blocks = slot_rows.reshape(devices, block, width)
         moved = lax.all_to_all(blocks, "expert", split_axis=0, concat_axis=0, tiled=True)
         return moved.reshape(devices * block, width)
-
-    def to_shards(x):
-        return [x] + [swap(x, "wshard", mask) for mask in range(1, shards)]
 
     def sum_back(parts):
         total = parts[0].astype(F32)
@@ -626,17 +600,23 @@
             total = total + swap(parts[mask], "wshard", mask).astype(F32)
         return total.astype(BF)
 
-    ups, in_pieces, out_chunks = tie(
-        exchange(dot(slots, own_grad).astype(BF)), in_pieces, out_chunks
-    )
-    ups_chunks = to_shards(ups)
-    if len(out_chunks) > 1:
-        out_chunks = chip_pieces(jnp.concatenate(out_chunks, axis=0))
-
-    sizes = (devices, shards, heads, head_dim, bucket_count, len(in_pieces))
-    xn_all, joined, joined_own, ext, w_in, window, mirror = call(
+    chip_tokens, in_chunks, attn_out, ups = tie(
+        chip_tokens, in_chunks, attn_out, dot(slots, own_grad).astype(BF)
+    )
+    in_pieces = in_chunks
+    if len(in_chunks) > 1:
+        in_pieces = chip_pieces(jnp.concatenate(in_chunks, axis=0))
+    token_pieces = core_pieces(chip_tokens)
+    w_out = lax.all_gather(attn_out, "wshard", axis=0, tiled=True)
+    in_pieces, token_pieces, ups = tie(in_pieces, token_pieces, exchange(ups))
+    if len(in_pieces) > 1:
+        in_pieces = core_pieces(in_pieces)
+    ups_all = lax.all_gather(ups, "wshard", axis=0, tiled=True)
+
+    sizes = (devices, shards, heads, head_dim, bucket_count, experts, len(in_pieces))
+    xn_all, joined, joined_own, ext, w_in, window, mirror, gains, router_pad = call(
         functools.partial(forward_body, sizes),
-        [ids, *token_pieces, *in_pieces, gains, table_t, window_buckets, mirror_buckets],
+        [ids, *token_pieces, *in_pieces, window_buckets, mirror_buckets],
         [
             ((keys, width), BF),
             ((keys, 3 * width), BF),
@@ -645,29 +625,20 @@
             ((width, 3 * width), BF),
             ((head_rows, window_width), F32),
             ((head_rows, window_width), F32),
+            ((8, width), F32),
+            ((width, LANES), BF),
         ],
         name="attention_forward",
-        us=18.0,
-    )
-    out_pieces, ext = tie(out_chunks, ext)
-    if len(out_pieces) > 1:
-        out_pieces = core_pieces(out_pieces)
-    after, gate, send, w_out = call(
-        functools.partial(route_body, (shards, experts, len(out_pieces))),
-        [ids, *out_pieces, own_tokens, ext, gains, router_pad, chosen, slots],
-        [
-            ((rows, width), F32),
-            ((rows, LANES), F32),
-            ((slot_count, width), BF),
-            ((width, width), BF),
-        ],
+        us=0.2,
+    )
+    after, gate, send = call(
+        functools.partial(route_body, experts),
+        [ids, w_out, own_tokens, ext, gains, router_pad, chosen, slots],
+        [((rows, width), F32), ((rows, LANES), F32), ((slot_count, width), BF)],
         name="route",
-        us=4.0,
+        us=0.2,
     )
     rows_own = exchange(send)
-    row_chunks = to_shards(rows_own)
-    ext_later, _ = tie(ext, rows_own)
-    ext_pieces = core_pieces(chip_pieces(ext_later))
     total = devices * block
     count = total // per_device
     ff = expert_in.shape[2]
@@ -680,7 +651,7 @@
     ups_all, spread_all = pl.pallas_call(
         functools.partial(upstream_body, (shards, per_device, capacity)),
         grid=(per_device,),
-        in_specs=[whole((total, width))] * shards + [by_expert],
+        in_specs=[pl.BlockSpec(memory_space=pltpu.SMEM), whole((shards * total, width)), by_expert],
         out_specs=[upstream_width, upstream_ff],
         out_shape=[
             jax.ShapeDtypeStruct((per_device, shards * count, width), BF),
@@ -689,12 +660,19 @@
         compiler_params=pltpu.CompilerParams(vmem_limit_bytes=VMEM_BYTES),
         cost_estimate=cost(5.0),
         name="upstream",
-    )(*ups_chunks, expert_down)
+    )(ids, ups_all, expert_down)
     rows_own, ups_all, spread_all = tie(rows_own, ups_all, spread_all)
-    row_chunks = [rows_own] + row_chunks[1:]
+    row_chunks = {0: rows_own}
+    steps = [1 << bit for bit in reversed(range((shards - 1).bit_length()))]
+    row_chunks.update({step: swap(rows_own, "wshard", step) for step in steps})
+    ext_later, _ = tie(ext, rows_own)
+    ext_all = lax.all_gather(ext_later, "expert", axis=0, tiled=True)
     kept = [[], [], [], [], []]
     back_parts = []
-    for step, row_chunk in enumerate(row_chunks):
+    for step in range(shards):
+        row_chunk = row_chunks[step]
+        if step:
+            row_chunk, _ = tie(row_chunk, back_parts[-1])
         back, *saved = pl.pallas_call(
             functools.partial(expert_body, (experts, per_device, capacity)),
             grid=(per_device,),
@@ -716,23 +694,31 @@
                 jax.ShapeDtypeStruct((per_device, count, LANES), F32),
             ],
             compiler_params=pltpu.CompilerParams(vmem_limit_bytes=VMEM_BYTES),
-            cost_estimate=cost(5.0),
+            cost_estimate=cost(0.5),
             name="experts",
         )(ids, row_chunk, ups_all, spread_all, expert_in, router_pad)
         back_parts.append(back)
         for group, value in zip(kept, saved):
             group.append(value)
-    returned_grad = exchange(sum_back(back_parts))
-    *out_parts, up_grad, down_grad, router_part = pl.pallas_call(
+        if step == 1:
+            for mask in range(1, shards):
+                nearer = mask & (-mask)
+                if mask != nearer:
+                    value, _ = tie(row_chunks[mask ^ nearer], back)
+                    row_chunks[mask] = swap(value, "wshard", nearer)
+    kept, back_sum = tie(kept, sum_back(back_parts))
+    returned_grad = exchange(back_sum)
+    out_parts, up_grad, down_grad, router_part = pl.pallas_call(
         functools.partial(expert_weights_body, (shards, per_device, capacity)),
         grid=(per_device,),
-        in_specs=[kept_width] * (2 * shards)
+        in_specs=[pl.BlockSpec(memory_space=pltpu.SMEM)]
+        + [kept_width] * (2 * shards)
         + [kept_ff] * (2 * shards)
         + [kept_lanes] * shards
         + [by_expert],
-        out_specs=[whole((total, width))] * shards + [by_expert, by_expert, whole((LANES, width))],
-        out_shape=[jax.ShapeDtypeStruct((total, width), BF)] * shards
-        + [
+        out_specs=[whole((shards * total, width)), by_expert, by_expert, whole((LANES, width))],
+        out_shape=[
+            jax.ShapeDtypeStruct((shards * total, width), BF),
             jax.ShapeDtypeStruct((per_device, width, ff), F32),
             jax.ShapeDtypeStruct((per_device, width, ff), F32),
             jax.ShapeDtypeStruct((LANES, width), F32),
@@ -740,7 +726,8 @@
         compiler_params=pltpu.CompilerParams(vmem_limit_bytes=VMEM_BYTES),
         cost_estimate=cost(8.0),
         name="expert_weights",
-    )(*[value for group in kept for value in group], expert_down)
+    )(ids, *[value for group in kept for value in group], expert_down)
+    out_parts, router_part, returned_grad = tie(out_parts, router_part, returned_grad)
     resid, resid_low, gain_two_part = call(
         residual_body,
         [ids, returned_grad, back_slots, after, own_grad, gains],
@@ -748,7 +735,8 @@
         name="residual",
         us=2.0,
     )
-    out_sum = sum_back(out_parts)
+    out_parts, _ = tie(out_parts, resid_low)
+    out_sum = lax.psum_scatter(out_parts, "wshard", scatter_dimension=0, tiled=True)
     resid_pieces = chip_pieces(resid_low)
     pairs = heads // 2
 
@@ -785,50 +773,37 @@
         name="query_grad",
     )(ids, resid_low, ext, joined_own, w_out, window, window_buckets, joined, joined)
     per = -(-4 * pairs // devices)
-    resid_pieces, query_grad, table_part, out_sum = tie(resid_pieces, query_grad, table_part, out_sum)
+    resid_pieces, query_grad = tie(resid_pieces, query_grad)
     resid_pieces = core_pieces(resid_pieces)
-    returned_rows = exchange(out_sum)
-    table_line = table_part[:heads].T.reshape(shards, table_rows * heads)
-    table_line = pad_to(table_line, (shards, part)).reshape(1, width)
-    lines = sum_lines(jnp.concatenate([router_part[:experts], gain_two_part, table_line], axis=0))
-    blocks, mixed_all = pl.pallas_call(
+    (blocks,) = pl.pallas_call(
         functools.partial(key_body, (devices, heads, head_dim)),
         grid=(pairs,),
         in_specs=[pl.BlockSpec(memory_space=pltpu.SMEM)]
         + [whole((rows, width))] * devices
-        + [whole((rows, width + LANES))] * devices
         + [
+            whole((keys, width + LANES)),
             whole((rows, 3 * width)),
             whole((width, width)),
             whole((head_rows, window_width)),
             whole((pairs, rows, LANES)),
             column_block(0),
         ],
-        out_specs=[whole((per * devices, rows, LANES)), whole((keys, width))],
+        out_specs=[whole((per * devices, rows, LANES))],
         out_shape=[
             jax.ShapeDtypeStruct((per * devices, rows, LANES), BF),
-            jax.ShapeDtypeStruct((keys, width), BF),
         ],
         scratch_shapes=[
             pltpu.VMEM((keys, width), BF),
             pltpu.VMEM((head_rows, keys), F32),
             pltpu.VMEM((head_rows, keys), F32),
-            pltpu.VMEM((keys, LANES), BF),
         ],
         compiler_params=pltpu.CompilerParams(vmem_limit_bytes=VMEM_BYTES),
         cost_estimate=cost(12.0),
         name="key_grad",
-    )(ids, *resid_pieces, *ext_pieces, joined_own, w_out, mirror, query_grad, joined)
-    blocks, lines, returned_rows = tie(blocks, lines, returned_rows)
+    )(ids, *resid_pieces, ext_all, joined_own, w_out, mirror, query_grad, joined)
+    blocks, out_sum = tie(blocks, out_sum)
     received = lax.all_to_all(
         blocks.reshape(devices, per, rows, LANES), "expert", split_axis=0, concat_axis=0, tiled=True
-    )
-    (result,) = call(
-        result_body,
-        [ids, returned_rows, back_slots, after, gate],
-        [((rows, width), BF)],
-        name="result",
-        us=2.0,
     )
     tokens_grad, gain_one_part = call(
         source_body,
@@ -838,32 +813,52 @@
         name="source_grad",
         us=4.0,
     )
+    table_line = table_part[:heads].T.reshape(shards, table_rows * heads)
+    table_line = pad_to(table_line, (shards, part)).reshape(1, width)
+    lines = jnp.concatenate([router_part[:experts], gain_one_part, gain_two_part, table_line], axis=0)
+    line_count = lines.shape[0]
+    groups = per * LANES // part
+    line_rows = -(-line_count // (16 * groups)) * 16
+    lines = pad_to(lines, (groups * line_rows, width)).reshape(groups, line_rows, shards, part)
+    lines = lines.transpose(2, 1, 0, 3).reshape(shards, line_rows, groups * part)
+    lines = pad_to(lines, (shards, line_rows, per * LANES)).astype(BF)
     (weight_part,) = call(
-        functools.partial(weight_body, per, pairs),
-        [ids, xn_all, mixed_all, received],
-        [((width, per * LANES), BF)],
+        functools.partial(weight_body, (per, pairs, shards)),
+        [ids, xn_all, ext_all, received, lines],
+        [((shards, part + line_rows, per * LANES), BF)],
         [pltpu.VMEM((keys, per * LANES), BF)],
         name="weight_grads",
         us=4.0,
     )
-
-    mine = scatter_rows(weight_part.reshape(shards, part, per * LANES)).astype(BF)
-    attn_in_grad, attn_out_grad = call(
-        functools.partial(spread_body, per, pairs),
-        [ids, *core_pieces(chip_pieces(mine))],
-        [((part, 3 * width), F32), ((part, width), F32)],
+    weight_part, out_sum = tie(weight_part, out_sum)
+    mine = scatter_rows(weight_part).astype(BF)
+    returned_rows = exchange(out_sum)
+    mine, returned_rows = tie(mine, returned_rows)
+    pieces = chip_pieces(mine)
+    (result,) = call(
+        result_body,
+        [ids, returned_rows, back_slots, after, gate],
+        [((rows, width), BF)],
+        name="result",
+        us=2.0,
+    )
+    pieces, result = tie(pieces, result)
+    attn_in_grad, attn_out_grad, lines = call(
+        functools.partial(spread_body, (per, pairs)),
+        [ids, *core_pieces(pieces)],
+        [((part, 3 * width), F32), ((part, width), F32), ((line_rows, per * LANES), F32)],
         name="spread",
         us=2.0,
     )
-
-    (gain_line,) = sum_lines(gain_one_part)
+    lines = lines[:, : groups * part].reshape(line_rows, groups, part).transpose(1, 0, 2)
+    lines = lines.reshape(groups * line_rows, part)
     router_grad = lines[:experts].T
-    table_grad = lines[experts + 1, : table_rows * heads].reshape(table_rows, heads)
+    table_grad = lines[experts + 2, : table_rows * heads].reshape(table_rows, heads)
     return (
         result[None],
         tokens_grad[None],
-        gain_line,
         lines[experts],
+        lines[experts + 1],
         attn_in_grad,
         attn_out_grad,
         router_grad,

time: 318 us -> 264 us (0.83)
  starting transfers between devices: 97.4 us -> 56.9 us
  waiting for transfers between devices: 79.7 us -> 63.4 us
  between operations: 1.63 us -> 14.4 us
  local copies, waits for them, and re-layouts: 24.4 us -> 17.7 us
    ppermute x78 -> x40, waiting for transfers between devices: 76.8 us -> 35.2 us  [swap(): return lax.ppermute(x, axis, [(i, i ^ mask) for i in range(count)])]
    ppermute x78 -> x40, starting transfers between devices: 78.8 us -> 38.9 us  [swap(): return lax.ppermute(x, axis, [(i, i ^ mask) for i in range(count)])]
    all_to_all x4, waiting for transfers between devices: 0.01 us -> 16.7 us  [exchange(): lax.all_to_all(blocks, 'expert', split_axis=0, concat_axis=0, tiled=True)]
    all_gather x0 -> x3, waiting for transfers between devices: none -> 3.75 us  [the longest x1 3.73 us: local(): ups_all = lax.all_gather(ups, 'wshard', axis=0, tiled=True)]
    unnamed x124 -> x92, local copies, waits for them, and re-layouts: 11.2 us -> 8.24 us
  transfers between devices with their start and end apart: 83 -> 49, of which waited for: 23 -> 21; matrix products, arithmetic and copies ran while one was open for 8% -> 5% of each run, Pallas kernels for 31% -> 35%
where the time goes in v2:
time: 264 us; the launch traced here: 262 us
  Pallas kernels  100 us (38%)
  waiting for transfers between devices  63.4 us (24%)
  starting transfers between devices  56.9 us (22%)
  local copies, waits for them, and re-layouts  17.7 us (7%)
  between operations  14.4 us (5%)
  other arithmetic  7.73 us (3%)
    ppermute x40, starting transfers between devices, swap(): return lax.ppermute(x, axis, [(i, i ^ mask) for i in range(count)])  38.9 us
    pallas_call x7, Pallas kernels, call(): pl.pallas_call(body, in_specs=[ids] + [pl.BlockSpec(memory_space=pltpu.VM...  38.3 us
    ppermute x40, waiting for transfers between devices, swap(): return lax.ppermute(x, axis, [(i, i ^ mask) for i in range(count)])  35.2 us
    pallas_call x4, Pallas kernels, local(): pl.pallas_call(functools.partial(expert_body, (experts, per_device, capac...  23 us
    all_to_all x4, waiting for transfers between devices, exchange(): lax.all_to_all(blocks, 'expert', split_axis=0, concat_axis=0, tiled=True)  16.7 us
    all_to_all x4, starting transfers between devices, exchange(): lax.all_to_all(blocks, 'expert', split_axis=0, concat_axis=0, tiled=True)  13.7 us
    pallas_call x1, Pallas kernels, local(): pl.pallas_call(functools.partial(key_body, (devices, heads, head_dim)), g...  12.6 us
    pallas_call x1, Pallas kernels, local(): pl.pallas_call(functools.partial(query_body, (head_dim, bucket_count)), g...  11.4 us
  transfers between devices with their start and end apart: 49, of which 21 were waited for; matrix products, arithmetic and copies ran while one was open for 5% of the time, Pallas kernels for 35%

profile of v2, /device:TPU:0, one launch (start us, length us, event | category | flops | bytes accessed | tf_op | source)
XLA Modules:
  0.0 262.2 jit_solution(5361596403088767055)
XLA Ops:
  32.3 3.4 %all-to-all-start = ((bf16[8,24,768]{2,1,0:T(8,128)(2,1)}), bf16[8,24,768]{2,1,0:T(8,128)(2,1)S(1)}, u32[]{:S(2)}, u32[]{:S(2)}) async-start(bf16[8,24,768]{2,1,0:T(8,128)(2,1)} %bitcast.7), calls=%async_computation | async-start | bytes 589824 | tf_op jit(solution)/shard_map/all_to_all | solution.py:594
  38.1 16.7 %all-to-all-done = bf16[8,24,768]{2,1,0:T(8,128)(2,1)S(1)} async-done(((bf16[8,24,768]{2,1,0:T(8,128)(2,1)}), bf16[8,24,768]{2,1,0:T(8,128)(2,1)S(1)}, u32[]{:S(2)}, u32[]{:S(2)}) %all-to-all-start) | async-done | bytes 294944 | tf_op jit(solution)/shard_map/all_to_all | solution.py:594
  61.1 18.5 %attention_forward.1 = (bf16[1024,768]{1,0:T(8,128)(2,1)}, bf16[1024,2304]{1,0:T(8,128)(2,1)}, bf16[128,2304]{1,0:T(8,128)(2,1)}, bf16[128,896]{1,0:T(8,128)(2,1...) custom-call(s32[2]{0:T(128)} %pad_add_fusion.refs_0_.ids, ...), custom_call_target="tpu_custom_call" | custom-call | flops 200000000 | bytes 200000 | tf_op jit(solution)/shard_map/attention_forward/pallas_call | solution.py:120
  82.9 3.4 %all-to-all-start.1 = ((bf16[8,24,768]{2,1,0:T(8,128)(2,1)}), bf16[8,24,768]{2,1,0:T(8,128)(2,1)S(1)}, u32[]{:S(2)}, u32[]{:S(2)}) async-start(bf16[8,24,768]{2,1,0:T(8,128)(2,1)} %bitcast.65), calls=%async_computation.1 | async-start | bytes 589824 | tf_op jit(solution)/shard_map/all_to_all | solution.py:594
  86.5 3.7 %all-gather.6.cloned.1.call-done.chunks = bf16[768,768]{1,0:T(8,128)(2,1)} async-done(((bf16[192,768]{1,0:T(8,128)(2,1)}), bf16[768,768]{1,0:T(8,128)(2,1)}) %all-gather.6.cloned.1.call-update) | async-done | bytes 1179664 | tf_op jit(solution)/shard_map/all_gather | solution.py:614
  90.3 4.3 %upstream.1 = (bf16[2,384,768]{2,1,0:T(8,128)(2,1)}, f32[2,384,768]{2,1,0:T(8,128)}) custom-call(s32[2]{0:T(128)} %pad_add_fusion.refs_0_.ids, bf16[768,768]{1,0:T(8,128)(2,1)} %all-gather.6.cloned.1.call-done.chunks, bf16[2,768,768]{2,1,0:T(8,128)(2,1)} %refs_20_.1), custom_call_target="tpu_custom_call" | custom-call | flops 5000000000 | bytes 5000000 | tf_op jit(solution)/shard_map/upstream/pallas_call | solution.py:651
  97.7 5.7 %experts.4 = (bf16[192,768]{1,0:T(8,128)(2,1)}, bf16[2,96,768]{2,1,0:T(8,128)(2,1)}, bf16[2,96,768]{2,1,0:T(8,128)(2,1)}, bf16[2,96,768]{2,1,0:T(8,128)(2,1)}, b...) custom-call(s32[2]{0:T(128)} %pad_add_fusion.refs_0_.ids, bf16[192,768]{1,0:T(8,128)(2,1)} %bitcast.53, ...), custom_call_target="tpu_custom_call" | custom-call | flops 500000000 | bytes 500000 | tf_op jit(solution)/shard_map/experts/pallas_call | solution.py:676
  103.4 5.4 %collective-permute-done.17.rows_in = bf16[192,768]{1,0:T(8,128)(2,1)S(1)} collective-permute-done((bf16[192,768]{1,0:T(8,128)(2,1)S(1)}, bf16[192,768]{1,0:T(8,128)(2,1)S(1)}, u32[]{:S(2)}, u32[]{:S(2)}) %collective-permute-start.17) | collective-permute-done | bytes 294944 | tf_op jit(solution)/shard_map/ppermute | solution.py:32
  109.5 5.8 %experts.5 = (bf16[192,768]{1,0:T(8,128)(2,1)}, bf16[2,96,768]{2,1,0:T(8,128)(2,1)}, bf16[2,96,768]{2,1,0:T(8,128)(2,1)}, bf16[2,96,768]{2,1,0:T(8,128)(2,1)}, b...) custom-call(s32[2]{0:T(128)} %pad_add_fusion.refs_0_.ids, bf16[192,768]{1,0:T(8,128)(2,1)} %copy-done.13, ...), custom_call_target="tpu_custom_call" | custom-call | flops 500000000 | bytes 500000 | tf_op jit(solution)/shard_map/experts/pallas_call | solution.py:676
  117.4 5.8 %experts.6 = (bf16[192,768]{1,0:T(8,128)(2,1)}, bf16[2,96,768]{2,1,0:T(8,128)(2,1)}, bf16[2,96,768]{2,1,0:T(8,128)(2,1)}, bf16[2,96,768]{2,1,0:T(8,128)(2,1)}, b...) custom-call(s32[2]{0:T(128)} %pad_add_fusion.refs_0_.ids, bf16[192,768]{1,0:T(8,128)(2,1)} %copy-done.11, ...), custom_call_target="tpu_custom_call" | custom-call | flops 500000000 | bytes 500000 | tf_op jit(solution)/shard_map/experts/pallas_call | solution.py:676
  123.4 3.7 %collective-permute-done.19.rows_in = bf16[192,768]{1,0:T(8,128)(2,1)S(1)} collective-permute-done((bf16[192,768]{1,0:T(8,128)(2,1)S(1)}, bf16[192,768]{1,0:T(8,128)(2,1)S(1)}, u32[]{:S(2)}, u32[]{:S(2)}) %collective-permute-start.19) | collective-permute-done | bytes 294944 | tf_op jit(solution)/shard_map/ppermute | solution.py:32
  127.8 5.8 %experts.7 = (bf16[192,768]{1,0:T(8,128)(2,1)}, bf16[2,96,768]{2,1,0:T(8,128)(2,1)}, bf16[2,96,768]{2,1,0:T(8,128)(2,1)}, bf16[2,96,768]{2,1,0:T(8,128)(2,1)}, b...) custom-call(s32[2]{0:T(128)} %pad_add_fusion.refs_0_.ids, bf16[192,768]{1,0:T(8,128)(2,1)} %copy-done.12, ...), custom_call_target="tpu_custom_call" | custom-call | flops 500000000 | bytes 500000 | tf_op jit(solution)/shard_map/experts/pallas_call | solution.py:676
  137.3 8.7 %collective-permute-done.21 = bf16[192,768]{1,0:T(8,128)(2,1)S(1)} collective-permute-done((bf16[192,768]{1,0:T(8,128)(2,1)}, bf16[192,768]{1,0:T(8,128)(2,1)S(1)}, u32[]{:S(2)}, u32[]{:S(2)}) %collective-permute-start.21) | collective-permute-done | bytes 294944 | tf_op jit(solution)/shard_map/ppermute | solution.py:32
  146.9 3.4 %all-to-all-start.2 = ((bf16[8,24,768]{2,1,0:T(8,128)(2,1)}), bf16[8,24,768]{2,1,0:T(8,128)(2,1)S(1)}, u32[]{:S(2)}, u32[]{:S(2)}) async-start(bf16[8,24,768]{2,1,0:T(8,128)(2,1)} %bitcast.11), calls=%async_computation.2 | async-start | bytes 589824 | tf_op jit(solution)/shard_map/all_to_all | solution.py:594
  150.6 10.7 %expert_weights.1 = (bf16[768,768]{1,0:T(8,128)(2,1)}, f32[2,768,768]{2,1,0:T(8,128)}, f32[2,768,768]{2,1,0:T(8,128)}, f32[128,768]{1,0:T(8,128)}) custom-call(s32[2]{0:T(128)} %pad_add_fusion.refs_0_.ids, bf16[2,96,768]{2,1,0:T(8,128)(2,1)} %get-tuple-element.194.refs_0_, bf16[2,96,768]{2,1,0:T(8,128)(2,1)} %get-tuple-element.195.refs_1_, ...), custom_call_target="tpu_custom_call" | custom-call | flops 8000000000 | bytes 8000000 | tf_op jit(solution)/shard_map/expert_weights/pallas_call | solution.py:711
  168.0 11.4 %query_grad.1 = (bf16[6,128,128]{2,1,0:T(8,128)(2,1)}, f32[16,32]{1,0:T(8,128)}) custom-call(s32[2]{0:T(128)} %pad_add_fusion.refs_0_.ids, bf16[128,768]{1,0:T(8,128)(2,1)} %get-tuple-element.224.resid_low.refs_1_, bf16[128,896]{1,0:T(8,128)(2,1)} %get-tuple-element.164.ext, bf16[128,2304]{1,0:T(8,128)(2,1)} %get-tuple-element.220.joined_own.refs_10_, ...), custom_call_target="tpu_custom_call" | custom-call | flops 10000000000 | bytes 10000000 | tf_op jit(solution)/shard_map/query_grad/pallas_call | solution.py:746
  182.4 12.6 %key_grad.1.blocks = bf16[24,128,128]{2,1,0:T(8,128)(2,1)} custom-call(s32[2]{0:T(128)} %pad_add_fusion.refs_0_.ids, bf16[128,768]{1,0:T(8,128)(2,1)} %get-tuple-element.224.resid_low.refs_1_, bf16[128,768]{1,0:T(8,128)(2,1)} %copy-done.32, bf16[128,768]{1,0:T(8,128)(2,1)} %copy-done.29, bf16[128,768]{1,0:T(8,128)(2,1)} %copy-done.33, ...), custom_call_target="tpu_custom_call" | custom-call | flops 12000000000 | bytes 12000000 | tf_op jit(solution)/shard_map/key_grad/pallas_call | solution.py:778
  197.4 3.7 %all-to-all-start.3 = ((bf16[8,3,128,128]{3,2,1,0:T(8,128)(2,1)}), bf16[8,3,128,128]{3,2,1,0:T(8,128)(2,1)S(1)}, u32[]{:S(2)}, u32[]{:S(2)}) async-start(bf16[8,3,128,128]{3,2,1,0:T(8,128)(2,1)} %bitcast.62), calls=%async_computation.4 | async-start | bytes 1572864 | tf_op jit(solution)/shard_map/all_to_all | solution.py:805
  202.2 4.5 %source_grad.1 = (bf16[128,768]{1,0:T(8,128)(2,1)}, f32[1,768]{1,0:T(1,128)}) custom-call(s32[2]{0:T(128)} %pad_add_fusion.refs_0_.ids, bf16[24,128,128]{2,1,0:T(8,128)(2,1)} %key_grad.1.blocks, bf16[768,2304]{1,0:T(8,128)(2,1)} %get-tuple-element.234.w_in, bf16[128,768]{1,0:T(8,128)(2,1)} %bitcast.60, f32[8,768]{1,0:T(8,128)} %get-tuple-element.157.gains, ...), custom_call_target="tpu_custom_call" | custom-call | flops 4000000000 | bytes 4000000 | tf_op jit(solution)/shard_map/source_grad/pallas_call | solution.py:120
  208.3 5.3 %all-to-all-done.3.received = bf16[8,3,128,128]{3,2,1,0:T(8,128)(2,1)S(1)} async-done(((bf16[8,3,128,128]{3,2,1,0:T(8,128)(2,1)}), bf16[8,3,128,128]{3,2,1,0:T(8,128)(2,1)S(1)}, u32[]{:S(2)}, u32[]{:S(2)}) %all-to-all-start.3) | async-done | bytes 786464 | tf_op jit(solution)/shard_map/all_to_all | solution.py:805
  214.5 4.4 %weight_grads.1 = bf16[4,208,384]{2,1,0:T(8,128)(2,1)} custom-call(s32[2]{0:T(128)} %pad_add_fusion.refs_0_.ids, bf16[1024,768]{1,0:T(8,128)(2,1)} %get-tuple-element.154.xn_all, bf16[1024,896]{1,0:T(8,128)(2,1)} %all-gather.8.cloned.1.call-done.refs_9_.ext_all, bf16[8,3,128,128]{3,2,1,0:T(8,128)(2,1)} %copy-done.3, ...), custom_call_target="tpu_custom_call" | custom-call | flops 4000000000 | bytes 4000000 | tf_op jit(solution)/shard_map/weight_grads/pallas_call | solution.py:120
  225.3 3.4 %all-to-all-start.4 = ((bf16[8,24,768]{2,1,0:T(8,128)(2,1)}), bf16[8,24,768]{2,1,0:T(8,128)(2,1)S(1)}, u32[]{:S(2)}, u32[]{:S(2)}) async-start(bf16[8,24,768]{2,1,0:T(8,128)(2,1)} %bitcast.20), calls=%async_computation.5 | async-start | bytes 589824 | tf_op jit(solution)/shard_map/all_to_all | solution.py:594
  228.7 6.3 %collective-permute-done.31 = bf16[208,384]{1,0:T(8,128)(2,1)S(1)} collective-permute-done((bf16[208,384]{1,0:T(8,128)(2,1)S(1)}, bf16[208,384]{1,0:T(8,128)(2,1)S(1)}, u32[]{:S(2)}, u32[]{:S(2)}) %collective-permute-start.31) | collective-permute-done | bytes 159776 | tf_op jit(solution)/shard_map/ppermute | solution.py:32
  249.7 3.2 %spread.1 = (f32[192,2304]{1,0:T(8,128)}, f32[192,768]{1,0:T(8,128)}, f32[16,384]{1,0:T(8,128)}) custom-call(s32[2]{0:T(128)} %pad_add_fusion.refs_0_.ids, bf16[208,384]{1,0:T(8,128)(2,1)} %copy-done.23, bf16[208,384]{1,0:T(8,128)(2,1)} %copy-done.39, bf16[208,384]{1,0:T(8,128)(2,1)} %copy-done.36, bf16[208,384]{1,0:T(8,128)(2,1)} %copy-done.40, ...), custom_call_target="tpu_custom_call" | custom-call | flops 2000000000 | bytes 2000000 | tf_op jit(solution)/shard_map/spread/pallas_call | solution.py:120
  (224 shorter events, 87.9 us)
Async XLA Ops:
  7.2 72.5 %all-gather.4.cloned.1.call-start = ((), (), s32[]{:S(2)}) async-start(), calls=%async_computation.6 | async-start | bytes 1474560 | tf_op jit(solution)/shard_map/all_gather | solution.py:610
  14.4 12.3 %collective-permute-start.4 = (bf16[48,1280]{1,0:T(8,128)(2,1)S(1)}, bf16[48,1280]{1,0:T(8,128)(2,1)S(1)}, u32[]{:S(2)}, u32[]{:S(2)}) collective-permute-start(bf16[48,1280]{1,0:T(8,128)(2,1)S(1)} %pad_maximum_fusion), channel_id=1, source_target_pairs={{0,2},{1,3},{2,0},{3,1},{4,6},{5,7},{6,4},{7,5},{8,10},{9,11},{10,... | collective-permute-start | bytes 368648 | tf_op jit(solution)/shard_map/ppermute | solution.py:32
  28.3 26.5 %collective-permute-start.6 = (bf16[192,1280]{1,0:T(8,128)(2,1)S(1)}, bf16[192,1280]{1,0:T(8,128)(2,1)S(1)}, u32[]{:S(2)}, u32[]{:S(2)}) collective-permute-start(bf16[192,1280]{1,0:T(8,128)(2,1)S(1)} %constant_dynamic-update-slice_fusion.refs_9_), channel_id=1, source_target_pairs={{0,8},{4,12},{8,0},{12,4},{16,24},{20,28},{24,16},{28,20},{1,9},{5... | collective-permute-start | bytes 1474568 | tf_op jit(solution)/shard_map/ppermute | solution.py:32
  29.5 25.3 %collective-permute-start.7 = (bf16[192,1280]{1,0:T(8,128)(2,1)S(1)}, bf16[192,1280]{1,0:T(8,128)(2,1)S(1)}, u32[]{:S(2)}, u32[]{:S(2)}) collective-permute-start(bf16[192,1280]{1,0:T(8,128)(2,1)S(1)} %constant_dynamic-update-slice_fusion.refs_9_), channel_id=1, source_target_pairs={{0,16},{4,20},{8,24},{12,28},{16,0},{20,4},{24,8},{28,12},{1,17},{... | collective-permute-start | bytes 1474568 | tf_op jit(solution)/shard_map/ppermute | solution.py:32
  30.4 24.4 %collective-permute-start.8 = (bf16[192,1280]{1,0:T(8,128)(2,1)S(1)}, bf16[192,1280]{1,0:T(8,128)(2,1)S(1)}, u32[]{:S(2)}, u32[]{:S(2)}) collective-permute-start(bf16[192,1280]{1,0:T(8,128)(2,1)S(1)} %constant_dynamic-update-slice_fusion.refs_9_), channel_id=1, source_target_pairs={{0,24},{4,28},{8,16},{12,20},{16,8},{20,12},{24,0},{28,4},{1,25},{... | collective-permute-start | bytes 1474568 | tf_op jit(solution)/shard_map/ppermute | solution.py:32
  32.3 22.5 %all-to-all-start = ((bf16[8,24,768]{2,1,0:T(8,128)(2,1)}), bf16[8,24,768]{2,1,0:T(8,128)(2,1)S(1)}, u32[]{:S(2)}, u32[]{:S(2)}) async-start(bf16[8,24,768]{2,1,0:T(8,128)(2,1)} %bitcast.7), calls=%async_computation | async-start | bytes 589824 | tf_op jit(solution)/shard_map/all_to_all | solution.py:594
  35.8 54.5 %all-gather.6.cloned.1.call-start = ((), (), s32[]{:S(2)}) async-start(), calls=%async_computation.7 | async-start | bytes 1474560 | tf_op jit(solution)/shard_map/all_gather | solution.py:614
  82.9 11.7 %all-to-all-start.1 = ((bf16[8,24,768]{2,1,0:T(8,128)(2,1)}), bf16[8,24,768]{2,1,0:T(8,128)(2,1)S(1)}, u32[]{:S(2)}, u32[]{:S(2)}) async-start(bf16[8,24,768]{2,1,0:T(8,128)(2,1)} %bitcast.65), calls=%async_computation.1 | async-start | bytes 589824 | tf_op jit(solution)/shard_map/all_to_all | solution.py:594
  86.3 95.5 %all-gather.8.cloned.1.call-start = ((), (), s32[]{:S(2)}) async-start(), calls=%async_computation.8 | async-start | bytes 2064384 | tf_op jit(solution)/shard_map/all_gather | solution.py:669
  94.6 14.2 %collective-permute-start.17 = (bf16[192,768]{1,0:T(8,128)(2,1)S(1)}, bf16[192,768]{1,0:T(8,128)(2,1)S(1)}, u32[]{:S(2)}, u32[]{:S(2)}) collective-permute-start(bf16[192,768]{1,0:T(8,128)(2,1)S(1)} %bitcast.51), channel_id=1, source_target_pairs={{0,1},{1,0},{2,3},{3,2},{4,5},{5,4},{6,7},{7,6},{8,9},{9,8},{10,11... | collective-permute-start | bytes 884744 | tf_op jit(solution)/shard_map/ppermute | solution.py:32
  95.7 19.6 %collective-permute-start.18 = (bf16[192,768]{1,0:T(8,128)(2,1)S(1)}, bf16[192,768]{1,0:T(8,128)(2,1)S(1)}, u32[]{:S(2)}, u32[]{:S(2)}) collective-permute-start(bf16[192,768]{1,0:T(8,128)(2,1)S(1)} %bitcast.52), channel_id=1, source_target_pairs={{0,2},{1,3},{2,0},{3,1},{4,6},{5,7},{6,4},{7,5},{8,10},{9,11},{10,... | collective-permute-start | bytes 884744 | tf_op jit(solution)/shard_map/ppermute | solution.py:32
  115.3 11.8 %collective-permute-start.19 = (bf16[192,768]{1,0:T(8,128)(2,1)S(1)}, bf16[192,768]{1,0:T(8,128)(2,1)S(1)}, u32[]{:S(2)}, u32[]{:S(2)}) collective-permute-start(bf16[192,768]{1,0:T(8,128)(2,1)S(1)} %collective-permute-done.18.rows_in), channel_id=1, source_target_pairs={{0,1},{1,0},{2,3},{3,2},{4,5},{5,4},{6,7},{7,6},{8,9},{9,8},{10,11... | collective-permute-start | bytes 884744 | tf_op jit(solution)/shard_map/ppermute | solution.py:32
  115.4 30.6 %collective-permute-start.20 = (bf16[192,768]{1,0:T(8,128)(2,1)}, bf16[192,768]{1,0:T(8,128)(2,1)S(1)}, u32[]{:S(2)}, u32[]{:S(2)}) collective-permute-start(bf16[192,768]{1,0:T(8,128)(2,1)} %get-tuple-element.171), channel_id=1, source_target_pairs={{0,1},{1,0},{2,3},{3,2},{4,5},{5,4},{6,7},{7,6},{8,9},{9,8},{10,11... | collective-permute-start | bytes 884744 | tf_op jit(solution)/shard_map/ppermute | solution.py:32
  123.2 22.8 %collective-permute-start.21 = (bf16[192,768]{1,0:T(8,128)(2,1)}, bf16[192,768]{1,0:T(8,128)(2,1)S(1)}, u32[]{:S(2)}, u32[]{:S(2)}) collective-permute-start(bf16[192,768]{1,0:T(8,128)(2,1)} %get-tuple-element.174), channel_id=1, source_target_pairs={{0,2},{1,3},{2,0},{3,1},{4,6},{5,7},{6,4},{7,5},{8,10},{9,11},{10,... | collective-permute-start | bytes 884744 | tf_op jit(solution)/shard_map/ppermute | solution.py:32
  133.6 12.4 %collective-permute-start.22 = (bf16[192,768]{1,0:T(8,128)(2,1)}, bf16[192,768]{1,0:T(8,128)(2,1)S(1)}, u32[]{:S(2)}, u32[]{:S(2)}) collective-permute-start(bf16[192,768]{1,0:T(8,128)(2,1)} %get-tuple-element.193), channel_id=1, source_target_pairs={{0,3},{1,2},{2,1},{3,0},{4,7},{5,6},{6,5},{7,4},{8,11},{9,10},{10,... | collective-permute-start | bytes 884744 | tf_op jit(solution)/shard_map/ppermute | solution.py:32
  146.9 14.4 %all-to-all-start.2 = ((bf16[8,24,768]{2,1,0:T(8,128)(2,1)}), bf16[8,24,768]{2,1,0:T(8,128)(2,1)S(1)}, u32[]{:S(2)}, u32[]{:S(2)}) async-start(bf16[8,24,768]{2,1,0:T(8,128)(2,1)} %bitcast.11), calls=%async_computation.2 | async-start | bytes 589824 | tf_op jit(solution)/shard_map/all_to_all | solution.py:594
  150.3 47.1 %reduce-scatter.2.cloned.1.call-start = ((), (), s32[]{:S(2)}) async-start(), calls=%async_computation.9 | async-start | bytes 1474560 | tf_op jit(solution)/shard_map/reduce_scatter | solution.py:739
  164.4 14.9 %collective-permute-start.23 = (bf16[128,768]{1,0:T(8,128)(2,1)}, bf16[128,768]{1,0:T(8,128)(2,1)S(1)}, u32[]{:S(2)}, u32[]{:S(2)}) collective-permute-start(bf16[128,768]{1,0:T(8,128)(2,1)} %get-tuple-element.224.resid_low.refs_1_), channel_id=1, source_target_pairs={{0,8},{4,12},{8,0},{12,4},{16,24},{20,28},{24,16},{28,20},{1,9},{5... | collective-permute-start | bytes 589832 | tf_op jit(solution)/shard_map/ppermute | solution.py:32
  166.1 13.2 %collective-permute-start.24 = (bf16[128,768]{1,0:T(8,128)(2,1)}, bf16[128,768]{1,0:T(8,128)(2,1)S(1)}, u32[]{:S(2)}, u32[]{:S(2)}) collective-permute-start(bf16[128,768]{1,0:T(8,128)(2,1)} %get-tuple-element.224.resid_low.refs_1_), channel_id=1, source_target_pairs={{0,16},{4,20},{8,24},{12,28},{16,0},{20,4},{24,8},{28,12},{1,17},{... | collective-permute-start | bytes 589832 | tf_op jit(solution)/shard_map/ppermute | solution.py:32
  167.6 11.8 %collective-permute-start.25 = (bf16[128,768]{1,0:T(8,128)(2,1)}, bf16[128,768]{1,0:T(8,128)(2,1)S(1)}, u32[]{:S(2)}, u32[]{:S(2)}) collective-permute-start(bf16[128,768]{1,0:T(8,128)(2,1)} %get-tuple-element.224.resid_low.refs_1_), channel_id=1, source_target_pairs={{0,24},{4,28},{8,16},{12,20},{16,8},{20,12},{24,0},{28,4},{1,25},{... | collective-permute-start | bytes 589832 | tf_op jit(solution)/shard_map/ppermute | solution.py:32
  197.4 16.3 %all-to-all-start.3 = ((bf16[8,3,128,128]{3,2,1,0:T(8,128)(2,1)}), bf16[8,3,128,128]{3,2,1,0:T(8,128)(2,1)S(1)}, u32[]{:S(2)}, u32[]{:S(2)}) async-start(bf16[8,3,128,128]{3,2,1,0:T(8,128)(2,1)} %bitcast.62), calls=%async_computation.4 | async-start | bytes 1572864 | tf_op jit(solution)/shard_map/all_to_all | solution.py:805
  222.8 12.2 %collective-permute-start.31 = (bf16[208,384]{1,0:T(8,128)(2,1)S(1)}, bf16[208,384]{1,0:T(8,128)(2,1)S(1)}, u32[]{:S(2)}, u32[]{:S(2)}) collective-permute-start(bf16[208,384]{1,0:T(8,128)(2,1)S(1)} %get-tuple-element.258), channel_id=1, source_target_pairs={{0,2},{1,3},{2,0},{3,1},{4,6},{5,7},{6,4},{7,5},{8,10},{9,11},{10,... | collective-permute-start | bytes 479240 | tf_op jit(solution)/shard_map/ppermute | solution.py:32
  223.9 11.2 %collective-permute-start.32 = (bf16[208,384]{1,0:T(8,128)(2,1)S(1)}, bf16[208,384]{1,0:T(8,128)(2,1)S(1)}, u32[]{:S(2)}, u32[]{:S(2)}) collective-permute-start(bf16[208,384]{1,0:T(8,128)(2,1)S(1)} %get-tuple-element.257), channel_id=1, source_target_pairs={{0,3},{1,2},{2,1},{3,0},{4,7},{5,6},{6,5},{7,4},{8,11},{9,10},{10,... | collective-permute-start | bytes 479240 | tf_op jit(solution)/shard_map/ppermute | solution.py:32
  225.3 10.8 %all-to-all-start.4 = ((bf16[8,24,768]{2,1,0:T(8,128)(2,1)}), bf16[8,24,768]{2,1,0:T(8,128)(2,1)S(1)}, u32[]{:S(2)}, u32[]{:S(2)}) async-start(bf16[8,24,768]{2,1,0:T(8,128)(2,1)} %bitcast.20), calls=%async_computation.5 | async-start | bytes 589824 | tf_op jit(solution)/shard_map/all_to_all | solution.py:594
  (68 other events, 549.1 us)
Sparse Core Ops, SparseCore 0:
  28.3 30.7 all-gather.3
  60.7 29.5 all-gather.5
  94.7 25.9 all-gather.7
  164.5 32.7 reduce-scatter.1

commit v3 on v2

--- a/solution.py
+++ b/solution.py
@@ -55,6 +55,24 @@
     beside = lax.dynamic_slice(small, (first, 0), (rows // chips, small.shape[1]))
     chunk = jnp.concatenate([chunk, beside], axis=1)
     return [chunk] + [swap(chunk, "wshard", mask) for mask in range(1, lax.axis_size("wshard"))]
+
+
+def doubling_steps(count):
+    return [1 << bit for bit in reversed(range((count - 1).bit_length()))]
+
+
+def doubling_order(count):
+    order = [0]
+    for step in doubling_steps(count):
+        order = order + [mask ^ step for mask in order]
+    return order
+
+
+def place_order(gathered, target, shard_id, shards):
+    rows = target.shape[0] // shards
+    for index, mask in enumerate(doubling_order(shards)):
+        row = pl.multiple_of((shard_id ^ mask) * rows, 16)
+        target[pl.ds(row, rows), :] = gathered[index * rows : (index + 1) * rows, :]
 
 
 def place_weight(pieces, target, small, expert_id, shard_id, shards):
@@ -115,12 +133,13 @@
     return pl.BlockSpec(shape, lambda *_: (0,) * len(shape))
 
 
-def call(body, args, outs, scratch=(), name=None, us=1.0):
+def call(body, args, outs, scratch=(), name=None, us=1.0, far=()):
     ids = pl.BlockSpec(memory_space=pltpu.SMEM)
+    near = pl.BlockSpec(memory_space=pltpu.VMEM)
     return pl.pallas_call(
         body,
-        in_specs=[ids] + [pl.BlockSpec(memory_space=pltpu.VMEM)] * (len(args) - 1),
-        out_specs=[pl.BlockSpec(memory_space=pltpu.VMEM)] * len(outs),
+        in_specs=[ids] + [near] * (len(args) - 1),
+        out_specs=[pl.BlockSpec(memory_space=pl.ANY) if k in far else near for k in range(len(outs))],
         out_shape=[jax.ShapeDtypeStruct(shape, kind) for shape, kind in outs],
         scratch_shapes=list(scratch),
         compiler_params=pltpu.CompilerParams(vmem_limit_bytes=VMEM_BYTES),
@@ -146,7 +165,7 @@
     tokens = [refs.pop(0) for _ in range(devices)]
     in_pieces = [refs.pop(0) for _ in range(in_count)]
     window_ref, mirror_ref = [refs.pop(0) for _ in range(2)]
-    xn_all, joined, joined_own, ext, w_in, window, mirror, gains, small = refs
+    xn_far, joined_far, joined_own, ext, window, mirror, gains, small, xn_all, joined, w_in, sems = refs
     expert_id = ids[0]
     shard_id = ids[1]
     rows, width = tokens[0].shape
@@ -156,6 +175,8 @@
     gains[...] = turned[experts : experts + 8, :]
     gain_one = gains[0:1, :]
     place_blocks(tokens, xn_all, expert_id, lambda block: normalize(block, gain_one))
+    xn_copy = pltpu.make_async_copy(xn_all, xn_far, sems.at[0])
+    xn_copy.start()
     head_rows = window.shape[0]
     per_shard = buckets // shards
     spot = lax.broadcasted_iota(jnp.int32, (buckets, width), 1)
@@ -174,6 +195,8 @@
         return carry
 
     lax.fori_loop(0, (3 * width // column_block) * (keys // row_block), project, 0)
+    joined_copy = pltpu.make_async_copy(joined, joined_far, sems.at[1])
+    joined_copy.start()
     window[...] = dot(table, bucket_hot(window_ref, buckets))
     mirror[...] = dot(table, bucket_hot(mirror_ref, buckets))
     own = pl.multiple_of(expert_id * rows, rows)
@@ -197,14 +220,15 @@
         return jnp.where(lane == 2 * pair + 1, total[rows:], masses)
 
     masses = lax.fori_loop(0, heads // 2, attend, jnp.zeros((rows, LANES), F32))
-    high = masses.astype(BF).astype(F32)
-    middle = (masses - high).astype(BF).astype(F32)
-    low = (masses - high - middle).astype(BF).astype(F32)
-    ext[:, width:] = (high + pltpu.roll(middle, 32, 1) + pltpu.roll(low, 64, 1)).astype(BF)
-
-
-def route_body(experts, ids, w_out, tokens, ext, gains, router, chosen, slots, after, gate, send):
+    ext[:, width:] = spread_parts(masses)
+    xn_copy.wait()
+    joined_copy.wait()
+
+
+def route_body(sizes, ids, w_rows, tokens, ext, gains, router, chosen, slots, after, gate, send, w_out):
+    experts, shards = sizes
     rows, width = tokens.shape
+    place_order(w_rows, w_out, ids[1], shards)
     lane = lax.broadcasted_iota(jnp.int32, (rows, LANES), 1)
     post = tokens[...].astype(F32) + dot(ext[:, :width], w_out[...])
     after[...] = post
@@ -225,14 +249,14 @@
     return (column == row // capacity * block + which * capacity + row % capacity).astype(BF)
 
 
-def upstream_body(sizes, ids, chunks, w_down, up_ref, spread_ref):
+def upstream_body(sizes, chunks, w_down, up_ref, spread_ref):
     shards, per_device, capacity = sizes
     total = chunks.shape[0] // shards
     count = total // per_device
     pick = slot_pick(count, total, capacity, pl.program_id(0))
-    for step in range(shards):
-        start = pl.multiple_of((ids[1] ^ step) * total, total)
-        up_ref[0, step * count : (step + 1) * count, :] = dot(pick, chunks[pl.ds(start, total), :]).astype(BF)
+    for index, mask in enumerate(doubling_order(shards)):
+        chunk = chunks[index * total : (index + 1) * total, :]
+        up_ref[0, mask * count : (mask + 1) * count, :] = dot(pick, chunk).astype(BF)
     spread_ref[0] = dot(up_ref[0], w_down[0])
 
 
@@ -279,35 +303,51 @@
         back_ref[...] = (back_ref[...].astype(F32) + back.astype(F32)).astype(BF)
 
 
-def expert_weights_body(sizes, ids, *refs):
+def expert_out_body(sizes, *refs):
     shards, per_device, capacity = sizes
     refs = list(refs)
-    x, up, hidden, pre, logit = [
-        jnp.concatenate([refs.pop(0)[0] for _ in range(shards)], axis=0) for _ in range(5)
+    x, hidden, logit = [
+        jnp.concatenate([refs.pop(0)[0] for _ in range(shards)], axis=0) for _ in range(3)
     ]
-    w_down, out_ref, up_grad, down_grad, router_part = refs
+    w_down = refs.pop(0)
+    out_refs, router_part = refs[:-1], refs[-1]
     which = pl.program_id(0)
-    down_grad[0] = dot(up, hidden, TN)
-    up_grad[0] = dot(x, pre, TN)
     router_add = dot_two(logit, x, TN)
     out = dot(hidden, w_down[0], NT).astype(BF)
     count = out.shape[0] // shards
+    pick = slot_pick(count, count * per_device, capacity, which)
     total = count * per_device
-    pick = slot_pick(count, total, capacity, which)
-    parts = [dot(pick, out[m * count : (m + 1) * count], TN).astype(BF) for m in range(shards)]
-    places = [pl.ds(pl.multiple_of((ids[1] ^ m) * total, total), total) for m in range(shards)]
+    half = shards // 2
+    parts = [
+        (
+            out_refs[index // half],
+            slice(index % half * total, (index % half + 1) * total),
+            dot(pick, out[mask * count : (mask + 1) * count], TN).astype(BF),
+        )
+        for index, mask in enumerate(doubling_order(shards))
+    ]
 
     @pl.when(which == 0)
     def _():
         router_part[...] = router_add
-        for place, part in zip(places, parts):
-            out_ref[place, :] = part
+        for ref, place, part in parts:
+            ref[place, :] = part
 
     @pl.when(which > 0)
     def _():
         router_part[...] = router_part[...] + router_add
-        for place, part in zip(places, parts):
-            out_ref[place, :] = (out_ref[place, :].astype(F32) + part.astype(F32)).astype(BF)
+        for ref, place, part in parts:
+            ref[place, :] = (ref[place, :].astype(F32) + part.astype(F32)).astype(BF)
+
+
+def expert_weights_body(shards, *refs):
+    refs = list(refs)
+    x, up, hidden, pre = [
+        jnp.concatenate([refs.pop(0)[0] for _ in range(shards)], axis=0) for _ in range(4)
+    ]
+    up_grad, down_grad = refs
+    down_grad[0] = dot(up, hidden, TN)
+    up_grad[0] = dot(x, pre, TN)
 
 
 def norm_back(values, gain, grad):
@@ -318,13 +358,19 @@
     return scale * (inner - unit * jnp.mean(inner * unit, axis=1, keepdims=True)), gain_grad
 
 
-def residual_body(ids, returned, back_slots, after, upstream, gains, resid, resid_low, gain_part):
+def residual_body(sizes, ids, returned, back_slots, after, upstream, gains, ext, w_out, resid, resid_low, grad_ext, gain_part):
+    heads, head_dim = sizes
+    rows, width = after.shape
     grad = dot(back_slots[...], returned[...])
     value, part = norm_back(after[...], gains[1:2, :], grad)
     value = value + upstream[...].astype(F32)
     resid[...] = value
     resid_low[...] = value.astype(BF)
     gain_part[...] = part
+    low = dot(value.astype(BF), w_out[...], NT).astype(BF)
+    grad_ext[:, :width] = low
+    product = low.astype(F32) * ext[:, :width].astype(F32)
+    grad_ext[:, width:] = spread_parts(dot_two(product, member_rows(LANES, width, head_dim), NT))
 
 
 def result_body(ids, returned, back_slots, after, gate, result):
@@ -343,6 +389,13 @@
     return total
 
 
+def spread_parts(values):
+    high = values.astype(BF).astype(F32)
+    middle = (values - high).astype(BF).astype(F32)
+    low = (values - high - middle).astype(BF).astype(F32)
+    return (high + pltpu.roll(middle, 32, 1) + pltpu.roll(low, 64, 1)).astype(BF)
+
+
 def member_rows(head_rows, width, head_dim):
     head_of = lax.broadcasted_iota(jnp.int32, (head_rows, width), 1) // head_dim
     return (head_of == lax.broadcasted_iota(jnp.int32, (head_rows, width), 0)).astype(BF)
@@ -353,19 +406,17 @@
     return (part_of == lax.broadcasted_iota(jnp.int32, (head_rows, LANES), 0)).astype(BF)
 
 
-def query_body(sizes, ids, resid_low, ext, joined_own, w_out, window, window_ref, keys_in, values_in, query_grad, table_part, grads, delta, mass, diagonals):
+def query_body(sizes, ids, grad_ext, ext, joined_own, window, window_ref, keys_in, values_in, query_grad, table_part, delta, mass, diagonals):
     head_dim, buckets = sizes
     pair = pl.program_id(0)
-    rows, width = resid_low.shape
+    rows = ext.shape[0]
+    width = ext.shape[1] - LANES
     keys = keys_in.shape[0]
     head_rows, span = window.shape
 
     @pl.when(pair == 0)
     def _():
-        low = dot(resid_low[...], w_out[...], NT).astype(BF)
-        grads[...] = low
-        product = low.astype(F32) * ext[:, :width].astype(F32)
-        delta[...] = dot_two(product, member_rows(head_rows, width, head_dim), NT)
+        delta[...] = dot(grad_ext[:, width:], part_rows(head_rows), NT)
         mass[...] = dot(ext[:, width:], part_rows(head_rows), NT)
 
     head_lane = lax.broadcasted_iota(jnp.int32, (rows, head_rows), 1)
@@ -381,7 +432,7 @@
 
     column = pl.multiple_of(pair * LANES, LANES)
     queries = pair_rows(joined_own[:, pl.ds(column, LANES)], head_dim)
-    grad_own = pair_rows(grads[:, pl.ds(column, LANES)], head_dim)
+    grad_own = pair_rows(grad_ext[:, pl.ds(column, LANES)], head_dim)
     scores = dot(queries, keys_in[...], NT) + jnp.concatenate(
         [bias_rows(window, 2 * pair + k, rows, keys) for k in range(2)], axis=0
     )
@@ -414,32 +465,27 @@
     devices, heads, head_dim = sizes
     refs = list(refs)
     ids = refs.pop(0)
-    resid_pieces = [refs.pop(0) for _ in range(devices)]
-    ext_all, joined_own, w_out, mirror, query_grad, queries_in = [refs.pop(0) for _ in range(6)]
+    grad_pieces = [refs.pop(0) for _ in range(devices)]
+    ext_pieces = [refs.pop(0) for _ in range(devices)]
+    joined_own, mirror, query_grad, resid_low, queries_in = [refs.pop(0) for _ in range(5)]
     blocks, grads, delta_rows, mass_rows = refs
     expert_id = ids[0]
     pair = pl.program_id(0)
-    rows, width = resid_pieces[0].shape
+    rows, width = resid_low.shape
     keys = rows * devices
     head_rows = mirror.shape[0]
     pairs = heads // 2
 
     @pl.when(pair == 0)
     def _():
-        place_blocks(resid_pieces, grads, expert_id)
-        mass_rows[...] = dot(part_rows(head_rows), ext_all[:, width:], NT)
-        member = member_rows(head_rows, width, head_dim)
-        step = min(1024, keys)
-        for start in range(0, keys, step):
-            low = dot(grads[start : start + step, :], w_out[...], NT).astype(BF)
-            grads[start : start + step, :] = low
-            product = low.astype(F32) * ext_all[start : start + step, :width].astype(F32)
-            high = product.astype(BF)
-            rest = (product - high.astype(F32)).astype(BF)
-            delta_rows[:, start : start + step] = dot(member, high, NT) + dot(member, rest, NT)
+        place_blocks(grad_pieces, grads, expert_id)
+        delta_rows[...] = dot(part_rows(head_rows), grads[:, width:], NT)
+        for mask, piece in enumerate(ext_pieces):
+            start = pl.multiple_of((expert_id ^ mask) * rows, rows)
+            mass_rows[:, pl.ds(start, rows)] = dot(part_rows(head_rows), piece[:, width:], NT)
         blocks[:pairs] = query_grad[...]
         for block in range(pairs):
-            blocks[3 * pairs + block] = resid_pieces[0][:, block * LANES : (block + 1) * LANES]
+            blocks[3 * pairs + block] = resid_low[:, block * LANES : (block + 1) * LANES]
         for block in range(4 * pairs, blocks.shape[0]):
             blocks[block] = jnp.zeros((rows, LANES), BF)
 
@@ -462,7 +508,11 @@
     blocks[2 * pairs + pair] = pair_join(dot(probs.astype(BF), grad_all), rows, head_dim).astype(BF)
 
 
-def source_body(ids, blocks, w_in, tokens, gains, resid, tokens_grad, gain_part, joined):
+def source_body(shards, ids, *refs):
+    refs = list(refs)
+    tokens_grad, gain_part, joined, w_in, small = refs[-5:]
+    blocks, tokens, gains, resid = refs[:4]
+    place_weight(refs[4:-5], w_in, small, ids[0], ids[1], shards)
     for block in range(joined.shape[1] // LANES):
         joined[:, block * LANES : (block + 1) * LANES] = blocks[block]
     grad = dot(joined[...], w_in[...], NT)
@@ -471,9 +521,10 @@
     gain_part[...] = part
 
 
-def weight_body(sizes, ids, xn_all, ext_all, received, lines, part, columns):
+def weight_body(sizes, ids, xn_all, received, lines, *refs):
     per, pairs, shards = sizes
     devices, _, rows, _ = received.shape
+    ext_pieces, parts, columns, mixed_all = refs[:devices], refs[devices:-2], refs[-2], refs[-1]
     width = xn_all.shape[1]
     rows_each = width // shards
     for source in range(devices):
@@ -484,7 +535,13 @@
 
     def store(value, line):
         for owner in range(shards):
-            part[owner, :rows_each, line] = value[owner * rows_each : (owner + 1) * rows_each].astype(BF)
+            for mask in range(shards):
+
+                @pl.when(ids[1] ^ mask == owner)
+                def _():
+                    parts[mask][:rows_each, line] = value[
+                        owner * rows_each : (owner + 1) * rows_each
+                    ].astype(BF)
 
     step = per if 3 * pairs % per == 0 else 1
     for block in range(0, per, step):
@@ -497,9 +554,13 @@
 
         @pl.when(jnp.logical_not(inside))
         def _():
-            store(dot(ext_all[:, :width], columns[:, line], TN), line)
-
-    part[:, rows_each:, :] = lines[...]
+            for mask, piece in enumerate(ext_pieces):
+                start = pl.multiple_of((ids[0] ^ mask) * rows, rows)
+                mixed_all[pl.ds(start, rows), :] = piece[:, :width]
+            store(dot(mixed_all[...], columns[:, line], TN), line)
+
+    for mask in range(shards):
+        parts[mask][rows_each:, :] = lines[ids[1] ^ mask]
 
 
 def spread_body(sizes, ids, *refs):
@@ -582,13 +643,6 @@
 
     block = per_device * capacity
 
-    def scatter_rows(parts):
-        mine = lax.dynamic_index_in_dim(parts, shard_id, 0, keepdims=False).astype(F32)
-        for mask in range(1, shards):
-            sent = lax.dynamic_index_in_dim(parts, shard_id ^ mask, 0, keepdims=False)
-            mine = mine + swap(sent, "wshard", mask).astype(F32)
-        return mine
-
     def exchange(slot_rows):
         blocks = slot_rows.reshape(devices, block, width)
         moved = lax.all_to_all(blocks, "expert", split_axis=0, concat_axis=0, tiled=True)
@@ -607,14 +661,29 @@
     if len(in_chunks) > 1:
         in_pieces = chip_pieces(jnp.concatenate(in_chunks, axis=0))
     token_pieces = core_pieces(chip_tokens)
-    w_out = lax.all_gather(attn_out, "wshard", axis=0, tiled=True)
-    in_pieces, token_pieces, ups = tie(in_pieces, token_pieces, exchange(ups))
+    first_step, *later_steps = doubling_steps(shards)
+    w_rows = swap(attn_out, "wshard", first_step)
+    in_pieces, token_pieces, w_rows, ups, ids, window_buckets, mirror_buckets, chosen, slots, back_slots = tie(
+        in_pieces,
+        token_pieces,
+        w_rows,
+        exchange(ups),
+        ids,
+        window_buckets,
+        mirror_buckets,
+        chosen,
+        slots,
+        back_slots,
+    )
+    w_rows = jnp.concatenate([attn_out, w_rows], axis=0)
+    for step in later_steps:
+        w_rows = jnp.concatenate([w_rows, swap(w_rows, "wshard", step)], axis=0)
+    ups_far = swap(ups, "wshard", first_step)
     if len(in_pieces) > 1:
         in_pieces = core_pieces(in_pieces)
-    ups_all = lax.all_gather(ups, "wshard", axis=0, tiled=True)
 
     sizes = (devices, shards, heads, head_dim, bucket_count, experts, len(in_pieces))
-    xn_all, joined, joined_own, ext, w_in, window, mirror, gains, router_pad = call(
+    xn_all, joined, joined_own, ext, window, mirror, gains, router_pad = call(
         functools.partial(forward_body, sizes),
         [ids, *token_pieces, *in_pieces, window_buckets, mirror_buckets],
         [
@@ -622,19 +691,29 @@
             ((keys, 3 * width), BF),
             ((rows, 3 * width), BF),
             ((rows, width + LANES), BF),
-            ((width, 3 * width), BF),
             ((head_rows, window_width), F32),
             ((head_rows, window_width), F32),
             ((8, width), F32),
             ((width, LANES), BF),
         ],
+        [
+            pltpu.VMEM((keys, width), BF),
+            pltpu.VMEM((keys, 3 * width), BF),
+            pltpu.VMEM((width, 3 * width), BF),
+            pltpu.SemaphoreType.DMA((2,)),
+        ],
+        far=(0, 1),
         name="attention_forward",
         us=0.2,
     )
-    after, gate, send = call(
-        functools.partial(route_body, experts),
-        [ids, w_out, own_tokens, ext, gains, router_pad, chosen, slots],
-        [((rows, width), F32), ((rows, LANES), F32), ((slot_count, width), BF)],
+    ups_far, w_rows, ext = tie(ups_far, w_rows, ext)
+    ups_all = jnp.concatenate([ups, ups_far], axis=0)
+    for step in later_steps:
+        ups_all = jnp.concatenate([ups_all, swap(ups_all, "wshard", step)], axis=0)
+    after, gate, send, w_out = call(
+        functools.partial(route_body, (experts, shards)),
+        [ids, w_rows, own_tokens, ext, gains, router_pad, chosen, slots],
+        [((rows, width), F32), ((rows, LANES), F32), ((slot_count, width), BF), ((width, width), BF)],
         name="route",
         us=0.2,
     )
@@ -648,25 +727,25 @@
     kept_lanes = pl.BlockSpec((1, count, LANES), lambda k: (k, 0, 0))
     upstream_width = pl.BlockSpec((1, shards * count, width), lambda k: (k, 0, 0))
     upstream_ff = pl.BlockSpec((1, shards * count, ff), lambda k: (k, 0, 0))
+    ups_all, rows_own = tie(ups_all, rows_own)
+    row_chunks = {0: rows_own}
+    steps = [1 << bit for bit in reversed(range((shards - 1).bit_length()))]
+    row_chunks.update({step: swap(rows_own, "wshard", step) for step in steps})
     ups_all, spread_all = pl.pallas_call(
         functools.partial(upstream_body, (shards, per_device, capacity)),
         grid=(per_device,),
-        in_specs=[pl.BlockSpec(memory_space=pltpu.SMEM), whole((shards * total, width)), by_expert],
+        in_specs=[whole((shards * total, width)), by_expert],
         out_specs=[upstream_width, upstream_ff],
         out_shape=[
             jax.ShapeDtypeStruct((per_device, shards * count, width), BF),
             jax.ShapeDtypeStruct((per_device, shards * count, ff), F32),
         ],
         compiler_params=pltpu.CompilerParams(vmem_limit_bytes=VMEM_BYTES),
-        cost_estimate=cost(5.0),
+        cost_estimate=cost(0.001),
         name="upstream",
-    )(ids, ups_all, expert_down)
-    rows_own, ups_all, spread_all = tie(rows_own, ups_all, spread_all)
-    row_chunks = {0: rows_own}
-    steps = [1 << bit for bit in reversed(range((shards - 1).bit_length()))]
-    row_chunks.update({step: swap(rows_own, "wshard", step) for step in steps})
+    )(ups_all, expert_down)
     ext_later, _ = tie(ext, rows_own)
-    ext_all = lax.all_gather(ext_later, "expert", axis=0, tiled=True)
+    ext_pieces = core_pieces(chip_pieces(ext_later))
     kept = [[], [], [], [], []]
     back_parts = []
     for step in range(shards):
@@ -694,7 +773,7 @@
                 jax.ShapeDtypeStruct((per_device, count, LANES), F32),
             ],
             compiler_params=pltpu.CompilerParams(vmem_limit_bytes=VMEM_BYTES),
-            cost_estimate=cost(0.5),
+            cost_estimate=cost(0.001),
             name="experts",
         )(ids, row_chunk, ups_all, spread_all, expert_in, router_pad)
         back_parts.append(back)
@@ -708,36 +787,27 @@
                     row_chunks[mask] = swap(value, "wshard", nearer)
     kept, back_sum = tie(kept, sum_back(back_parts))
     returned_grad = exchange(back_sum)
-    out_parts, up_grad, down_grad, router_part = pl.pallas_call(
-        functools.partial(expert_weights_body, (shards, per_device, capacity)),
+    out_near, out_far, router_part = pl.pallas_call(
+        functools.partial(expert_out_body, (shards, per_device, capacity)),
         grid=(per_device,),
-        in_specs=[pl.BlockSpec(memory_space=pltpu.SMEM)]
-        + [kept_width] * (2 * shards)
-        + [kept_ff] * (2 * shards)
-        + [kept_lanes] * shards
-        + [by_expert],
-        out_specs=[whole((shards * total, width)), by_expert, by_expert, whole((LANES, width))],
-        out_shape=[
-            jax.ShapeDtypeStruct((shards * total, width), BF),
-            jax.ShapeDtypeStruct((per_device, width, ff), F32),
-            jax.ShapeDtypeStruct((per_device, width, ff), F32),
-            jax.ShapeDtypeStruct((LANES, width), F32),
-        ],
+        in_specs=[kept_width] * shards + [kept_ff] * shards + [kept_lanes] * shards + [by_expert],
+        out_specs=[whole((shards // 2 * total, width))] * 2 + [whole((LANES, width))],
+        out_shape=[jax.ShapeDtypeStruct((shards // 2 * total, width), BF)] * 2
+        + [jax.ShapeDtypeStruct((LANES, width), F32)],
         compiler_params=pltpu.CompilerParams(vmem_limit_bytes=VMEM_BYTES),
-        cost_estimate=cost(8.0),
-        name="expert_weights",
-    )(ids, *[value for group in kept for value in group], expert_down)
-    out_parts, router_part, returned_grad = tie(out_parts, router_part, returned_grad)
-    resid, resid_low, gain_two_part = call(
-        residual_body,
-        [ids, returned_grad, back_slots, after, own_grad, gains],
-        [((rows, width), F32), ((rows, width), BF), ((1, width), F32)],
+        cost_estimate=cost(5.0),
+        name="expert_out",
+    )(*kept[0], *kept[2], *kept[4], expert_down)
+    out_near, out_far, router_part, returned_grad = tie(out_near, out_far, router_part, returned_grad)
+    out_sum = (out_near.astype(F32) + swap(out_far, "wshard", 1).astype(F32)).astype(BF)
+    resid, resid_low, grad_ext, gain_two_part = call(
+        functools.partial(residual_body, (heads, head_dim)),
+        [ids, returned_grad, back_slots, after, own_grad, gains, ext, w_out],
+        [((rows, width), F32), ((rows, width), BF), ((rows, width + LANES), BF), ((1, width), F32)],
         name="residual",
         us=2.0,
     )
-    out_parts, _ = tie(out_parts, resid_low)
-    out_sum = lax.psum_scatter(out_parts, "wshard", scatter_dimension=0, tiled=True)
-    resid_pieces = chip_pieces(resid_low)
+    grad_pieces = chip_pieces(grad_ext)
     pairs = heads // 2
 
     def column_block(offset):
@@ -748,10 +818,9 @@
         grid=(pairs,),
         in_specs=[
             pl.BlockSpec(memory_space=pltpu.SMEM),
-            whole((rows, width)),
+            whole((rows, width + LANES)),
             whole((rows, width + LANES)),
             whole((rows, 3 * width)),
-            whole((width, width)),
             whole((head_rows, window_width)),
             whole((1, window_width)),
             column_block(1),
@@ -763,7 +832,6 @@
             jax.ShapeDtypeStruct((head_rows, bucket_count), F32),
         ],
         scratch_shapes=[
-            pltpu.VMEM((rows, width), BF),
             pltpu.VMEM((rows, head_rows), F32),
             pltpu.VMEM((rows, head_rows), F32),
             pltpu.VMEM((head_rows * 8, window_width), F32),
@@ -771,21 +839,20 @@
         compiler_params=pltpu.CompilerParams(vmem_limit_bytes=VMEM_BYTES),
         cost_estimate=cost(10.0),
         name="query_grad",
-    )(ids, resid_low, ext, joined_own, w_out, window, window_buckets, joined, joined)
+    )(ids, grad_ext, ext, joined_own, window, window_buckets, joined, joined)
     per = -(-4 * pairs // devices)
-    resid_pieces, query_grad = tie(resid_pieces, query_grad)
-    resid_pieces = core_pieces(resid_pieces)
+    grad_pieces, query_grad = tie(grad_pieces, query_grad)
+    grad_pieces = core_pieces(grad_pieces)
     (blocks,) = pl.pallas_call(
         functools.partial(key_body, (devices, heads, head_dim)),
         grid=(pairs,),
         in_specs=[pl.BlockSpec(memory_space=pltpu.SMEM)]
-        + [whole((rows, width))] * devices
+        + [whole((rows, width + LANES))] * (2 * devices)
         + [
-            whole((keys, width + LANES)),
             whole((rows, 3 * width)),
-            whole((width, width)),
             whole((head_rows, window_width)),
             whole((pairs, rows, LANES)),
+            whole((rows, width)),
             column_block(0),
         ],
         out_specs=[whole((per * devices, rows, LANES))],
@@ -793,23 +860,30 @@
             jax.ShapeDtypeStruct((per * devices, rows, LANES), BF),
         ],
         scratch_shapes=[
-            pltpu.VMEM((keys, width), BF),
+            pltpu.VMEM((keys, width + LANES), BF),
             pltpu.VMEM((head_rows, keys), F32),
             pltpu.VMEM((head_rows, keys), F32),
         ],
         compiler_params=pltpu.CompilerParams(vmem_limit_bytes=VMEM_BYTES),
         cost_estimate=cost(12.0),
         name="key_grad",
-    )(ids, *resid_pieces, ext_all, joined_own, w_out, mirror, query_grad, joined)
-    blocks, out_sum = tie(blocks, out_sum)
+    )(ids, *grad_pieces, *ext_pieces, joined_own, mirror, query_grad, resid_low, joined)
+    for step in reversed(doubling_steps(shards)[:-1]):
+        half = out_sum.shape[0] // 2
+        moved = swap(out_sum[half:], "wshard", step)
+        out_sum = (out_sum[:half].astype(F32) + moved.astype(F32)).astype(BF)
     received = lax.all_to_all(
         blocks.reshape(devices, per, rows, LANES), "expert", split_axis=0, concat_axis=0, tiled=True
     )
     tokens_grad, gain_one_part = call(
-        source_body,
-        [ids, blocks, w_in, own_tokens, gains, resid],
+        functools.partial(source_body, shards),
+        [ids, blocks, own_tokens, gains, resid, *in_pieces],
         [((rows, width), BF), ((1, width), F32)],
-        [pltpu.VMEM((rows, 3 * width), BF)],
+        [
+            pltpu.VMEM((rows, 3 * width), BF),
+            pltpu.VMEM((width, 3 * width), BF),
+            pltpu.VMEM((width, LANES), BF),
+        ],
         name="source_grad",
         us=4.0,
     )
@@ -822,18 +896,28 @@
     lines = pad_to(lines, (groups * line_rows, width)).reshape(groups, line_rows, shards, part)
     lines = lines.transpose(2, 1, 0, 3).reshape(shards, line_rows, groups * part)
     lines = pad_to(lines, (shards, line_rows, per * LANES)).astype(BF)
-    (weight_part,) = call(
+    weight_parts = call(
         functools.partial(weight_body, (per, pairs, shards)),
-        [ids, xn_all, ext_all, received, lines],
-        [((shards, part + line_rows, per * LANES), BF)],
-        [pltpu.VMEM((keys, per * LANES), BF)],
+        [ids, xn_all, received, lines, *ext_pieces],
+        [((part + line_rows, per * LANES), BF)] * shards,
+        [pltpu.VMEM((keys, per * LANES), BF), pltpu.VMEM((keys, width), BF)],
         name="weight_grads",
         us=4.0,
     )
-    weight_part, out_sum = tie(weight_part, out_sum)
-    mine = scatter_rows(weight_part).astype(BF)
+    weight_parts, out_sum, kept = tie(weight_parts, out_sum, kept)
+    up_grad, down_grad = pl.pallas_call(
+        functools.partial(expert_weights_body, shards),
+        grid=(per_device,),
+        in_specs=[kept_width] * (2 * shards) + [kept_ff] * (2 * shards),
+        out_specs=[by_expert, by_expert],
+        out_shape=[jax.ShapeDtypeStruct((per_device, width, ff), F32)] * 2,
+        compiler_params=pltpu.CompilerParams(vmem_limit_bytes=VMEM_BYTES),
+        cost_estimate=cost(7.0),
+        name="expert_weights",
+    )(*kept[0], *kept[1], *kept[2], *kept[3])
+    mine = sum_back(weight_parts)
     returned_rows = exchange(out_sum)
-    mine, returned_rows = tie(mine, returned_rows)
+    mine, returned_rows, up_grad, down_grad = tie(mine, returned_rows, up_grad, down_grad)
     pieces = chip_pieces(mine)
     (result,) = call(
         result_body,

time: 264 us -> 257 us (0.973)
  starting transfers between devices: 56.9 us -> 71.2 us
  between operations: 14.4 us -> 1.34 us
  waiting for transfers between devices: 63.4 us -> 57.8 us
  Pallas kernels: 100 us -> 96.6 us
    ppermute x40 -> x53, starting transfers between devices: 38.9 us -> 52.9 us  [swap(): return lax.ppermute(x, axis, [(i, i ^ mask) for i in range(count)])]
    ppermute x40 -> x53, waiting for transfers between devices: 35.2 us -> 46.4 us  [swap(): return lax.ppermute(x, axis, [(i, i ^ mask) for i in range(count)])]
    all_to_all x1, waiting for transfers between devices: 5.34 us -> 0.01 us  [local(): lax.all_to_all(blocks.reshape(devices, per, rows, LANES), 'expert', split...]
    all_to_all x4, waiting for transfers between devices: 16.7 us -> 11.4 us  [exchange(): lax.all_to_all(blocks, 'expert', split_axis=0, concat_axis=0, tiled=True)]
    all_gather x3 -> x0, waiting for transfers between devices: 3.75 us -> none  [the longest x1 3.73 us: local(): ups_all = lax.all_gather(ups, 'wshard', axis=0, tiled=True)]
    pallas_call x1, Pallas kernels: 12.6 us -> 9.26 us  [local(): pl.pallas_call(functools.partial(key_body, (devices, heads, head_dim)), g...]
    pallas_call x8 -> x9, Pallas kernels: 49 us -> 49.8 us  [the longest x7 37.1 us: call(): pl.pallas_call(body, in_specs=[ids] + [near] * (len(args) - 1), out_specs...]
    unnamed x92 -> x98, local copies, waits for them, and re-layouts: 8.24 us -> 8.29 us
  transfers between devices with their start and end apart: 49 -> 58, of which waited for: 21 -> 24; matrix products, arithmetic and copies ran while one was open for 5% -> 6% of each run, Pallas kernels for 35% -> 35%
where the time goes in v3:
time: 257 us; the launch traced here: 256 us
  Pallas kernels  96.6 us (38%)
  starting transfers between devices  71.2 us (28%)
  waiting for transfers between devices  57.8 us (22%)
  local copies, waits for them, and re-layouts  17.4 us (7%)
  other arithmetic  9.98 us (4%)
    ppermute x53, starting transfers between devices, swap(): return lax.ppermute(x, axis, [(i, i ^ mask) for i in range(count)])  52.9 us
    ppermute x53, waiting for transfers between devices, swap(): return lax.ppermute(x, axis, [(i, i ^ mask) for i in range(count)])  46.4 us
    pallas_call x7, Pallas kernels, call(): pl.pallas_call(body, in_specs=[ids] + [near] * (len(args) - 1), out_specs...  37.1 us
    pallas_call x4, Pallas kernels, local(): pl.pallas_call(functools.partial(expert_body, (experts, per_device, capac...  23 us
    all_to_all x4, starting transfers between devices, exchange(): lax.all_to_all(blocks, 'expert', split_axis=0, concat_axis=0, tiled=True)  14.6 us
    all_to_all x4, waiting for transfers between devices, exchange(): lax.all_to_all(blocks, 'expert', split_axis=0, concat_axis=0, tiled=True)  11.4 us
    pallas_call x1, Pallas kernels, local(): pl.pallas_call(functools.partial(query_body, (head_dim, bucket_count)), g...  10.3 us
    pallas_call x1, Pallas kernels, local(): pl.pallas_call(functools.partial(key_body, (devices, heads, head_dim)), g...  9.26 us
  transfers between devices with their start and end apart: 58, of which 24 were waited for; matrix products, arithmetic and copies ran while one was open for 6% of the time, Pallas kernels for 35%

profile of v3, /device:TPU:0, one launch (start us, length us, event | category | flops | bytes accessed | tf_op | source)
XLA Modules:
  0.0 256.1 jit_solution(374802331083232119)
XLA Ops:
  37.3 10.5 %all-to-all-done = bf16[8,24,768]{2,1,0:T(8,128)(2,1)S(1)} async-done(((bf16[8,24,768]{2,1,0:T(8,128)(2,1)}), bf16[8,24,768]{2,1,0:T(8,128)(2,1)S(1)}, u32[]{:S(2)}, u32[]{:S(2)}) %all-to-all-start) | async-done | bytes 294944 | tf_op jit(solution)/shard_map/all_to_all | solution.py:648
  55.1 15.8 %attention_forward.1 = (bf16[1024,768]{1,0:T(8,128)(2,1)}, bf16[1024,2304]{1,0:T(8,128)(2,1)}, bf16[128,2304]{1,0:T(8,128)(2,1)}, bf16[128,896]{1,0:T(8,128)(2,1...) custom-call(s32[2]{0:T(128)} %pad_add_fusion.refs_0_.ids, ...), custom_call_target="tpu_custom_call" | custom-call | flops 200000000 | bytes 200000 | tf_op jit(solution)/shard_map/attention_forward/pallas_call | solution.py:139
  76.1 3.9 %all-to-all-start.1 = ((bf16[8,24,768]{2,1,0:T(8,128)(2,1)}), bf16[8,24,768]{2,1,0:T(8,128)(2,1)S(1)}, u32[]{:S(2)}, u32[]{:S(2)}) async-start(bf16[8,24,768]{2,1,0:T(8,128)(2,1)} %bitcast.58), calls=%async_computation.1 | async-start | bytes 589824 | tf_op jit(solution)/shard_map/all_to_all | solution.py:648
  79.9 7.5 %collective-permute-done.20 = bf16[384,768]{1,0:T(8,128)(2,1)S(1)} collective-permute-done((bf16[384,768]{1,0:T(8,128)(2,1)S(1)}, bf16[384,768]{1,0:T(8,128)(2,1)S(1)}, u32[]{:S(2)}, u32[]{:S(2)}) %collective-permute-start.20) | collective-permute-done | bytes 589856 | tf_op jit(solution)/shard_map/ppermute | solution.py:32
  91.3 4.3 %upstream.1 = (bf16[2,384,768]{2,1,0:T(8,128)(2,1)}, f32[2,384,768]{2,1,0:T(8,128)}) custom-call(bf16[768,768]{1,0:T(8,128)(2,1)} %pad_maximum_fusion.1.chunks, bf16[2,768,768]{2,1,0:T(8,128)(2,1)} %refs_12_.1), custom_call_target="tpu_custom_call" | custom-call | flops 1000000 | bytes 1000 | tf_op jit(solution)/shard_map/upstream/pallas_call | solution.py:734
  95.6 5.7 %experts.4 = (bf16[192,768]{1,0:T(8,128)(2,1)}, bf16[2,96,768]{2,1,0:T(8,128)(2,1)}, bf16[2,96,768]{2,1,0:T(8,128)(2,1)}, bf16[2,96,768]{2,1,0:T(8,128)(2,1)}, b...) custom-call(s32[2]{0:T(128)} %pad_add_fusion.refs_0_.ids, bf16[192,768]{1,0:T(8,128)(2,1)} %bitcast.47, ...), custom_call_target="tpu_custom_call" | custom-call | flops 1000000 | bytes 1000 | tf_op jit(solution)/shard_map/experts/pallas_call | solution.py:755
  103.7 5.7 %experts.5 = (bf16[192,768]{1,0:T(8,128)(2,1)}, bf16[2,96,768]{2,1,0:T(8,128)(2,1)}, bf16[2,96,768]{2,1,0:T(8,128)(2,1)}, bf16[2,96,768]{2,1,0:T(8,128)(2,1)}, b...) custom-call(s32[2]{0:T(128)} %pad_add_fusion.refs_0_.ids, bf16[192,768]{1,0:T(8,128)(2,1)} %copy-done.14, ...), custom_call_target="tpu_custom_call" | custom-call | flops 1000000 | bytes 1000 | tf_op jit(solution)/shard_map/experts/pallas_call | solution.py:755
  111.6 5.8 %experts.6 = (bf16[192,768]{1,0:T(8,128)(2,1)}, bf16[2,96,768]{2,1,0:T(8,128)(2,1)}, bf16[2,96,768]{2,1,0:T(8,128)(2,1)}, bf16[2,96,768]{2,1,0:T(8,128)(2,1)}, b...) custom-call(s32[2]{0:T(128)} %pad_add_fusion.refs_0_.ids, bf16[192,768]{1,0:T(8,128)(2,1)} %copy-done.12, ...), custom_call_target="tpu_custom_call" | custom-call | flops 1000000 | bytes 1000 | tf_op jit(solution)/shard_map/experts/pallas_call | solution.py:755
  117.4 3.5 %collective-permute-done.23.rows_in = bf16[192,768]{1,0:T(8,128)(2,1)S(1)} collective-permute-done((bf16[192,768]{1,0:T(8,128)(2,1)S(1)}, bf16[192,768]{1,0:T(8,128)(2,1)S(1)}, u32[]{:S(2)}, u32[]{:S(2)}) %collective-permute-start.23) | collective-permute-done | bytes 294944 | tf_op jit(solution)/shard_map/ppermute | solution.py:32
  121.6 5.7 %experts.7 = (bf16[192,768]{1,0:T(8,128)(2,1)}, bf16[2,96,768]{2,1,0:T(8,128)(2,1)}, bf16[2,96,768]{2,1,0:T(8,128)(2,1)}, bf16[2,96,768]{2,1,0:T(8,128)(2,1)}, b...) custom-call(s32[2]{0:T(128)} %pad_add_fusion.refs_0_.ids, bf16[192,768]{1,0:T(8,128)(2,1)} %copy-done.13, ...), custom_call_target="tpu_custom_call" | custom-call | flops 1000000 | bytes 1000 | tf_op jit(solution)/shard_map/experts/pallas_call | solution.py:755
  133.8 6.3 %collective-permute-done.25 = bf16[192,768]{1,0:T(8,128)(2,1)S(1)} collective-permute-done((bf16[192,768]{1,0:T(8,128)(2,1)}, bf16[192,768]{1,0:T(8,128)(2,1)S(1)}, u32[]{:S(2)}, u32[]{:S(2)}) %collective-permute-start.25) | collective-permute-done | bytes 294944 | tf_op jit(solution)/shard_map/ppermute | solution.py:32
  143.5 3.6 %all-to-all-start.2 = ((bf16[8,24,768]{2,1,0:T(8,128)(2,1)}), bf16[8,24,768]{2,1,0:T(8,128)(2,1)S(1)}, u32[]{:S(2)}, u32[]{:S(2)}) async-start(bf16[8,24,768]{2,1,0:T(8,128)(2,1)} %bitcast.11), calls=%async_computation.2 | async-start | bytes 589824 | tf_op jit(solution)/shard_map/all_to_all | solution.py:648
  147.2 6.2 %expert_out.1 = (bf16[384,768]{1,0:T(8,128)(2,1)}, bf16[384,768]{1,0:T(8,128)(2,1)}, f32[128,768]{1,0:T(8,128)}) custom-call(bf16[2,96,768]{2,1,0:T(8,128)(2,1)} %get-tuple-element.292.refs_0_, bf16[2,96,768]{2,1,0:T(8,128)(2,1)} %get-tuple-element.293.refs_1_, bf16[2,96,768]{2,1,0:T(8,128)(2,1)} %get-tuple-element.294.refs_2_, ...), custom_call_target="tpu_custom_call" | custom-call | flops 5000000000 | bytes 5000000 | tf_op jit(solution)/shard_map/expert_out/pallas_call | solution.py:790
  154.9 3.6 %residual.1 = (f32[128,768]{1,0:T(8,128)}, bf16[128,768]{1,0:T(8,128)(2,1)}, bf16[128,896]{1,0:T(8,128)(2,1)}, f32[1,768]{1,0:T(1,128)}) custom-call(s32[2]{0:T(128)} %pad_add_fusion.refs_0_.ids, bf16[192,768]{1,0:T(8,128)(2,1)} %bitcast.57, bf16[128,192]{1,0:T(8,128)(2,1)} %fusion.back_slots, f32[128,768]{1,0:T(8,128)} %get-tuple-element.253.after, ...), custom_call_target="tpu_custom_call" | custom-call | flops 2000000000 | bytes 2000000 | tf_op jit(solution)/shard_map/residual/pallas_call | solution.py:139
  161.6 4.1 %collective-permute-done.27.refs_3_ = bf16[128,896]{1,0:T(8,128)(2,1)S(1)} collective-permute-done((bf16[128,896]{1,0:T(8,128)(2,1)}, bf16[128,896]{1,0:T(8,128)(2,1)S(1)}, u32[]{:S(2)}, u32[]{:S(2)}) %collective-permute-start.27) | collective-permute-done | bytes 229408 | tf_op jit(solution)/shard_map/ppermute | solution.py:32
  168.3 10.3 %query_grad.1 = (bf16[6,128,128]{2,1,0:T(8,128)(2,1)}, f32[16,32]{1,0:T(8,128)}) custom-call(s32[2]{0:T(128)} %pad_add_fusion.refs_0_.ids, bf16[128,896]{1,0:T(8,128)(2,1)} %get-tuple-element.260.grad_ext.refs_1_, bf16[128,896]{1,0:T(8,128)(2,1)} %get-tuple-element.264.ext.refs_9_.refs_0_, bf16[128,2304]{1,0:T(8,128)(2,1)} %get-tuple-element.256.joined_own.refs_17_, ...), custom_call_target="tpu_custom_call" | custom-call | flops 10000000000 | bytes 10000000 | tf_op jit(solution)/shard_map/query_grad/pallas_call | solution.py:816
  185.3 9.3 %key_grad.1.refs_0_ = bf16[24,128,128]{2,1,0:T(8,128)(2,1)} custom-call(s32[2]{0:T(128)} %pad_add_fusion.refs_0_.ids, bf16[128,896]{1,0:T(8,128)(2,1)} %get-tuple-element.260.grad_ext.refs_1_, bf16[128,896]{1,0:T(8,128)(2,1)} %collective-permute-done.30.refs_2_, bf16[128,896]{1,0:T(8,128)(2,1)} %copy-done.36, ...), custom_call_target="tpu_custom_call" | custom-call | flops 12000000000 | bytes 12000000 | tf_op jit(solution)/shard_map/key_grad/pallas_call | solution.py:846
  194.5 3.7 %all-to-all-start.3 = ((bf16[8,3,128,128]{3,2,1,0:T(8,128)(2,1)}), bf16[8,3,128,128]{3,2,1,0:T(8,128)(2,1)S(1)}, u32[]{:S(2)}, u32[]{:S(2)}) async-start(bf16[8,3,128,128]{3,2,1,0:T(8,128)(2,1)} %bitcast.55), calls=%async_computation.3 | async-start | bytes 1572864 | tf_op jit(solution)/shard_map/all_to_all | solution.py:875
  199.5 4.9 %source_grad.1 = (bf16[128,768]{1,0:T(8,128)(2,1)}, f32[1,768]{1,0:T(1,128)}) custom-call(s32[2]{0:T(128)} %pad_add_fusion.refs_0_.ids, bf16[24,128,128]{2,1,0:T(8,128)(2,1)} %key_grad.1.refs_0_, bf16[128,768]{1,0:T(8,128)(2,1)} %bitcast.52, f32[8,768]{1,0:T(8,128)} %get-tuple-element.199.gains.refs_2_, f32[128,768]{1,0:T(8,128)} %get-tuple-element.269.refs_3_, ...), custom_call_target="tpu_custom_call" | custom-call | flops 4000000000 | bytes 4000000 | tf_op jit(solution)/shard_map/source_grad/pallas_call | solution.py:139
  206.0 9.0 %collective-permute-done.42 = bf16[192,768]{1,0:T(8,128)(2,1)S(1)} collective-permute-done((bf16[192,768]{1,0:T(8,128)(2,1)S(1)}, bf16[192,768]{1,0:T(8,128)(2,1)S(1)}, u32[]{:S(2)}, u32[]{:S(2)}) %collective-permute-start.42) | collective-permute-done | bytes 294944 | tf_op jit(solution)/shard_map/ppermute | solution.py:32
  216.7 4.3 %weight_grads.1 = (bf16[208,384]{1,0:T(8,128)(2,1)}, bf16[208,384]{1,0:T(8,128)(2,1)}, bf16[208,384]{1,0:T(8,128)(2,1)}, bf16[208,384]{1,0:T(8,128)(2,1)}) custom-call(s32[2]{0:T(128)} %pad_add_fusion.refs_0_.ids, bf16[1024,768]{1,0:T(8,128)(2,1)} %get-tuple-element.192.xn_all, bf16[8,3,128,128]{3,2,1,0:T(8,128)(2,1)} %copy-done.3, ...), custom_call_target="tpu_custom_call" | custom-call | flops 4000000000 | bytes 4000000 | tf_op jit(solution)/shard_map/weight_grads/pallas_call | solution.py:139
  225.4 3.7 %all-to-all-start.4 = ((bf16[8,24,768]{2,1,0:T(8,128)(2,1)}), bf16[8,24,768]{2,1,0:T(8,128)(2,1)S(1)}, u32[]{:S(2)}, u32[]{:S(2)}) async-start(bf16[8,24,768]{2,1,0:T(8,128)(2,1)} %bitcast.16), calls=%async_computation.4 | async-start | bytes 589824 | tf_op jit(solution)/shard_map/all_to_all | solution.py:648
  229.1 6.4 %expert_weights.1 = (f32[2,768,768]{2,1,0:T(8,128)}, f32[2,768,768]{2,1,0:T(8,128)}) custom-call(bf16[2,96,768]{2,1,0:T(8,128)(2,1)} %get-tuple-element.292.refs_0_, bf16[2,96,768]{2,1,0:T(8,128)(2,1)} %get-tuple-element.293.refs_1_, bf16[2,96,768]{2,1,0:T(8,128)(2,1)} %get-tuple-element.294.refs_2_, bf16[2,96,768]{2,1,0:T(8,128)(2,1)} %get-tuple-element.295.refs_3_, ...), custom_call_target="tpu_custom_call" | custom-call | flops 7000000000 | bytes 7000000 | tf_op jit(solution)/shard_map/expert_weights/pallas_call | solution.py:908
  242.8 4.0 %collective-permute-done.47.refs_4_ = bf16[208,384]{1,0:T(8,128)(2,1)S(1)} collective-permute-done((bf16[208,384]{1,0:T(8,128)(2,1)S(1)}, bf16[208,384]{1,0:T(8,128)(2,1)S(1)}, u32[]{:S(2)}, u32[]{:S(2)}) %collective-permute-start.47) | collective-permute-done | bytes 159776 | tf_op jit(solution)/shard_map/ppermute | solution.py:32
  (250 shorter events, 106.9 us)
Async XLA Ops:
  23.2 25.5 %collective-permute-start.6 = (bf16[192,1280]{1,0:T(8,128)(2,1)S(1)}, bf16[192,1280]{1,0:T(8,128)(2,1)S(1)}, u32[]{:S(2)}, u32[]{:S(2)}) collective-permute-start(bf16[192,1280]{1,0:T(8,128)(2,1)S(1)} %constant_dynamic-update-slice_fusion.refs_9_.refs_4_), channel_id=1, source_target_pairs={{0,8},{4,12},{8,0},{12,4},{16,24},{20,28},{24,16},{28,20},{1,9},{5... | collective-permute-start | bytes 1474568 | tf_op jit(solution)/shard_map/ppermute | solution.py:32
  23.8 24.9 %collective-permute-start.7 = (bf16[192,1280]{1,0:T(8,128)(2,1)S(1)}, bf16[192,1280]{1,0:T(8,128)(2,1)S(1)}, u32[]{:S(2)}, u32[]{:S(2)}) collective-permute-start(bf16[192,1280]{1,0:T(8,128)(2,1)S(1)} %constant_dynamic-update-slice_fusion.refs_9_.refs_4_), channel_id=1, source_target_pairs={{0,16},{4,20},{8,24},{12,28},{16,0},{20,4},{24,8},{28,12},{1,17},{... | collective-permute-start | bytes 1474568 | tf_op jit(solution)/shard_map/ppermute | solution.py:32
  24.8 24.0 %collective-permute-start.8 = (bf16[192,1280]{1,0:T(8,128)(2,1)S(1)}, bf16[192,1280]{1,0:T(8,128)(2,1)S(1)}, u32[]{:S(2)}, u32[]{:S(2)}) collective-permute-start(bf16[192,1280]{1,0:T(8,128)(2,1)S(1)} %constant_dynamic-update-slice_fusion.refs_9_.refs_4_), channel_id=1, source_target_pairs={{0,24},{4,28},{8,16},{12,20},{16,8},{20,12},{24,0},{28,4},{1,25},{... | collective-permute-start | bytes 1474568 | tf_op jit(solution)/shard_map/ppermute | solution.py:32
  28.7 19.1 %all-to-all-start = ((bf16[8,24,768]{2,1,0:T(8,128)(2,1)}), bf16[8,24,768]{2,1,0:T(8,128)(2,1)S(1)}, u32[]{:S(2)}, u32[]{:S(2)}) async-start(bf16[8,24,768]{2,1,0:T(8,128)(2,1)} %bitcast.5), calls=%async_computation | async-start | bytes 589824 | tf_op jit(solution)/shard_map/all_to_all | solution.py:648
  32.1 16.6 %collective-permute-start.13 = (bf16[192,768]{1,0:T(8,128)(2,1)S(1)}, bf16[192,768]{1,0:T(8,128)(2,1)S(1)}, u32[]{:S(2)}, u32[]{:S(2)}) collective-permute-start(bf16[192,768]{1,0:T(8,128)(2,1)S(1)} %copy-done.1), channel_id=1, source_target_pairs={{0,2},{1,3},{2,0},{3,1},{4,6},{5,7},{6,4},{7,5},{8,10},{9,11},{10,... | collective-permute-start | bytes 884744 | tf_op jit(solution)/shard_map/ppermute | solution.py:32
  49.6 21.4 %collective-permute-start.19 = (bf16[384,768]{1,0:T(8,128)(2,1)S(1)}, bf16[384,768]{1,0:T(8,128)(2,1)S(1)}, u32[]{:S(2)}, u32[]{:S(2)}) collective-permute-start(bf16[384,768]{1,0:T(8,128)(2,1)S(1)} %pad_maximum_fusion.2), channel_id=1, source_target_pairs={{0,1},{1,0},{2,3},{3,2},{4,5},{5,4},{6,7},{7,6},{8,9},{9,8},{10,11... | collective-permute-start | bytes 1769480 | tf_op jit(solution)/shard_map/ppermute | solution.py:32
  50.7 21.4 %collective-permute-start.18 = (bf16[192,768]{1,0:T(8,128)(2,1)S(1)}, bf16[192,768]{1,0:T(8,128)(2,1)S(1)}, u32[]{:S(2)}, u32[]{:S(2)}) collective-permute-start(bf16[192,768]{1,0:T(8,128)(2,1)S(1)} %bitcast.42), channel_id=1, source_target_pairs={{0,2},{1,3},{2,0},{3,1},{4,6},{5,7},{6,4},{7,5},{8,10},{9,11},{10,... | collective-permute-start | bytes 884744 | tf_op jit(solution)/shard_map/ppermute | solution.py:32
  72.2 15.3 %collective-permute-start.20 = (bf16[384,768]{1,0:T(8,128)(2,1)S(1)}, bf16[384,768]{1,0:T(8,128)(2,1)S(1)}, u32[]{:S(2)}, u32[]{:S(2)}) collective-permute-start(bf16[384,768]{1,0:T(8,128)(2,1)S(1)} %pad_maximum_fusion.3), channel_id=1, source_target_pairs={{0,1},{1,0},{2,3},{3,2},{4,5},{5,4},{6,7},{7,6},{8,9},{9,8},{10,11... | collective-permute-start | bytes 1769480 | tf_op jit(solution)/shard_map/ppermute | solution.py:32
  89.3 20.1 %collective-permute-start.22 = (bf16[192,768]{1,0:T(8,128)(2,1)S(1)}, bf16[192,768]{1,0:T(8,128)(2,1)S(1)}, u32[]{:S(2)}, u32[]{:S(2)}) collective-permute-start(bf16[192,768]{1,0:T(8,128)(2,1)S(1)} %bitcast.46), channel_id=1, source_target_pairs={{0,2},{1,3},{2,0},{3,1},{4,6},{5,7},{6,4},{7,5},{8,10},{9,11},{10,... | collective-permute-start | bytes 884744 | tf_op jit(solution)/shard_map/ppermute | solution.py:32
  109.6 33.1 %collective-permute-start.24 = (bf16[192,768]{1,0:T(8,128)(2,1)}, bf16[192,768]{1,0:T(8,128)(2,1)S(1)}, u32[]{:S(2)}, u32[]{:S(2)}) collective-permute-start(bf16[192,768]{1,0:T(8,128)(2,1)} %get-tuple-element.212), channel_id=1, source_target_pairs={{0,1},{1,0},{2,3},{3,2},{4,5},{5,4},{6,7},{7,6},{8,9},{9,8},{10,11... | collective-permute-start | bytes 884744 | tf_op jit(solution)/shard_map/ppermute | solution.py:32
  117.3 22.7 %collective-permute-start.25 = (bf16[192,768]{1,0:T(8,128)(2,1)}, bf16[192,768]{1,0:T(8,128)(2,1)S(1)}, u32[]{:S(2)}, u32[]{:S(2)}) collective-permute-start(bf16[192,768]{1,0:T(8,128)(2,1)} %get-tuple-element.215), channel_id=1, source_target_pairs={{0,2},{1,3},{2,0},{3,1},{4,6},{5,7},{6,4},{7,5},{8,10},{9,11},{10,... | collective-permute-start | bytes 884744 | tf_op jit(solution)/shard_map/ppermute | solution.py:32
  127.3 15.3 %collective-permute-start.26 = (bf16[192,768]{1,0:T(8,128)(2,1)}, bf16[192,768]{1,0:T(8,128)(2,1)S(1)}, u32[]{:S(2)}, u32[]{:S(2)}) collective-permute-start(bf16[192,768]{1,0:T(8,128)(2,1)} %get-tuple-element.234), channel_id=1, source_target_pairs={{0,3},{1,2},{2,1},{3,0},{4,7},{5,6},{6,5},{7,4},{8,11},{9,10},{10,... | collective-permute-start | bytes 884744 | tf_op jit(solution)/shard_map/ppermute | solution.py:32
  130.7 28.8 %collective-permute-start.35 = (bf16[128,896]{1,0:T(8,128)(2,1)}, bf16[128,896]{1,0:T(8,128)(2,1)S(1)}, u32[]{:S(2)}, u32[]{:S(2)}) collective-permute-start(bf16[128,896]{1,0:T(8,128)(2,1)} %get-tuple-element.264.ext.refs_9_.refs_0_), channel_id=1, source_target_pairs={{0,8},{4,12},{8,0},{12,4},{16,24},{20,28},{24,16},{28,20},{1,9},{5... | collective-permute-start | bytes 688136 | tf_op jit(solution)/shard_map/ppermute | solution.py:32
  132.3 27.7 %collective-permute-start.37 = (bf16[128,896]{1,0:T(8,128)(2,1)}, bf16[128,896]{1,0:T(8,128)(2,1)S(1)}, u32[]{:S(2)}, u32[]{:S(2)}) collective-permute-start(bf16[128,896]{1,0:T(8,128)(2,1)} %get-tuple-element.264.ext.refs_9_.refs_0_), channel_id=1, source_target_pairs={{0,16},{4,20},{8,24},{12,28},{16,0},{20,4},{24,8},{28,12},{1,17},{... | collective-permute-start | bytes 688136 | tf_op jit(solution)/shard_map/ppermute | solution.py:32
  140.0 20.0 %collective-permute-start.39 = (bf16[128,896]{1,0:T(8,128)(2,1)}, bf16[128,896]{1,0:T(8,128)(2,1)S(1)}, u32[]{:S(2)}, u32[]{:S(2)}) collective-permute-start(bf16[128,896]{1,0:T(8,128)(2,1)} %get-tuple-element.264.ext.refs_9_.refs_0_), channel_id=1, source_target_pairs={{0,24},{4,28},{8,16},{12,20},{16,8},{20,12},{24,0},{28,4},{1,25},{... | collective-permute-start | bytes 688136 | tf_op jit(solution)/shard_map/ppermute | solution.py:32
  159.4 19.7 %collective-permute-start.34 = (bf16[128,896]{1,0:T(8,128)(2,1)}, bf16[128,896]{1,0:T(8,128)(2,1)S(1)}, u32[]{:S(2)}, u32[]{:S(2)}) collective-permute-start(bf16[128,896]{1,0:T(8,128)(2,1)} %get-tuple-element.264.ext.refs_9_.refs_0_), channel_id=1, source_target_pairs={{0,4},{4,0},{8,12},{12,8},{16,20},{20,16},{24,28},{28,24},{1,5},{5... | collective-permute-start | bytes 688136 | tf_op jit(solution)/shard_map/ppermute | solution.py:32
  159.5 19.9 %collective-permute-start.36 = (bf16[128,896]{1,0:T(8,128)(2,1)S(1)}, bf16[128,896]{1,0:T(8,128)(2,1)S(1)}, u32[]{:S(2)}, u32[]{:S(2)}) collective-permute-start(bf16[128,896]{1,0:T(8,128)(2,1)S(1)} %collective-permute-done.35.refs_11_.refs_2_), channel_id=1, source_target_pairs={{0,4},{4,0},{8,12},{12,8},{16,20},{20,16},{24,28},{28,24},{1,5},{5... | collective-permute-start | bytes 688136 | tf_op jit(solution)/shard_map/ppermute | solution.py:32
  160.0 19.8 %collective-permute-start.38 = (bf16[128,896]{1,0:T(8,128)(2,1)S(1)}, bf16[128,896]{1,0:T(8,128)(2,1)S(1)}, u32[]{:S(2)}, u32[]{:S(2)}) collective-permute-start(bf16[128,896]{1,0:T(8,128)(2,1)S(1)} %collective-permute-done.37.refs_13_.refs_4_), channel_id=1, source_target_pairs={{0,4},{4,0},{8,12},{12,8},{16,20},{20,16},{24,28},{28,24},{1,5},{5... | collective-permute-start | bytes 688136 | tf_op jit(solution)/shard_map/ppermute | solution.py:32
  160.1 18.5 %collective-permute-start.28 = (bf16[128,896]{1,0:T(8,128)(2,1)}, bf16[128,896]{1,0:T(8,128)(2,1)}, u32[]{:S(2)}, u32[]{:S(2)}) collective-permute-start(bf16[128,896]{1,0:T(8,128)(2,1)} %get-tuple-element.260.grad_ext.refs_1_), channel_id=1, source_target_pairs={{0,16},{4,20},{8,24},{12,28},{16,0},{20,4},{24,8},{28,12},{1,17},{... | collective-permute-start | bytes 688136 | tf_op jit(solution)/shard_map/ppermute | solution.py:32
  181.7 16.7 %collective-permute-start.41 = (bf16[384,768]{1,0:T(8,128)(2,1)S(1)}, bf16[384,768]{1,0:T(8,128)(2,1)S(1)}, u32[]{:S(2)}, u32[]{:S(2)}) collective-permute-start(bf16[384,768]{1,0:T(8,128)(2,1)S(1)} %copy-done.27), channel_id=1, source_target_pairs={{0,1},{1,0},{2,3},{3,2},{4,5},{5,4},{6,7},{7,6},{8,9},{9,8},{10,11... | collective-permute-start | bytes 1769480 | tf_op jit(solution)/shard_map/ppermute | solution.py:32
  194.5 21.3 %all-to-all-start.3 = ((bf16[8,3,128,128]{3,2,1,0:T(8,128)(2,1)}), bf16[8,3,128,128]{3,2,1,0:T(8,128)(2,1)S(1)}, u32[]{:S(2)}, u32[]{:S(2)}) async-start(bf16[8,3,128,128]{3,2,1,0:T(8,128)(2,1)} %bitcast.55), calls=%async_computation.3 | async-start | bytes 1572864 | tf_op jit(solution)/shard_map/all_to_all | solution.py:875
  198.6 16.4 %collective-permute-start.42 = (bf16[192,768]{1,0:T(8,128)(2,1)S(1)}, bf16[192,768]{1,0:T(8,128)(2,1)S(1)}, u32[]{:S(2)}, u32[]{:S(2)}) collective-permute-start(bf16[192,768]{1,0:T(8,128)(2,1)S(1)} %slice.41), channel_id=1, source_target_pairs={{0,2},{1,3},{2,0},{3,1},{4,6},{5,7},{6,4},{7,5},{8,10},{9,11},{10,... | collective-permute-start | bytes 884744 | tf_op jit(solution)/shard_map/ppermute | solution.py:32
  221.0 14.5 %collective-permute-start.43 = (bf16[208,384]{1,0:T(8,128)(2,1)}, bf16[208,384]{1,0:T(8,128)(2,1)S(1)}, u32[]{:S(2)}, u32[]{:S(2)}) collective-permute-start(bf16[208,384]{1,0:T(8,128)(2,1)} %get-tuple-element.288), channel_id=1, source_target_pairs={{0,1},{1,0},{2,3},{3,2},{4,5},{5,4},{6,7},{7,6},{8,9},{9,8},{10,11... | collective-permute-start | bytes 479240 | tf_op jit(solution)/shard_map/ppermute | solution.py:32
  221.0 14.9 %collective-permute-start.44 = (bf16[208,384]{1,0:T(8,128)(2,1)}, bf16[208,384]{1,0:T(8,128)(2,1)S(1)}, u32[]{:S(2)}, u32[]{:S(2)}) collective-permute-start(bf16[208,384]{1,0:T(8,128)(2,1)} %get-tuple-element.289), channel_id=1, source_target_pairs={{0,2},{1,3},{2,0},{3,1},{4,6},{5,7},{6,4},{7,5},{8,10},{9,11},{10,... | collective-permute-start | bytes 479240 | tf_op jit(solution)/shard_map/ppermute | solution.py:32
  (80 other events, 639.3 us)

commit v4 on v3

--- a/solution.py
+++ b/solution.py
@@ -565,7 +565,7 @@
 
 def spread_body(sizes, ids, *refs):
     per, pairs = sizes
-    pieces, (in_grad, out_grad, lines) = refs[:-3], refs[-3:]
+    pieces, (in_grad, out_grad, router_grad, gain_one, gain_two, table_grad) = refs[:-6], refs[-6:]
     rows = in_grad.shape[0]
     total = None
     for mask, piece in enumerate(pieces):
@@ -584,7 +584,14 @@
             def _():
                 out_grad[:, pl.ds(pl.multiple_of((index - 3 * pairs) * LANES, LANES), LANES)] = values
 
-    lines[...] = total
+    line_rows, span = total.shape
+    line = 0
+    for ref in (router_grad, gain_one, gain_two, table_grad):
+        count, lanes = ref.shape
+        group, row = divmod(line, line_rows)
+        moved = pltpu.roll(total, span - group * rows, 1) if group else total
+        ref[...] = moved[row : row + count, :lanes]
+        line += count
 
 
 def pad_to(x, shape):
@@ -745,13 +752,16 @@
         name="upstream",
     )(ups_all, expert_down)
     ext_later, _ = tie(ext, rows_own)
-    ext_pieces = core_pieces(chip_pieces(ext_later))
+    ext_chips = chip_pieces(ext_later)
     kept = [[], [], [], [], []]
     back_parts = []
     for step in range(shards):
         row_chunk = row_chunks[step]
         if step:
             row_chunk, _ = tie(row_chunk, back_parts[-1])
+        if step == shards - 1:
+            row_chunk, ext_chips = tie(row_chunk, ext_chips)
+            ext_pieces = core_pieces(ext_chips)
         back, *saved = pl.pallas_call(
             functools.partial(expert_body, (experts, per_device, capacity)),
             grid=(per_device,),
@@ -785,7 +795,7 @@
                 if mask != nearer:
                     value, _ = tie(row_chunks[mask ^ nearer], back)
                     row_chunks[mask] = swap(value, "wshard", nearer)
-    kept, back_sum = tie(kept, sum_back(back_parts))
+    kept, back_sum, ext_pieces = tie(kept, sum_back(back_parts), ext_pieces)
     returned_grad = exchange(back_sum)
     out_near, out_far, router_part = pl.pallas_call(
         functools.partial(expert_out_body, (shards, per_device, capacity)),
@@ -868,10 +878,12 @@
         cost_estimate=cost(12.0),
         name="key_grad",
     )(ids, *grad_pieces, *ext_pieces, joined_own, mirror, query_grad, resid_low, joined)
-    for step in reversed(doubling_steps(shards)[:-1]):
+    *nearer_steps, far_step = reversed(doubling_steps(shards)[:-1])
+    for step in nearer_steps:
         half = out_sum.shape[0] // 2
         moved = swap(out_sum[half:], "wshard", step)
         out_sum = (out_sum[:half].astype(F32) + moved.astype(F32)).astype(BF)
+    out_moved = swap(out_sum[out_sum.shape[0] // 2 :], "wshard", far_step)
     received = lax.all_to_all(
         blocks.reshape(devices, per, rows, LANES), "expert", split_axis=0, concat_axis=0, tiled=True
     )
@@ -887,9 +899,9 @@
         name="source_grad",
         us=4.0,
     )
-    table_line = table_part[:heads].T.reshape(shards, table_rows * heads)
-    table_line = pad_to(table_line, (shards, part)).reshape(1, width)
-    lines = jnp.concatenate([router_part[:experts], gain_one_part, gain_two_part, table_line], axis=0)
+    table_lines = table_part[:heads].reshape(heads, shards, table_rows)
+    table_lines = pad_to(table_lines, (heads, shards, part)).reshape(heads, width)
+    lines = jnp.concatenate([router_part[:experts], gain_one_part, gain_two_part, table_lines], axis=0)
     line_count = lines.shape[0]
     groups = per * LANES // part
     line_rows = -(-line_count // (16 * groups)) * 16
@@ -904,7 +916,7 @@
         name="weight_grads",
         us=4.0,
     )
-    weight_parts, out_sum, kept = tie(weight_parts, out_sum, kept)
+    weight_parts, kept = tie(weight_parts, kept)
     up_grad, down_grad = pl.pallas_call(
         functools.partial(expert_weights_body, shards),
         grid=(per_device,),
@@ -916,9 +928,10 @@
         name="expert_weights",
     )(*kept[0], *kept[1], *kept[2], *kept[3])
     mine = sum_back(weight_parts)
+    mine, out_moved, up_grad, down_grad = tie(mine, out_moved, up_grad, down_grad)
+    pieces, out_moved = tie(chip_pieces(mine), out_moved)
+    out_sum = (out_sum[: out_moved.shape[0]].astype(F32) + out_moved.astype(F32)).astype(BF)
     returned_rows = exchange(out_sum)
-    mine, returned_rows, up_grad, down_grad = tie(mine, returned_rows, up_grad, down_grad)
-    pieces = chip_pieces(mine)
     (result,) = call(
         result_body,
         [ids, returned_rows, back_slots, after, gate],
@@ -926,27 +939,29 @@
         name="result",
         us=2.0,
     )
-    pieces, result = tie(pieces, result)
-    attn_in_grad, attn_out_grad, lines = call(
+    attn_in_grad, attn_out_grad, router_grad, gain_one_grad, gain_two_grad, table_grad = call(
         functools.partial(spread_body, (per, pairs)),
         [ids, *core_pieces(pieces)],
-        [((part, 3 * width), F32), ((part, width), F32), ((line_rows, per * LANES), F32)],
+        [
+            ((part, 3 * width), F32),
+            ((part, width), F32),
+            ((experts, part), F32),
+            ((1, part), F32),
+            ((1, part), F32),
+            ((heads, table_rows), F32),
+        ],
         name="spread",
         us=2.0,
     )
-    lines = lines[:, : groups * part].reshape(line_rows, groups, part).transpose(1, 0, 2)
-    lines = lines.reshape(groups * line_rows, part)
-    router_grad = lines[:experts].T
-    table_grad = lines[experts + 2, : table_rows * heads].reshape(table_rows, heads)
     return (
         result[None],
         tokens_grad[None],
-        lines[experts],
-        lines[experts + 1],
+        gain_one_grad[0],
+        gain_two_grad[0],
         attn_in_grad,
         attn_out_grad,
-        router_grad,
-        table_grad,
+        router_grad.T,
+        table_grad.T,
         up_grad,
         down_grad,
     )

time: 257 us -> 258 us (level)
    ppermute x53, waiting for transfers between devices: 46.4 us -> 39.5 us  [swap(): return lax.ppermute(x, axis, [(i, i ^ mask) for i in range(count)])]
    all_to_all x1, waiting for transfers between devices: 0.01 us -> 5.62 us  [local(): lax.all_to_all(blocks.reshape(devices, per, rows, LANES), 'expert', split...]
    unnamed x98 -> x111, local copies, waits for them, and re-layouts: 8.29 us -> 10.5 us
  transfers between devices with their start and end apart: 58 -> 58, of which waited for: 24 -> 18; matrix products, arithmetic and copies ran while one was open for 6% -> 6% of each run, Pallas kernels for 35% -> 36%
where the time goes in v4:
time: 258 us; the launch traced here: 256 us
  Pallas kernels  97.1 us (38%)
  starting transfers between devices  70.6 us (27%)
  waiting for transfers between devices  57.9 us (22%)
  local copies, waits for them, and re-layouts  16.8 us (7%)
  other arithmetic  9.94 us (4%)
    ppermute x53, starting transfers between devices, swap(): return lax.ppermute(x, axis, [(i, i ^ mask) for i in range(count)])  53 us
    ppermute x53, waiting for transfers between devices, swap(): return lax.ppermute(x, axis, [(i, i ^ mask) for i in range(count)])  39.5 us
    pallas_call x7, Pallas kernels, call(): pl.pallas_call(body, in_specs=[ids] + [near] * (len(args) - 1), out_specs...  37.5 us
    pallas_call x4, Pallas kernels, local(): pl.pallas_call(functools.partial(expert_body, (experts, per_device, capac...  23.1 us
    all_to_all x4, starting transfers between devices, exchange(): lax.all_to_all(blocks, 'expert', split_axis=0, concat_axis=0, tiled=True)  14.1 us
    all_to_all x4, waiting for transfers between devices, exchange(): lax.all_to_all(blocks, 'expert', split_axis=0, concat_axis=0, tiled=True)  12.8 us
    unnamed x111, local copies, waits for them, and re-layouts  10.5 us
    pallas_call x1, Pallas kernels, local(): pl.pallas_call(functools.partial(query_body, (head_dim, bucket_count)), g...  10.3 us
  transfers between devices with their start and end apart: 58, of which 18 were waited for; matrix products, arithmetic and copies ran while one was open for 6% of the time, Pallas kernels for 36%

profile of v4, /device:TPU:0, one launch (start us, length us, event | category | flops | bytes accessed | tf_op | source)
XLA Modules:
  0.0 255.8 jit_solution(3070289967058979817)
XLA Ops:
  4.8 5.1 %collective-permute-start.5 = (bf16[48,1280]{1,0:T(8,128)(2,1)S(1)}, bf16[48,1280]{1,0:T(8,128)(2,1)S(1)}, u32[]{:S(2)}, u32[]{:S(2)}) collective-permute-start(bf16[48,1280]{1,0:T(8,128)(2,1)S(1)} %pad_maximum_fusion.4), channel_id=1, source_target_pairs={{0,3},{1,2},{2,1},{3,0},{4,7},{5,6},{6,5},{7,4},{8,11},{9,10},{10,... | collective-permute-start | bytes 368648 | tf_op jit(solution)/shard_map/ppermute | solution.py:32
  31.6 4.0 %collective-permute-start.13 = (bf16[192,768]{1,0:T(8,128)(2,1)S(1)}, bf16[192,768]{1,0:T(8,128)(2,1)S(1)}, u32[]{:S(2)}, u32[]{:S(2)}) collective-permute-start(bf16[192,768]{1,0:T(8,128)(2,1)S(1)} %copy-done.1), channel_id=1, source_target_pairs={{0,2},{1,3},{2,0},{3,1},{4,6},{5,7},{6,4},{7,5},{8,10},{9,11},{10,... | collective-permute-start | bytes 884744 | tf_op jit(solution)/shard_map/ppermute | solution.py:32
  39.0 10.9 %all-to-all-done = bf16[8,24,768]{2,1,0:T(8,128)(2,1)S(1)} async-done(((bf16[8,24,768]{2,1,0:T(8,128)(2,1)}), bf16[8,24,768]{2,1,0:T(8,128)(2,1)S(1)}, u32[]{:S(2)}, u32[]{:S(2)}) %all-to-all-start) | async-done | bytes 294944 | tf_op jit(solution)/shard_map/all_to_all | solution.py:655
  57.1 15.8 %attention_forward.1 = (bf16[1024,768]{1,0:T(8,128)(2,1)}, bf16[1024,2304]{1,0:T(8,128)(2,1)}, bf16[128,2304]{1,0:T(8,128)(2,1)}, bf16[128,896]{1,0:T(8,128)(2,1...) custom-call(s32[2]{0:T(128)} %pad_add_fusion.refs_0_.ids, ...), custom_call_target="tpu_custom_call" | custom-call | flops 200000000 | bytes 200000 | tf_op jit(solution)/shard_map/attention_forward/pallas_call | solution.py:139
  77.8 3.6 %all-to-all-start.1 = ((bf16[8,24,768]{2,1,0:T(8,128)(2,1)}), bf16[8,24,768]{2,1,0:T(8,128)(2,1)S(1)}, u32[]{:S(2)}, u32[]{:S(2)}) async-start(bf16[8,24,768]{2,1,0:T(8,128)(2,1)} %bitcast.52), calls=%async_computation.1 | async-start | bytes 589824 | tf_op jit(solution)/shard_map/all_to_all | solution.py:655
  81.4 8.0 %collective-permute-done.20 = bf16[384,768]{1,0:T(8,128)(2,1)S(1)} collective-permute-done((bf16[384,768]{1,0:T(8,128)(2,1)S(1)}, bf16[384,768]{1,0:T(8,128)(2,1)S(1)}, u32[]{:S(2)}, u32[]{:S(2)}) %collective-permute-start.20) | collective-permute-done | bytes 589856 | tf_op jit(solution)/shard_map/ppermute | solution.py:32
  93.0 4.3 %upstream.1 = (bf16[2,384,768]{2,1,0:T(8,128)(2,1)}, f32[2,384,768]{2,1,0:T(8,128)}) custom-call(bf16[768,768]{1,0:T(8,128)(2,1)} %pad_maximum_fusion.1.chunks, bf16[2,768,768]{2,1,0:T(8,128)(2,1)} %refs_12_.1), custom_call_target="tpu_custom_call" | custom-call | flops 1000000 | bytes 1000 | tf_op jit(solution)/shard_map/upstream/pallas_call | solution.py:741
  97.3 5.7 %experts.4 = (bf16[192,768]{1,0:T(8,128)(2,1)}, bf16[2,96,768]{2,1,0:T(8,128)(2,1)}, bf16[2,96,768]{2,1,0:T(8,128)(2,1)}, bf16[2,96,768]{2,1,0:T(8,128)(2,1)}, b...) custom-call(s32[2]{0:T(128)} %pad_add_fusion.refs_0_.ids, bf16[192,768]{1,0:T(8,128)(2,1)} %bitcast.40, ...), custom_call_target="tpu_custom_call" | custom-call | flops 1000000 | bytes 1000 | tf_op jit(solution)/shard_map/experts/pallas_call | solution.py:765
  105.9 5.8 %experts.5 = (bf16[192,768]{1,0:T(8,128)(2,1)}, bf16[2,96,768]{2,1,0:T(8,128)(2,1)}, bf16[2,96,768]{2,1,0:T(8,128)(2,1)}, bf16[2,96,768]{2,1,0:T(8,128)(2,1)}, b...) custom-call(s32[2]{0:T(128)} %pad_add_fusion.refs_0_.ids, bf16[192,768]{1,0:T(8,128)(2,1)} %copy-done.14, ...), custom_call_target="tpu_custom_call" | custom-call | flops 1000000 | bytes 1000 | tf_op jit(solution)/shard_map/experts/pallas_call | solution.py:765
  117.3 5.7 %experts.6 = (bf16[192,768]{1,0:T(8,128)(2,1)}, bf16[2,96,768]{2,1,0:T(8,128)(2,1)}, bf16[2,96,768]{2,1,0:T(8,128)(2,1)}, bf16[2,96,768]{2,1,0:T(8,128)(2,1)}, b...) custom-call(s32[2]{0:T(128)} %pad_add_fusion.refs_0_.ids, bf16[192,768]{1,0:T(8,128)(2,1)} %copy-done.12, ...), custom_call_target="tpu_custom_call" | custom-call | flops 1000000 | bytes 1000 | tf_op jit(solution)/shard_map/experts/pallas_call | solution.py:765
  124.2 5.9 %experts.7 = (bf16[192,768]{1,0:T(8,128)(2,1)}, bf16[2,96,768]{2,1,0:T(8,128)(2,1)}, bf16[2,96,768]{2,1,0:T(8,128)(2,1)}, bf16[2,96,768]{2,1,0:T(8,128)(2,1)}, b...) custom-call(s32[2]{0:T(128)} %pad_add_fusion.refs_0_.ids, bf16[192,768]{1,0:T(8,128)(2,1)} %copy-done.13, ...), custom_call_target="tpu_custom_call" | custom-call | flops 1000000 | bytes 1000 | tf_op jit(solution)/shard_map/experts/pallas_call | solution.py:765
  132.2 11.1 %collective-permute-done.28 = bf16[192,768]{1,0:T(8,128)(2,1)S(1)} collective-permute-done((bf16[192,768]{1,0:T(8,128)(2,1)}, bf16[192,768]{1,0:T(8,128)(2,1)S(1)}, u32[]{:S(2)}, u32[]{:S(2)}) %collective-permute-start.28) | collective-permute-done | bytes 294944 | tf_op jit(solution)/shard_map/ppermute | solution.py:32
  144.7 3.6 %all-to-all-start.2 = ((bf16[8,24,768]{2,1,0:T(8,128)(2,1)}), bf16[8,24,768]{2,1,0:T(8,128)(2,1)S(1)}, u32[]{:S(2)}, u32[]{:S(2)}) async-start(bf16[8,24,768]{2,1,0:T(8,128)(2,1)} %bitcast.11), calls=%async_computation.2 | async-start | bytes 589824 | tf_op jit(solution)/shard_map/all_to_all | solution.py:655
  148.4 6.2 %expert_out.1 = (bf16[384,768]{1,0:T(8,128)(2,1)}, bf16[384,768]{1,0:T(8,128)(2,1)}, f32[128,768]{1,0:T(8,128)}) custom-call(bf16[2,96,768]{2,1,0:T(8,128)(2,1)} %get-tuple-element.319.refs_0_, bf16[2,96,768]{2,1,0:T(8,128)(2,1)} %get-tuple-element.320.refs_1_, bf16[2,96,768]{2,1,0:T(8,128)(2,1)} %get-tuple-element.321.refs_2_, ...), custom_call_target="tpu_custom_call" | custom-call | flops 5000000000 | bytes 5000000 | tf_op jit(solution)/shard_map/expert_out/pallas_call | solution.py:800
  156.1 3.6 %residual.1 = (f32[128,768]{1,0:T(8,128)}, bf16[128,768]{1,0:T(8,128)(2,1)}, bf16[128,896]{1,0:T(8,128)(2,1)}, f32[1,768]{1,0:T(1,128)}) custom-call(s32[2]{0:T(128)} %pad_add_fusion.refs_0_.ids, bf16[192,768]{1,0:T(8,128)(2,1)} %bitcast.51, bf16[128,192]{1,0:T(8,128)(2,1)} %fusion.back_slots, f32[128,768]{1,0:T(8,128)} %get-tuple-element.276.after, ...), custom_call_target="tpu_custom_call" | custom-call | flops 2000000000 | bytes 2000000 | tf_op jit(solution)/shard_map/residual/pallas_call | solution.py:139
  163.2 10.3 %query_grad.1 = (bf16[6,128,128]{2,1,0:T(8,128)(2,1)}, f32[16,32]{1,0:T(8,128)}) custom-call(s32[2]{0:T(128)} %pad_add_fusion.refs_0_.ids, bf16[128,896]{1,0:T(8,128)(2,1)} %get-tuple-element.283.grad_ext.refs_1_, bf16[128,896]{1,0:T(8,128)(2,1)} %get-tuple-element.287.ext.refs_9_.refs_0_, bf16[128,2304]{1,0:T(8,128)(2,1)} %get-tuple-element.279.joined_own.refs_17_, ...), custom_call_target="tpu_custom_call" | custom-call | flops 10000000000 | bytes 10000000 | tf_op jit(solution)/shard_map/query_grad/pallas_call | solution.py:826
  176.5 6.3 %collective-permute-start.34 = (bf16[384,768]{1,0:T(8,128)(2,1)S(1)}, bf16[384,768]{1,0:T(8,128)(2,1)S(1)}, u32[]{:S(2)}, u32[]{:S(2)}) collective-permute-start(bf16[384,768]{1,0:T(8,128)(2,1)S(1)} %copy-done.29), channel_id=1, source_target_pairs={{0,1},{1,0},{2,3},{3,2},{4,5},{5,4},{6,7},{7,6},{8,9},{9,8},{10,11... | collective-permute-start | bytes 1769480 | tf_op jit(solution)/shard_map/ppermute | solution.py:32
  183.7 9.3 %key_grad.1.refs_0_ = bf16[24,128,128]{2,1,0:T(8,128)(2,1)} custom-call(s32[2]{0:T(128)} %pad_add_fusion.refs_0_.ids, bf16[128,896]{1,0:T(8,128)(2,1)} %get-tuple-element.283.grad_ext.refs_1_, bf16[128,896]{1,0:T(8,128)(2,1)} %copy-done.41, bf16[128,896]{1,0:T(8,128)(2,1)} %copy-done.40, bf16[128,896]{1,0:T(8,128)(2,1)} %copy-done.42, ...), custom_call_target="tpu_custom_call" | custom-call | flops 12000000000 | bytes 12000000 | tf_op jit(solution)/shard_map/key_grad/pallas_call | solution.py:856
  196.6 5.0 %source_grad.1 = (bf16[128,768]{1,0:T(8,128)(2,1)}, f32[1,768]{1,0:T(1,128)}) custom-call(s32[2]{0:T(128)} %pad_add_fusion.refs_0_.ids, bf16[24,128,128]{2,1,0:T(8,128)(2,1)} %key_grad.1.refs_0_, bf16[128,768]{1,0:T(8,128)(2,1)} %bitcast.45, f32[8,768]{1,0:T(8,128)} %get-tuple-element.213.gains.refs_2_, f32[128,768]{1,0:T(8,128)} %get-tuple-element.299.refs_3_, ...), custom_call_target="tpu_custom_call" | custom-call | flops 4000000000 | bytes 4000000 | tf_op jit(solution)/shard_map/source_grad/pallas_call | solution.py:139
  203.5 5.6 %all-to-all-done.3.received = bf16[8,3,128,128]{3,2,1,0:T(8,128)(2,1)S(1)} async-done(((bf16[8,3,128,128]{3,2,1,0:T(8,128)(2,1)}), bf16[8,3,128,128]{3,2,1,0:T(8,128)(2,1)S(1)}, u32[]{:S(2)}, u32[]{:S(2)}) %all-to-all-start.3) | async-done | bytes 786464 | tf_op jit(solution)/shard_map/all_to_all | solution.py:887
  210.0 4.6 %weight_grads.1 = (bf16[208,384]{1,0:T(8,128)(2,1)}, bf16[208,384]{1,0:T(8,128)(2,1)}, bf16[208,384]{1,0:T(8,128)(2,1)}, bf16[208,384]{1,0:T(8,128)(2,1)}) custom-call(s32[2]{0:T(128)} %pad_add_fusion.refs_0_.ids, bf16[1024,768]{1,0:T(8,128)(2,1)} %get-tuple-element.273.xn_all, bf16[8,3,128,128]{3,2,1,0:T(8,128)(2,1)} %copy-done.3, ...), custom_call_target="tpu_custom_call" | custom-call | flops 4000000000 | bytes 4000000 | tf_op jit(solution)/shard_map/weight_grads/pallas_call | solution.py:139
  218.9 6.4 %expert_weights.1 = (f32[2,768,768]{2,1,0:T(8,128)}, f32[2,768,768]{2,1,0:T(8,128)}) custom-call(bf16[2,96,768]{2,1,0:T(8,128)(2,1)} %get-tuple-element.319.refs_0_, bf16[2,96,768]{2,1,0:T(8,128)(2,1)} %get-tuple-element.320.refs_1_, bf16[2,96,768]{2,1,0:T(8,128)(2,1)} %get-tuple-element.321.refs_2_, bf16[2,96,768]{2,1,0:T(8,128)(2,1)} %get-tuple-element.322.refs_3_, ...), custom_call_target="tpu_custom_call" | custom-call | flops 7000000000 | bytes 7000000 | tf_op jit(solution)/shard_map/expert_weights/pallas_call | solution.py:920
  225.4 4.4 %collective-permute-done.43 = bf16[208,384]{1,0:T(8,128)(2,1)S(1)} collective-permute-done((bf16[208,384]{1,0:T(8,128)(2,1)}, bf16[208,384]{1,0:T(8,128)(2,1)S(1)}, u32[]{:S(2)}, u32[]{:S(2)}) %collective-permute-start.43) | collective-permute-done | bytes 159776 | tf_op jit(solution)/shard_map/ppermute | solution.py:32
  233.5 4.2 %collective-permute-done.48.refs_6_ = bf16[208,384]{1,0:T(8,128)(2,1)S(1)} collective-permute-done((bf16[208,384]{1,0:T(8,128)(2,1)S(1)}, bf16[208,384]{1,0:T(8,128)(2,1)S(1)}, u32[]{:S(2)}, u32[]{:S(2)}) %collective-permute-start.48) | collective-permute-done | bytes 159776 | tf_op jit(solution)/shard_map/ppermute | solution.py:32
  (256 shorter events, 98.9 us)
Async XLA Ops:
  22.3 27.6 %collective-permute-start.8 = (bf16[192,1280]{1,0:T(8,128)(2,1)S(1)}, bf16[192,1280]{1,0:T(8,128)(2,1)S(1)}, u32[]{:S(2)}, u32[]{:S(2)}) collective-permute-start(bf16[192,1280]{1,0:T(8,128)(2,1)S(1)} %constant_dynamic-update-slice_fusion.refs_9_.refs_4_), channel_id=1, source_target_pairs={{0,24},{4,28},{8,16},{12,20},{16,8},{20,12},{24,0},{28,4},{1,25},{... | collective-permute-start | bytes 1474568 | tf_op jit(solution)/shard_map/ppermute | solution.py:32
  23.9 26.0 %collective-permute-start.7 = (bf16[192,1280]{1,0:T(8,128)(2,1)S(1)}, bf16[192,1280]{1,0:T(8,128)(2,1)S(1)}, u32[]{:S(2)}, u32[]{:S(2)}) collective-permute-start(bf16[192,1280]{1,0:T(8,128)(2,1)S(1)} %constant_dynamic-update-slice_fusion.refs_9_.refs_4_), channel_id=1, source_target_pairs={{0,16},{4,20},{8,24},{12,28},{16,0},{20,4},{24,8},{28,12},{1,17},{... | collective-permute-start | bytes 1474568 | tf_op jit(solution)/shard_map/ppermute | solution.py:32
  24.8 25.1 %collective-permute-start.6 = (bf16[192,1280]{1,0:T(8,128)(2,1)S(1)}, bf16[192,1280]{1,0:T(8,128)(2,1)S(1)}, u32[]{:S(2)}, u32[]{:S(2)}) collective-permute-start(bf16[192,1280]{1,0:T(8,128)(2,1)S(1)} %constant_dynamic-update-slice_fusion.refs_9_.refs_4_), channel_id=1, source_target_pairs={{0,8},{4,12},{8,0},{12,4},{16,24},{20,28},{24,16},{28,20},{1,9},{5... | collective-permute-start | bytes 1474568 | tf_op jit(solution)/shard_map/ppermute | solution.py:32
  28.2 21.7 %all-to-all-start = ((bf16[8,24,768]{2,1,0:T(8,128)(2,1)}), bf16[8,24,768]{2,1,0:T(8,128)(2,1)S(1)}, u32[]{:S(2)}, u32[]{:S(2)}) async-start(bf16[8,24,768]{2,1,0:T(8,128)(2,1)} %bitcast.5), calls=%async_computation | async-start | bytes 589824 | tf_op jit(solution)/shard_map/all_to_all | solution.py:655
  31.6 18.3 %collective-permute-start.13 = (bf16[192,768]{1,0:T(8,128)(2,1)S(1)}, bf16[192,768]{1,0:T(8,128)(2,1)S(1)}, u32[]{:S(2)}, u32[]{:S(2)}) collective-permute-start(bf16[192,768]{1,0:T(8,128)(2,1)S(1)} %copy-done.1), channel_id=1, source_target_pairs={{0,2},{1,3},{2,0},{3,1},{4,6},{5,7},{6,4},{7,5},{8,10},{9,11},{10,... | collective-permute-start | bytes 884744 | tf_op jit(solution)/shard_map/ppermute | solution.py:32
  50.8 22.1 %collective-permute-start.15 = (bf16[384,768]{1,0:T(8,128)(2,1)S(1)}, bf16[384,768]{1,0:T(8,128)(2,1)S(1)}, u32[]{:S(2)}, u32[]{:S(2)}) collective-permute-start(bf16[384,768]{1,0:T(8,128)(2,1)S(1)} %pad_maximum_fusion.2), channel_id=1, source_target_pairs={{0,1},{1,0},{2,3},{3,2},{4,5},{5,4},{6,7},{7,6},{8,9},{9,8},{10,11... | collective-permute-start | bytes 1769480 | tf_op jit(solution)/shard_map/ppermute | solution.py:32
  52.8 21.2 %collective-permute-start.14 = (bf16[192,768]{1,0:T(8,128)(2,1)S(1)}, bf16[192,768]{1,0:T(8,128)(2,1)S(1)}, u32[]{:S(2)}, u32[]{:S(2)}) collective-permute-start(bf16[192,768]{1,0:T(8,128)(2,1)S(1)} %bitcast.35), channel_id=1, source_target_pairs={{0,2},{1,3},{2,0},{3,1},{4,6},{5,7},{6,4},{7,5},{8,10},{9,11},{10,... | collective-permute-start | bytes 884744 | tf_op jit(solution)/shard_map/ppermute | solution.py:32
  74.0 15.5 %collective-permute-start.20 = (bf16[384,768]{1,0:T(8,128)(2,1)S(1)}, bf16[384,768]{1,0:T(8,128)(2,1)S(1)}, u32[]{:S(2)}, u32[]{:S(2)}) collective-permute-start(bf16[384,768]{1,0:T(8,128)(2,1)S(1)} %pad_maximum_fusion.3), channel_id=1, source_target_pairs={{0,1},{1,0},{2,3},{3,2},{4,5},{5,4},{6,7},{7,6},{8,9},{9,8},{10,11... | collective-permute-start | bytes 1769480 | tf_op jit(solution)/shard_map/ppermute | solution.py:32
  77.8 12.7 %all-to-all-start.1 = ((bf16[8,24,768]{2,1,0:T(8,128)(2,1)}), bf16[8,24,768]{2,1,0:T(8,128)(2,1)S(1)}, u32[]{:S(2)}, u32[]{:S(2)}) async-start(bf16[8,24,768]{2,1,0:T(8,128)(2,1)} %bitcast.52), calls=%async_computation.1 | async-start | bytes 589824 | tf_op jit(solution)/shard_map/all_to_all | solution.py:655
  90.6 14.6 %collective-permute-start.21 = (bf16[192,768]{1,0:T(8,128)(2,1)S(1)}, bf16[192,768]{1,0:T(8,128)(2,1)S(1)}, u32[]{:S(2)}, u32[]{:S(2)}) collective-permute-start(bf16[192,768]{1,0:T(8,128)(2,1)S(1)} %bitcast.38), channel_id=1, source_target_pairs={{0,1},{1,0},{2,3},{3,2},{4,5},{5,4},{6,7},{7,6},{8,9},{9,8},{10,11... | collective-permute-start | bytes 884744 | tf_op jit(solution)/shard_map/ppermute | solution.py:32
  90.9 20.8 %collective-permute-start.22 = (bf16[192,768]{1,0:T(8,128)(2,1)S(1)}, bf16[192,768]{1,0:T(8,128)(2,1)S(1)}, u32[]{:S(2)}, u32[]{:S(2)}) collective-permute-start(bf16[192,768]{1,0:T(8,128)(2,1)S(1)} %bitcast.39), channel_id=1, source_target_pairs={{0,2},{1,3},{2,0},{3,1},{4,6},{5,7},{6,4},{7,5},{8,10},{9,11},{10,... | collective-permute-start | bytes 884744 | tf_op jit(solution)/shard_map/ppermute | solution.py:32
  115.3 16.8 %collective-permute-start.27 = (bf16[192,768]{1,0:T(8,128)(2,1)}, bf16[192,768]{1,0:T(8,128)(2,1)S(1)}, u32[]{:S(2)}, u32[]{:S(2)}) collective-permute-start(bf16[192,768]{1,0:T(8,128)(2,1)} %get-tuple-element.226), channel_id=1, source_target_pairs={{0,1},{1,0},{2,3},{3,2},{4,5},{5,4},{6,7},{7,6},{8,9},{9,8},{10,11... | collective-permute-start | bytes 884744 | tf_op jit(solution)/shard_map/ppermute | solution.py:32
  123.0 20.2 %collective-permute-start.28 = (bf16[192,768]{1,0:T(8,128)(2,1)}, bf16[192,768]{1,0:T(8,128)(2,1)S(1)}, u32[]{:S(2)}, u32[]{:S(2)}) collective-permute-start(bf16[192,768]{1,0:T(8,128)(2,1)} %get-tuple-element.229), channel_id=1, source_target_pairs={{0,2},{1,3},{2,0},{3,1},{4,6},{5,7},{6,4},{7,5},{8,10},{9,11},{10,... | collective-permute-start | bytes 884744 | tf_op jit(solution)/shard_map/ppermute | solution.py:32
  130.0 13.2 %collective-permute-start.29 = (bf16[192,768]{1,0:T(8,128)(2,1)}, bf16[192,768]{1,0:T(8,128)(2,1)S(1)}, u32[]{:S(2)}, u32[]{:S(2)}) collective-permute-start(bf16[192,768]{1,0:T(8,128)(2,1)} %get-tuple-element.250), channel_id=1, source_target_pairs={{0,3},{1,2},{2,1},{3,0},{4,7},{5,6},{6,5},{7,4},{8,11},{9,10},{10,... | collective-permute-start | bytes 884744 | tf_op jit(solution)/shard_map/ppermute | solution.py:32
  131.6 12.5 %collective-permute-start.30 = (bf16[128,896]{1,0:T(8,128)(2,1)S(1)}, bf16[128,896]{1,0:T(8,128)(2,1)S(1)}, u32[]{:S(2)}, u32[]{:S(2)}) collective-permute-start(bf16[128,896]{1,0:T(8,128)(2,1)S(1)} %copy-done.18), channel_id=1, source_target_pairs={{0,4},{4,0},{8,12},{12,8},{16,20},{20,16},{24,28},{28,24},{1,5},{5... | collective-permute-start | bytes 688136 | tf_op jit(solution)/shard_map/ppermute | solution.py:32
  131.6 12.5 %collective-permute-start.31 = (bf16[128,896]{1,0:T(8,128)(2,1)S(1)}, bf16[128,896]{1,0:T(8,128)(2,1)S(1)}, u32[]{:S(2)}, u32[]{:S(2)}) collective-permute-start(bf16[128,896]{1,0:T(8,128)(2,1)S(1)} %collective-permute-done.24.refs_11_.refs_2_), channel_id=1, source_target_pairs={{0,4},{4,0},{8,12},{12,8},{16,20},{20,16},{24,28},{28,24},{1,5},{5... | collective-permute-start | bytes 688136 | tf_op jit(solution)/shard_map/ppermute | solution.py:32
  132.1 12.0 %collective-permute-start.32 = (bf16[128,896]{1,0:T(8,128)(2,1)S(1)}, bf16[128,896]{1,0:T(8,128)(2,1)S(1)}, u32[]{:S(2)}, u32[]{:S(2)}) collective-permute-start(bf16[128,896]{1,0:T(8,128)(2,1)S(1)} %collective-permute-done.25.refs_13_.refs_4_), channel_id=1, source_target_pairs={{0,4},{4,0},{8,12},{12,8},{16,20},{20,16},{24,28},{28,24},{1,5},{5... | collective-permute-start | bytes 688136 | tf_op jit(solution)/shard_map/ppermute | solution.py:32
  159.7 13.8 %collective-permute-start.37 = (bf16[128,896]{1,0:T(8,128)(2,1)}, bf16[128,896]{1,0:T(8,128)(2,1)S(1)}, u32[]{:S(2)}, u32[]{:S(2)}) collective-permute-start(bf16[128,896]{1,0:T(8,128)(2,1)} %get-tuple-element.283.grad_ext.refs_1_), channel_id=1, source_target_pairs={{0,24},{4,28},{8,16},{12,20},{16,8},{20,12},{24,0},{28,4},{1,25},{... | collective-permute-start | bytes 688136 | tf_op jit(solution)/shard_map/ppermute | solution.py:32
  161.6 12.0 %collective-permute-start.36 = (bf16[128,896]{1,0:T(8,128)(2,1)}, bf16[128,896]{1,0:T(8,128)(2,1)S(1)}, u32[]{:S(2)}, u32[]{:S(2)}) collective-permute-start(bf16[128,896]{1,0:T(8,128)(2,1)} %get-tuple-element.283.grad_ext.refs_1_), channel_id=1, source_target_pairs={{0,16},{4,20},{8,24},{12,28},{16,0},{20,4},{24,8},{28,12},{1,17},{... | collective-permute-start | bytes 688136 | tf_op jit(solution)/shard_map/ppermute | solution.py:32
  176.5 26.7 %collective-permute-start.34 = (bf16[384,768]{1,0:T(8,128)(2,1)S(1)}, bf16[384,768]{1,0:T(8,128)(2,1)S(1)}, u32[]{:S(2)}, u32[]{:S(2)}) collective-permute-start(bf16[384,768]{1,0:T(8,128)(2,1)S(1)} %copy-done.29), channel_id=1, source_target_pairs={{0,1},{1,0},{2,3},{3,2},{4,5},{5,4},{6,7},{7,6},{8,9},{9,8},{10,11... | collective-permute-start | bytes 1769480 | tf_op jit(solution)/shard_map/ppermute | solution.py:32
  193.0 16.1 %all-to-all-start.3 = ((bf16[8,3,128,128]{3,2,1,0:T(8,128)(2,1)}), bf16[8,3,128,128]{3,2,1,0:T(8,128)(2,1)S(1)}, u32[]{:S(2)}, u32[]{:S(2)}) async-start(bf16[8,3,128,128]{3,2,1,0:T(8,128)(2,1)} %bitcast.48), calls=%async_computation.3 | async-start | bytes 1572864 | tf_op jit(solution)/shard_map/all_to_all | solution.py:887
  203.4 26.5 %collective-permute-start.45 = (bf16[192,768]{1,0:T(8,128)(2,1)S(1)}, bf16[192,768]{1,0:T(8,128)(2,1)S(1)}, u32[]{:S(2)}, u32[]{:S(2)}) collective-permute-start(bf16[192,768]{1,0:T(8,128)(2,1)S(1)} %slice.21), channel_id=1, source_target_pairs={{0,2},{1,3},{2,0},{3,1},{4,6},{5,7},{6,4},{7,5},{8,10},{9,11},{10,... | collective-permute-start | bytes 884744 | tf_op jit(solution)/shard_map/ppermute | solution.py:32
  214.6 15.2 %collective-permute-start.43 = (bf16[208,384]{1,0:T(8,128)(2,1)}, bf16[208,384]{1,0:T(8,128)(2,1)S(1)}, u32[]{:S(2)}, u32[]{:S(2)}) collective-permute-start(bf16[208,384]{1,0:T(8,128)(2,1)} %get-tuple-element.317), channel_id=1, source_target_pairs={{0,2},{1,3},{2,0},{3,1},{4,6},{5,7},{6,4},{7,5},{8,10},{9,11},{10,... | collective-permute-start | bytes 479240 | tf_op jit(solution)/shard_map/ppermute | solution.py:32
  215.7 14.1 %collective-permute-start.44 = (bf16[208,384]{1,0:T(8,128)(2,1)}, bf16[208,384]{1,0:T(8,128)(2,1)S(1)}, u32[]{:S(2)}, u32[]{:S(2)}) collective-permute-start(bf16[208,384]{1,0:T(8,128)(2,1)} %get-tuple-element.318), channel_id=1, source_target_pairs={{0,3},{1,2},{2,1},{3,0},{4,7},{5,6},{6,5},{7,4},{8,11},{9,10},{10,... | collective-permute-start | bytes 479240 | tf_op jit(solution)/shard_map/ppermute | solution.py:32
  (86 other events, 720.9 us)
